TPU v7x, 32 devices: a whole 2x2x4 slice. The times are simulated.
32 devices in a mesh: dp: 4 (over z), mp: 8 (over y, x, core).
Axes of the slice: x: 2, y: 2, z: 4, core: 2. Of those that a mesh axis runs over, the one named last changes fastest.
Arguments:
- code_ids: int32 [16, 1024], P('dp'), may hold values from 0 to 8191
- code_mask: int32 [16, 1024], P('dp'), may hold values from 0 to 1
- caption_ids: int32 [8, 128], P('dp'), may hold values from 0 to 15999
- caption_segments: int32 [8, 128], P('dp'), may hold values from 0 to 15, as said below
- image_row: int32 [16], P('dp'), may hold values from 0 to 7, as said below
- attention_master: float32 [3, 4, 1024, 1024], P(None, None, 'dp', 'mp')
- attention_momentum: float32 [3, 4, 1024, 1024], P(None, None, 'dp', 'mp'), may hold values from -1.9073486e-05 to 1.9073486e-05
- attention_average: float32 [3, 4, 1024, 1024], P(None, None, 'dp', 'mp')
- dense_master: float32 [2, 2, 1024, 4096], P(None, None, 'dp', 'mp'), may hold values from -0.1875 to 0.1875
- dense_momentum: float32 [2, 2, 1024, 4096], P(None, None, 'dp', 'mp'), may hold values from -1.9073486e-05 to 1.9073486e-05
- dense_average: float32 [2, 2, 1024, 4096], P(None, None, 'dp', 'mp'), may hold values from -0.1875 to 0.1875
- text_master: float32 [16000, 1024], P('mp', 'dp'), may hold values from -1 to 1
- text_momentum: float32 [16000, 1024], P('mp', 'dp'), may hold values from -1.9073486e-05 to 1.9073486e-05
- text_average: float32 [16000, 1024], P('mp', 'dp'), may hold values from -1 to 1
- code_master: float32 [2, 8192, 1024], P(None, 'mp', 'dp'), may hold values from -1 to 1
- code_momentum: float32 [2, 8192, 1024], P(None, 'mp', 'dp'), may hold values from -1.9073486e-05 to 1.9073486e-05
- code_average: float32 [2, 8192, 1024], P(None, 'mp', 'dp'), may hold values from -1 to 1
- gain_master: float32 [7, 1024], P(None, ('dp', 'mp'))
- gain_momentum: float32 [7, 1024], P(None, ('dp', 'mp')), may hold values from -0.00018310547 to 0.00018310547
- gain_average: float32 [7, 1024], P(None, ('dp', 'mp')), may hold values from 0.5 to 1.5
Outputs:
- loss: float32 [], replicated
- clip_norm: float32 [], replicated
- attention_new: float32 [3, 4, 1024, 1024], P(None, None, 'dp', 'mp')
- attention_moment: float32 [3, 4, 1024, 1024], P(None, None, 'dp', 'mp')
- attention_mean: float32 [3, 4, 1024, 1024], P(None, None, 'dp', 'mp')
- attention_copy: bfloat16 [3, 4, 1024, 1024], P(None, None, 'dp', 'mp')
- dense_new: float32 [2, 2, 1024, 4096], P(None, None, 'dp', 'mp')
- dense_moment: float32 [2, 2, 1024, 4096], P(None, None, 'dp', 'mp')
- dense_mean: float32 [2, 2, 1024, 4096], P(None, None, 'dp', 'mp')
- dense_copy: bfloat16 [2, 2, 1024, 4096], P(None, None, 'dp', 'mp')
- text_new: float32 [16000, 1024], P('mp', 'dp')
- text_moment: float32 [16000, 1024], P('mp', 'dp')
- text_mean: float32 [16000, 1024], P('mp', 'dp')
- text_copy: bfloat16 [16000, 1024], P('mp', 'dp')
- code_new: float32 [2, 8192, 1024], P(None, 'mp', 'dp')
- code_moment: float32 [2, 8192, 1024], P(None, 'mp', 'dp')
- code_mean: float32 [2, 8192, 1024], P(None, 'mp', 'dp')
- code_copy: bfloat16 [2, 8192, 1024], P(None, 'mp', 'dp')
- gain_new: float32 [7, 1024], P(None, ('dp', 'mp'))
- gain_moment: float32 [7, 1024], P(None, ('dp', 'mp'))
- gain_mean: float32 [7, 1024], P(None, ('dp', 'mp'))
- gain_copy: bfloat16 [7, 1024], P(None, ('dp', 'mp'))
- token_loss: float32 [16, 1024], P('dp')
Inputs may be any that keep to these rules, and one draw needn't show every extreme that they name: `caption_segments`: each caption row holds the captions of two images, one after the other, each of 32 or more tokens; the images of a row lie in the same group of 4 consecutive images, and every image has its caption in exactly one row. image_row[i] is the row that holds image i's caption.
All inputs are finite; a program needn't handle non-finite values.
Results may differ from a plain program's by a relative error of at most 0.014.
Values may be sent and summed in bfloat16 or wider, within the bound.
A program may use at most 320 MiB of HBM per device.

v0:
```python
from functools import partial
import math

import jax
import jax.numpy as jnp
from jax import lax
from jax.sharding import PartitionSpec as P

D = 1024
HEAD_DIM = 64
FF = 4096
VC = 8192
VT = 16000


EPS = 1e-06
CLIP = 0.01
MOMENT = 0.9
DECAY = 0.75
SMOOTH = 0.1
Z_WEIGHT = 0.01
NEGATIVE = -1e30
LAST = (((1,), (1,)), ((), ()))
FIRST = (((0,), (0,)), ((), ()))


def for_sending(value):

    def short(part):
        return part.astype(jnp.bfloat16) if part.dtype == jnp.float32 else part

    return jax.tree.map(short, value)


def joined(value, axis, join):
    gathered = jax.tree.map(
        lambda a, kind: lax.all_gather(a.astype(kind), axis),
        value,
        (jnp.bfloat16, jnp.bfloat16, jnp.bfloat16, jnp.bfloat16),
    )

    def take(source):
        return jax.tree.map(
            lambda a, own: lax.dynamic_index_in_dim(a, source, 0, False).astype(own.dtype),
            gathered,
            value,
        )

    return lax.fori_loop(
        1, lax.axis_size(axis), lambda source, state: join(state, take(source)), take(0)
    )


def rms_norm(values, gain):
    return values * lax.rsqrt(jnp.mean(values * values, axis=-1, keepdims=True) + EPS) * gain


def norm_back(values, gain, upstream):
    _, pull = jax.vjp(rms_norm, values, gain)
    return pull(upstream)


def gelu_exact(values):
    return jax.nn.gelu(values, approximate=False)


def spread_forward(values):
    return jax.tree.map(
        lambda part, own: part.astype(own.dtype),
        lax.all_gather(for_sending(values), "mp", axis=0, tiled=True),
        values,
    )


def collect_forward(values):
    return lax.psum_scatter(
        values.astype(jnp.bfloat16), "mp", scatter_dimension=0, tiled=True
    ).astype(jnp.float32)


def spread_backward(values):
    return lax.all_gather(values, "mp", axis=0, tiled=True)


def collect_backward(values):
    return jax.tree.map(
        lambda part: part.astype(jnp.float32),
        lax.psum_scatter(for_sending(values), "mp", scatter_dimension=0, tiled=True),
    )


def product(left, right, dims):
    return lax.dot_general(left, right, dims, preferred_element_type=jnp.float32)


def split_heads(values, groups):
    return values.reshape(groups, values.shape[0] // groups, values.shape[1] // HEAD_DIM, HEAD_DIM)


def core_forward(query, key, value, allowed, scale):
    scores = jnp.einsum("bqhe,bkhe->bhqk", query, key, preferred_element_type=jnp.float32) * scale
    scores = jnp.where(allowed[:, None], scores, NEGATIVE)
    highest = jnp.max(scores, axis=-1, keepdims=True)
    weight = jnp.exp(scores - highest)
    totals = jnp.sum(weight, axis=-1, keepdims=True)
    shares = (weight / totals).astype(jnp.bfloat16)
    mixed = jnp.einsum("bhqk,bkhe->bqhe", shares, value, preferred_element_type=jnp.float32)
    return (mixed.astype(jnp.bfloat16), highest + jnp.log(totals))


def core_backward(query, key, value, allowed, scale, partition, upstream):
    scores = jnp.einsum("bqhe,bkhe->bhqk", query, key, preferred_element_type=jnp.float32) * scale
    scores = jnp.where(allowed[:, None], scores, NEGATIVE)
    shares = jnp.exp(scores - partition)
    grad_value = jnp.einsum(
        "bhqk,bqhe->bkhe", shares.astype(jnp.bfloat16), upstream, preferred_element_type=jnp.float32
    )
    grad_shares = jnp.einsum("bqhe,bkhe->bhqk", upstream, value, preferred_element_type=jnp.float32)
    inner = jnp.sum(shares * grad_shares, axis=-1, keepdims=True)
    grad_scores = (shares * (grad_shares - inner)).astype(jnp.bfloat16)
    grad_query = (
        jnp.einsum("bhqk,bkhe->bqhe", grad_scores, key, preferred_element_type=jnp.float32) * scale
    )
    grad_key = (
        jnp.einsum("bhqk,bqhe->bkhe", grad_scores, query, preferred_element_type=jnp.float32)
        * scale
    )
    return (grad_query, grad_key, grad_value)


def causal_forward(parts, scale):
    query, key, value = parts
    length = query.shape[0]
    block = min(512, length)
    places = jnp.arange(length)
    outputs = []
    partitions = []
    for begin in range(0, length, block):
        allowed = begin + places[:block, None] >= places[None, :]
        mixed, partition = core_forward(
            query[None, begin : begin + block], key[None], value[None], allowed[None], scale
        )
        outputs.append(mixed[0])
        partitions.append(partition[0])
    return (jnp.concatenate(outputs, axis=0), jnp.concatenate(partitions, axis=1))


def causal_backward(parts, scale):
    query, key, value, partition, upstream = parts
    length = query.shape[0]
    block = min(512, length)
    places = jnp.arange(length)
    query_parts = []
    grad_key = jnp.zeros(key.shape, jnp.float32)
    grad_value = jnp.zeros(value.shape, jnp.float32)
    for begin in range(0, length, block):
        allowed = begin + places[:block, None] >= places[None, :]
        part_query, part_key, part_value = core_backward(
            query[None, begin : begin + block],
            key[None],
            value[None],
            allowed[None],
            scale,
            partition[None, :, begin : begin + block],
            upstream[None, begin : begin + block],
        )
        query_parts.append(part_query[0])
        grad_key = grad_key + part_key[0]
        grad_value = grad_value + part_value[0]
    return (jnp.concatenate(query_parts, axis=0), grad_key, grad_value)


def cross_inputs(key, value, context):
    segments = context["segments"]
    picked = context["rows"]
    groups = segments.shape[0]
    picked_key = jnp.take(split_heads(key, groups), picked, axis=0)
    picked_value = jnp.take(split_heads(value, groups), picked, axis=0)
    allowed = (jnp.take(segments, picked, axis=0) == context["images"][:, None])[:, None, :]
    return (picked_key, picked_value, allowed)


def mix_forward(query, key, value, kind, context):
    scale = HEAD_DIM ** (-0.5)
    width = query.shape[1]
    if kind == "self":
        groups = context["count"]
        mixed, partition = lax.map(
            partial(causal_forward, scale=scale),
            (split_heads(query, groups), split_heads(key, groups), split_heads(value, groups)),
        )
    elif kind == "cross":
        picked_key, picked_value, allowed = cross_inputs(key, value, context)
        mixed, partition = core_forward(
            split_heads(query, picked_key.shape[0]), picked_key, picked_value, allowed, scale
        )
    else:
        segments = context["segments"]
        allowed = (segments[:, None] == segments[None, :])[None]
        mixed, partition = core_forward(
            split_heads(query, 1), split_heads(key, 1), split_heads(value, 1), allowed, scale
        )
    return (mixed.reshape(-1, width), partition)


def mix_backward(query, key, value, partition, upstream, kind, context):
    scale = HEAD_DIM ** (-0.5)
    width = query.shape[1]
    if kind == "self":
        groups = context["count"]
        grad_query, grad_key, grad_value = lax.map(
            partial(causal_backward, scale=scale),
            (
                split_heads(query, groups),
                split_heads(key, groups),
                split_heads(value, groups),
                partition,
                split_heads(upstream, groups),
            ),
        )
    elif kind == "cross":
        picked_key, picked_value, allowed = cross_inputs(key, value, context)
        grad_query, part_key, part_value = core_backward(
            split_heads(query, picked_key.shape[0]),
            picked_key,
            picked_value,
            allowed,
            scale,
            partition,
            split_heads(upstream, picked_key.shape[0]),
        )
        groups = context["segments"].shape[0]
        grad_key = (
            jnp.zeros((groups,) + part_key.shape[1:], jnp.float32).at[context["rows"]].add(part_key)
        )
        grad_value = (
            jnp.zeros((groups,) + part_value.shape[1:], jnp.float32)
            .at[context["rows"]]
            .add(part_value)
        )
    else:
        segments = context["segments"]
        allowed = (segments[:, None] == segments[None, :])[None]
        grad_query, grad_key, grad_value = core_backward(
            split_heads(query, 1),
            split_heads(key, 1),
            split_heads(value, 1),
            allowed,
            scale,
            partition,
            split_heads(upstream, 1),
        )
    return (
        grad_query.reshape(-1, width),
        grad_key.reshape(-1, width),
        grad_value.reshape(-1, width),
    )


def attention_forward(values, gain, weights, kind, context, encoded):
    normed = rms_norm(values, gain).astype(jnp.bfloat16)
    if kind == "cross":
        inputs, source = spread_forward((normed, encoded))
    else:
        inputs = spread_forward(normed)
        source = inputs
    query = jnp.dot(inputs, weights[0], preferred_element_type=jnp.float32).astype(jnp.bfloat16)
    key = jnp.dot(source, weights[1], preferred_element_type=jnp.float32).astype(jnp.bfloat16)
    value = jnp.dot(source, weights[2], preferred_element_type=jnp.float32).astype(jnp.bfloat16)
    mixed, partition = mix_forward(query, key, value, kind, context)
    output = collect_forward(product(mixed, weights[3], LAST))
    return (output, (inputs, source, query, key, value, mixed, partition))


def attention_backward(upstream, values, gain, weights, kind, context, kept):
    inputs, source, query, key, value, mixed, partition = kept
    grad_rows = spread_backward(upstream.astype(jnp.bfloat16))
    grad_out = product(grad_rows, mixed, FIRST)
    grad_mixed = jnp.dot(grad_rows, weights[3], preferred_element_type=jnp.float32).astype(
        jnp.bfloat16
    )
    grad_query, grad_key, grad_value = mix_backward(
        query, key, value, partition, grad_mixed, kind, context
    )
    grad_query = grad_query.astype(jnp.bfloat16)
    grad_key = grad_key.astype(jnp.bfloat16)
    grad_value = grad_value.astype(jnp.bfloat16)
    grads = jnp.stack(
        [
            product(inputs, grad_query, FIRST),
            product(source, grad_key, FIRST),
            product(source, grad_value, FIRST),
            grad_out,
        ]
    )
    from_query = product(grad_query, weights[0], LAST)
    from_source = product(grad_key, weights[1], LAST) + product(grad_value, weights[2], LAST)
    if kind == "cross":
        grad_normed, grad_encoded = collect_backward((from_query, from_source))
    else:
        grad_normed = collect_backward(from_query + from_source)
        grad_encoded = None
    grad_values, grad_gain = norm_back(values, gain, grad_normed)
    return (grad_values, grad_gain, grads, grad_encoded)


def dense_forward(values, gain, weights):
    normed = rms_norm(values, gain).astype(jnp.bfloat16)
    inputs = spread_forward(normed)
    hidden = jnp.dot(inputs, weights[0], preferred_element_type=jnp.float32)
    active = gelu_exact(hidden).astype(jnp.bfloat16)
    partial_out = product(active, weights[1], LAST)
    output = collect_forward(partial_out)
    return (output, (inputs, weights, hidden, active))


def dense_backward(upstream, values, gain, kept):
    inputs, matrices, hidden, active = kept
    upstream_low = upstream.astype(jnp.bfloat16)
    grad_rows = spread_backward(upstream_low)
    grad_active = jnp.dot(grad_rows, matrices[1], preferred_element_type=jnp.float32)
    _, pull = jax.vjp(gelu_exact, hidden)
    grad_hidden = pull(grad_active)[0].astype(jnp.bfloat16)
    grads = jnp.stack([product(inputs, grad_hidden, FIRST), product(grad_rows, active, FIRST)])
    grad_normed = product(grad_hidden, matrices[0], LAST)
    grad_normed = collect_backward(grad_normed)
    grad_values, grad_gain = norm_back(values, gain, grad_normed)
    return (grad_values, grad_gain, grads)


def embed_forward(token_ids, usable, table):
    vocab = table.shape[0]
    local = token_ids - lax.axis_index("mp") * vocab
    inside = usable & (local >= 0) & (local < vocab)
    local = jnp.clip(local, 0, vocab - 1)
    picked = jnp.take(table, local, axis=0).astype(jnp.float32) * inside[:, None].astype(
        jnp.float32
    )
    return (collect_forward(picked), (local, inside, vocab))


def embed_backward(upstream, kept):
    local, inside, vocab = kept
    gathered = spread_backward(upstream.astype(jnp.bfloat16)).astype(jnp.float32)
    return (
        jnp.zeros((vocab, gathered.shape[1]), jnp.float32)
        .at[local]
        .add(gathered * inside[:, None].astype(jnp.float32))
    )


def merge_stats(first, second):
    highest = jnp.maximum(first[0], second[0])
    mass = first[1] * jnp.exp(first[0] - highest) + second[1] * jnp.exp(second[0] - highest)
    return (highest, mass, first[2] + second[2], first[3] + second[3])


def update(master, moment, average, gradient, factor, rate):
    clipped = gradient * factor
    moment_new = MOMENT * moment + clipped
    master_new = master - rate * (clipped + MOMENT * moment_new)
    average_new = DECAY * average + (1.0 - DECAY) * master_new
    return (master_new, moment_new, average_new, master_new.astype(jnp.bfloat16))


def per_device(
    code_ids,
    code_mask,
    caption_ids,
    caption_segments,
    image_row,
    attention_master,
    attention_momentum,
    attention_average,
    dense_master,
    dense_momentum,
    dense_average,
    text_master,
    text_momentum,
    text_average,
    code_master,
    code_momentum,
    code_average,
    gain_master,
    gain_momentum,
    gain_average,
):
    attention_set, dense_set, text_table, code_tables = (
        lax.all_gather(attention_master.astype(jnp.bfloat16), "dp", axis=2, tiled=True),
        lax.all_gather(dense_master.astype(jnp.bfloat16), "dp", axis=2, tiled=True),
        lax.all_gather(text_master.astype(jnp.bfloat16), "dp", axis=1, tiled=True),
        lax.all_gather(code_master.astype(jnp.bfloat16), "dp", axis=2, tiled=True),
    )
    gain_set = lax.all_gather(
        gain_master.astype(jnp.bfloat16), ("dp", "mp"), axis=1, tiled=True
    ).astype(jnp.float32)
    images, length = code_ids.shape
    caption_rows = caption_ids.shape[0]
    encoder_context = {"segments": caption_segments.reshape(-1)}
    self_context = {"count": images}
    cross_context = {
        "rows": image_row - lax.axis_index("dp") * caption_rows,
        "images": lax.axis_index("dp") * images + jnp.arange(images, dtype=jnp.int32),
        "segments": caption_segments,
    }
    text_ids = caption_ids.reshape(-1)
    encoder_in, text_keep = embed_forward(text_ids, jnp.ones(text_ids.shape, bool), text_table)
    branch, encoder_attention_keep = attention_forward(
        encoder_in, gain_set[0], attention_set[0], "encoder", encoder_context, None
    )
    encoder_mid = encoder_in + branch
    branch, encoder_dense_keep = dense_forward(encoder_mid, gain_set[1], dense_set[0])
    encoder_top = encoder_mid + branch
    encoded = rms_norm(encoder_top, gain_set[2]).astype(jnp.bfloat16)
    previous = jnp.concatenate(
        [jnp.zeros((images, 1), jnp.int32), code_ids[:, :-1]], axis=1
    ).reshape(-1)
    starting = jnp.broadcast_to(jnp.arange(length) > 0, (images, length)).reshape(-1)
    decoder_in, code_keep = embed_forward(previous, starting, code_tables[0])
    branch, self_keep = attention_forward(
        decoder_in, gain_set[3], attention_set[1], "self", self_context, None
    )
    decoder_one = decoder_in + branch
    branch, cross_keep = attention_forward(
        decoder_one, gain_set[4], attention_set[2], "cross", cross_context, encoded
    )
    decoder_two = decoder_one + branch
    branch, decoder_dense_keep = dense_forward(decoder_two, gain_set[5], dense_set[1])
    decoder_top = decoder_two + branch
    final = spread_forward(rms_norm(decoder_top, gain_set[6]).astype(jnp.bfloat16))
    logits = product(final, code_tables[1], LAST)
    vocab = logits.shape[1]
    local_target = code_ids.reshape(-1) - lax.axis_index("mp") * vocab
    hits = (jnp.arange(vocab, dtype=jnp.int32)[None, :] == local_target[:, None]).astype(
        jnp.float32
    )
    highest = jnp.max(logits, axis=-1)
    highest, mass, target_logit, logit_total = joined(
        (
            highest,
            jnp.sum(jnp.exp(logits - highest[:, None]), axis=-1),
            jnp.sum(hits * logits, axis=-1),
            jnp.sum(logits, axis=-1),
        ),
        "mp",
        merge_stats,
    )
    partition = highest + jnp.log(mass)
    valid = code_mask.reshape(-1).astype(jnp.float32)
    per_token = (
        partition
        - (1.0 - SMOOTH) * target_logit
        - SMOOTH * logit_total / VC
        + Z_WEIGHT * partition * partition
    )
    count, loss_total = lax.psum((jnp.sum(valid), jnp.sum(per_token * valid)), "dp")
    loss = loss_total / count
    weighting = valid / count
    grad_logits = weighting[:, None] * (
        (1.0 + 2.0 * Z_WEIGHT * partition)[:, None] * jnp.exp(logits - partition[:, None])
        - (1.0 - SMOOTH) * hits
        - SMOOTH / VC
    )
    grad_logits = grad_logits.astype(jnp.bfloat16)
    grad_out_table = product(grad_logits, final, FIRST)
    grad_final = collect_backward(
        jnp.dot(grad_logits, code_tables[1], preferred_element_type=jnp.float32)
    )
    grad_top, gain_six = norm_back(decoder_top, gain_set[6], grad_final)
    grad_branch, gain_five, dense_one = dense_backward(
        grad_top, decoder_two, gain_set[5], decoder_dense_keep
    )
    grad_two = grad_top + grad_branch
    grad_branch, gain_four, attention_two, grad_encoded = attention_backward(
        grad_two, decoder_one, gain_set[4], attention_set[2], "cross", cross_context, cross_keep
    )
    grad_one = grad_two + grad_branch
    grad_branch, gain_three, attention_one, nothing = attention_backward(
        grad_one, decoder_in, gain_set[3], attention_set[1], "self", self_context, self_keep
    )
    grad_start = grad_one + grad_branch
    grad_code_in = embed_backward(grad_start, code_keep)
    grad_encoder_top, gain_two = norm_back(encoder_top, gain_set[2], grad_encoded)
    grad_branch, gain_one, dense_zero = dense_backward(
        grad_encoder_top, encoder_mid, gain_set[1], encoder_dense_keep
    )
    grad_encoder_mid = grad_encoder_top + grad_branch
    grad_branch, gain_zero, attention_zero, nothing = attention_backward(
        grad_encoder_mid,
        encoder_in,
        gain_set[0],
        attention_set[0],
        "encoder",
        encoder_context,
        encoder_attention_keep,
    )
    grad_text = embed_backward(grad_encoder_mid + grad_branch, text_keep)
    attention_grads, dense_grads, text_grads, code_grads = (
        lax.psum_scatter(
            jnp.stack([attention_zero, attention_one, attention_two]).astype(jnp.bfloat16),
            "dp",
            scatter_dimension=2,
            tiled=True,
        ).astype(jnp.float32),
        lax.psum_scatter(
            jnp.stack([dense_zero, dense_one]).astype(jnp.bfloat16),
            "dp",
            scatter_dimension=2,
            tiled=True,
        ).astype(jnp.float32),
        lax.psum_scatter(
            grad_text.astype(jnp.bfloat16), "dp", scatter_dimension=1, tiled=True
        ).astype(jnp.float32),
        lax.psum_scatter(
            jnp.stack([grad_code_in, grad_out_table]).astype(jnp.bfloat16),
            "dp",
            scatter_dimension=2,
            tiled=True,
        ).astype(jnp.float32),
    )
    gain_grads = lax.psum_scatter(
        jnp.stack([gain_zero, gain_one, gain_two, gain_three, gain_four, gain_five, gain_six]),
        ("dp", "mp"),
        scatter_dimension=1,
        tiled=True,
    )
    squares = (
        jnp.sum(attention_grads * attention_grads)
        + jnp.sum(dense_grads * dense_grads)
        + jnp.sum(text_grads * text_grads)
        + jnp.sum(code_grads * code_grads)
        + jnp.sum(gain_grads * gain_grads)
    )
    norm = jnp.sqrt(lax.psum(squares, ("dp", "mp")))
    factor = jnp.minimum(1.0, CLIP / norm)
    rate = 0.012 * math.sqrt(12 * D * D + 4 * D * FF + VT * D + 2 * VC * D + 7 * D) / CLIP
    attention_out = update(
        attention_master, attention_momentum, attention_average, attention_grads, factor, rate
    )
    dense_out = update(dense_master, dense_momentum, dense_average, dense_grads, factor, rate)
    text_out = update(text_master, text_momentum, text_average, text_grads, factor, rate)
    code_out = update(code_master, code_momentum, code_average, code_grads, factor, rate)
    gain_out = update(gain_master, gain_momentum, gain_average, gain_grads, factor, rate)
    return (
        loss,
        norm,
        attention_out[0],
        attention_out[1],
        attention_out[2],
        attention_out[3],
        dense_out[0],
        dense_out[1],
        dense_out[2],
        dense_out[3],
        text_out[0],
        text_out[1],
        text_out[2],
        text_out[3],
        code_out[0],
        code_out[1],
        code_out[2],
        code_out[3],
        gain_out[0],
        gain_out[1],
        gain_out[2],
        gain_out[3],
        per_token.reshape(images, length),
    )


def solution(mesh):
    return jax.shard_map(
        per_device,
        mesh=mesh,
        in_specs=(
            P("dp", None),
            P("dp", None),
            P("dp", None),
            P("dp", None),
            P("dp"),
            P(None, None, "dp", "mp"),
            P(None, None, "dp", "mp"),
            P(None, None, "dp", "mp"),
            P(None, None, "dp", "mp"),
            P(None, None, "dp", "mp"),
            P(None, None, "dp", "mp"),
            P("mp", "dp"),
            P("mp", "dp"),
            P("mp", "dp"),
            P(None, "mp", "dp"),
            P(None, "mp", "dp"),
            P(None, "mp", "dp"),
            P(None, ("dp", "mp")),
            P(None, ("dp", "mp")),
            P(None, ("dp", "mp")),
        ),
        out_specs=(
            P(),
            P(),
            P(None, None, "dp", "mp"),
            P(None, None, "dp", "mp"),
            P(None, None, "dp", "mp"),
            P(None, None, "dp", "mp"),
            P(None, None, "dp", "mp"),
            P(None, None, "dp", "mp"),
            P(None, None, "dp", "mp"),
            P(None, None, "dp", "mp"),
            P("mp", "dp"),
            P("mp", "dp"),
            P("mp", "dp"),
            P("mp", "dp"),
            P(None, "mp", "dp"),
            P(None, "mp", "dp"),
            P(None, "mp", "dp"),
            P(None, "mp", "dp"),
            P(None, ("dp", "mp")),
            P(None, ("dp", "mp")),
            P(None, ("dp", "mp")),
            P(None, ("dp", "mp")),
            P("dp", None),
        ),
        check_vma=False,
    )
```

profile of v0, /device:TPU:0, one launch (start us, length us, event | category | flops | bytes accessed | tf_op | source)
XLA Modules:
  0.0 2394.1 jit_solution(9687123401545024503)
XLA Ops:
  12.2 81.3 %all-gather.18.cloned.1.call-done = bf16[2,1024,1024]{2,1,0:T(8,128)(2,1)} async-done(((bf16[2,1024,256]{2,1,0:T(8,128)(2,1)}), bf16[2,1024,1024]{2,1,0:T(8,128)(2,1)}) %all-gather.18.cloned.1.call-update) | async-done | bytes 4194320 | tf_op jit(solution)/shard_map/all_gather | solution.py:392
  122.7 50.1 %all-gather.24.cloned.1.call-done = bf16[2000,1024]{1,0:T(8,128)(2,1)} async-done(((bf16[2000,256]{1,0:T(8,128)(2,1)}), bf16[2000,1024]{1,0:T(8,128)(2,1)}) %all-gather.24.cloned.1.call-update) | async-done | bytes 4096016 | tf_op jit(solution)/shard_map/all_gather | solution.py:391
  179.3 39.2 %all-gather.4 = bf16[32,32,7]{1,2,0:T(8,128)(2,1)S(1)} all-gather(bf16[1,32,7]{1,2,0:T(8,128)(2,1)S(1)} %convert_bitcast_fusion.4), channel_id=1, replica_groups=mesh['dp'=4,'mp'=8] {'dp','mp'}, dimensions={0}, use_global_device_ids=true | all-gather | bytes 14784 | tf_op jit(solution)/shard_map/all_gather | solution.py:394
  219.3 26.7 %reduce-scatter.22.cloned.1.call-done = bf16[512,1024]{1,0:T(8,128)(2,1)} async-done(((bf16[4096,1024]{1,0:T(8,128)(2,1)}), bf16[512,1024]{1,0:T(8,128)(2,1)}) %reduce-scatter.22.cloned.1.call-update) | async-done | bytes 1048592 | tf_op jit(solution)/shard_map/reduce_scatter | solution.py:76
  250.2 33.7 %reduce-scatter.26.cloned.1.call-done = bf16[32,1024]{1,0:T(8,128)(2,1)} async-done(((bf16[256,1024]{1,0:T(8,128)(2,1)}), bf16[32,1024]{1,0:T(8,128)(2,1)}) %reduce-scatter.26.cloned.1.call-update) | async-done | bytes 65552 | tf_op jit(solution)/shard_map/reduce_scatter | solution.py:76
  296.2 53.2 %all-gather.22.cloned.1.call-done = bf16[3,4,1024,128]{3,2,1,0:T(8,128)(2,1)} async-done(((bf16[3,4,256,128]{3,2,1,0:T(8,128)(2,1)}), bf16[3,4,1024,128]{3,2,1,0:T(8,128)(2,1)}) %all-gather.22.cloned.1.call-update) | async-done | bytes 3145744 | tf_op jit(solution)/shard_map/all_gather | solution.py:389
  357.4 47.4 %all-gather.20.cloned.1.call-done = bf16[4096,1024]{1,0:T(8,128)(2,1)} async-done(((bf16[512,1024]{1,0:T(8,128)(2,1)}), bf16[4096,1024]{1,0:T(8,128)(2,1)}) %all-gather.20.cloned.1.call-update) | async-done | bytes 8388624 | tf_op jit(solution)/shard_map/all_gather | solution.py:70
  437.6 38.5 %while.47 = (s32[]{:T(128)}, bf16[4,1024,2,64]{1,3,2,0:T(8,128)(2,1)}, f32[4,2,1024,1]{2,1,3,0:T(2,128)}, bf16[4,1024,2,64]{1,3,2,0:T(8,128)(2,1)S(1)}, bf16[4,1...) while((s32[]{:T(128)}, ...), condition=%wide.region_7.8_spmd, body=%wide.region_2.7_spmd.sunk | while | flops 563741184 | bytes 31556224 | solution.py:188
  500.1 25.5 %all-gather.26.cloned.1.call-done = bf16[2,2,1024,512]{3,2,1,0:T(8,128)(2,1)} async-done(((bf16[2,2,256,512]{3,2,1,0:T(8,128)(2,1)}), bf16[2,2,1024,512]{3,2,1,0:T(8,128)(2,1)}) %all-gather.26.cloned.1.call-update) | async-done | bytes 4194320 | tf_op jit(solution)/shard_map/all_gather | solution.py:390
  531.9 67.5 %reduce-scatter.24.cloned.1.call-done = bf16[512,1024]{1,0:T(8,128)(2,1)} async-done(((bf16[4096,1024]{1,0:T(8,128)(2,1)}), bf16[512,1024]{1,0:T(8,128)(2,1)}) %reduce-scatter.24.cloned.1.call-update) | async-done | bytes 1048592 | tf_op jit(solution)/shard_map/reduce_scatter | solution.py:76
  605.0 32.0 %reduce-scatter.30.cloned.1.call-done = bf16[32,1024]{1,0:T(8,128)(2,1)} async-done(((bf16[256,1024]{1,0:T(8,128)(2,1)}), bf16[32,1024]{1,0:T(8,128)(2,1)}) %reduce-scatter.30.cloned.1.call-update) | async-done | bytes 65552 | tf_op jit(solution)/shard_map/reduce_scatter | solution.py:76
  653.5 40.5 %all-gather.28.cloned.1.call-done = bf16[4096,1024]{1,0:T(8,128)(2,1)} async-done(((bf16[512,1024]{1,0:T(8,128)(2,1)}), bf16[4096,1024]{1,0:T(8,128)(2,1)}) %all-gather.28.cloned.1.call-update) | async-done | bytes 8388624 | tf_op jit(solution)/shard_map/all_gather | solution.py:70
  722.8 71.4 %reduce-scatter.32.cloned.1.call-done = bf16[512,1024]{1,0:T(8,128)(2,1)} async-done(((bf16[4096,1024]{1,0:T(8,128)(2,1)}), bf16[512,1024]{1,0:T(8,128)(2,1)}) %reduce-scatter.32.cloned.1.call-update) | async-done | bytes 1048592 | tf_op jit(solution)/shard_map/reduce_scatter | solution.py:76
  797.6 54.5 %all-gather.30.cloned.1.call-done = bf16[4096,1024]{1,0:T(8,128)(2,1)} async-done(((bf16[512,1024]{1,0:T(8,128)(2,1)}), bf16[4096,1024]{1,0:T(8,128)(2,1)}) %all-gather.30.cloned.1.call-update) | async-done | bytes 8388624 | tf_op jit(solution)/shard_map/all_gather | solution.py:70
  852.1 25.7 %multiply_convert_fusion.4 = (bf16[4096,512]{1,0:T(8,128)(2,1)S(1)}, f32[4096,512]{1,0:T(8,128)}, f32[4096,512]{1,0:T(8,128)}) fusion(bf16[4096,1024]{1,0:T(8,128)(2,1)} %all-gather.30.cloned.1.call-done, bf16[2,2,1024,512]{3,2,1,0:T(8,128)(2,1)} %all-gather.26.cloned.1.call-done), kind=kOutput, calls=%fused_computation.137 | convolution fusion | flops 4431282176 | bytes 30408704 | tf_op jit(solution)/shard_map/dot_general | solution.py:310
  887.9 71.3 %reduce-scatter.34.cloned.1.call-done = bf16[512,1024]{1,0:T(8,128)(2,1)} async-done(((bf16[4096,1024]{1,0:T(8,128)(2,1)}), bf16[512,1024]{1,0:T(8,128)(2,1)}) %reduce-scatter.34.cloned.1.call-update) | async-done | bytes 1048592 | tf_op jit(solution)/shard_map/reduce_scatter | solution.py:76
  964.1 53.8 %all-gather.32.cloned.1.call-done = bf16[4096,1024]{1,0:T(8,128)(2,1)} async-done(((bf16[512,1024]{1,0:T(8,128)(2,1)}), bf16[4096,1024]{1,0:T(8,128)(2,1)}) %all-gather.32.cloned.1.call-update) | async-done | bytes 8388624 | tf_op jit(solution)/shard_map/all_gather | solution.py:70
  1105.3 68.6 %reduce-scatter.36.cloned.1.call-done = bf16[512,1024]{1,0:T(8,128)(2,1)} async-done(((bf16[4096,1024]{1,0:T(8,128)(2,1)}), bf16[512,1024]{1,0:T(8,128)(2,1)}) %reduce-scatter.36.cloned.1.call-update) | async-done | bytes 1048592 | tf_op jit(solution)/shard_map/reduce_scatter | solution.py:88
  1178.4 54.5 %all-gather.34.cloned.1.call-done = bf16[4096,1024]{1,0:T(8,128)(2,1)} async-done(((bf16[512,1024]{1,0:T(8,128)(2,1)}), bf16[4096,1024]{1,0:T(8,128)(2,1)}) %all-gather.34.cloned.1.call-update) | async-done | bytes 8388624 | tf_op jit(solution)/shard_map/all_gather | solution.py:82
  1256.7 71.4 %reduce-scatter.38.cloned.1.call-done = bf16[512,1024]{1,0:T(8,128)(2,1)} async-done(((bf16[4096,1024]{1,0:T(8,128)(2,1)}), bf16[512,1024]{1,0:T(8,128)(2,1)}) %reduce-scatter.38.cloned.1.call-update) | async-done | bytes 1048592 | tf_op jit(solution)/shard_map/reduce_scatter | solution.py:88
  1334.2 54.4 %all-gather.36.cloned.1.call-done = bf16[4096,1024]{1,0:T(8,128)(2,1)} async-done(((bf16[512,1024]{1,0:T(8,128)(2,1)}), bf16[4096,1024]{1,0:T(8,128)(2,1)}) %all-gather.36.cloned.1.call-update) | async-done | bytes 8388624 | tf_op jit(solution)/shard_map/all_gather | solution.py:82
  1424.6 59.3 %reduce-scatter.44.cloned.1.call-done = bf16[512,1024]{1,0:T(8,128)(2,1)} async-done(((bf16[4096,1024]{1,0:T(8,128)(2,1)}), bf16[512,1024]{1,0:T(8,128)(2,1)}) %reduce-scatter.44.cloned.1.call-update) | async-done | bytes 1048592 | tf_op jit(solution)/shard_map/reduce_scatter | solution.py:88
  1490.0 31.7 %reduce-scatter.40.cloned.1.call-done = bf16[32,1024]{1,0:T(8,128)(2,1)} async-done(((bf16[256,1024]{1,0:T(8,128)(2,1)}), bf16[32,1024]{1,0:T(8,128)(2,1)}) %reduce-scatter.40.cloned.1.call-update) | async-done | bytes 65552 | tf_op jit(solution)/shard_map/reduce_scatter | solution.py:88
  1539.0 39.8 %all-gather.38.cloned.1.call-done = bf16[4096,1024]{1,0:T(8,128)(2,1)} async-done(((bf16[512,1024]{1,0:T(8,128)(2,1)}), bf16[4096,1024]{1,0:T(8,128)(2,1)}) %all-gather.38.cloned.1.call-update) | async-done | bytes 8388624 | tf_op jit(solution)/shard_map/all_gather | solution.py:82
  1596.9 77.3 %while.49 = (s32[]{:T(128)}, bf16[4,1024,2,64]{1,3,2,0:T(8,128)(2,1)}, bf16[4,1024,2,64]{1,3,2,0:T(8,128)(2,1)}, bf16[4,1024,2,64]{1,3,2,0:T(8,128)(2,1)}, bf16[...) while((s32[]{:T(128)}, ...), condition=%wide.region_51.54_spmd, body=%wide.region_48.53_spmd.sunk | while | flops 1375861248 | bytes 98924368 | solution.py:211
  1736.6 50.0 %reduce-scatter.54.cloned.1.call-done = bf16[512,1024]{1,0:T(8,128)(2,1)} async-done(((bf16[4096,1024]{1,0:T(8,128)(2,1)}), bf16[512,1024]{1,0:T(8,128)(2,1)}) %reduce-scatter.54.cloned.1.call-update) | async-done | bytes 1048592 | tf_op jit(solution)/shard_map/reduce_scatter | solution.py:88
  1895.6 38.2 %scatter_custom_fusion.3 = f32[1024,1024]{1,0:T(8,128)} fusion(s32[4096]{0:T(1024)} %bitcast.636, bf16[4096,1024]{1,0:T(8,128)(2,1)} %all-gather.40.cloned.1.call-done, f32[4096]{0:T(1024)S(1)} %bitcast.608, f32[]{:T(128)} %constant.124.clone.1), kind=kCustom, calls=%fused_computation.125 | custom fusion | flops 12582912 | bytes 12599808 | tf_op jit(solution)/shard_map/scatter-add | solution.py:348
  1962.9 75.8 %reduce-scatter.52.cloned.1.call-done = bf16[2000,256]{1,0:T(8,128)(2,1)} async-done(((bf16[2000,1024]{1,0:T(8,128)(2,1)}), bf16[2000,256]{1,0:T(8,128)(2,1)}) %reduce-scatter.52.cloned.1.call-update) | async-done | bytes 1024016 | tf_op jit(solution)/shard_map/reduce_scatter | solution.py:511
  2041.1 60.7 %reduce-scatter.46.cloned.1.call-done = bf16[3,4,256,128]{3,2,1,0:T(8,128)(2,1)} async-done(((bf16[3,4,1024,128]{3,2,1,0:T(8,128)(2,1)}), bf16[3,4,256,128]{3,2,1,0:T(8,128)(2,1)}) %reduce-scatter.46.cloned.1.call-update) | async-done | bytes 786448 | tf_op jit(solution)/shard_map/reduce_scatter | solution.py:499
  2105.9 132.2 %reduce-scatter.58.cloned.1.call-done = f32[32,7]{1,0:T(8,128)} async-done(((f32[1024,7]{1,0:T(8,128)}), f32[32,7]{1,0:T(8,128)}) %reduce-scatter.58.cloned.1.call-update) | async-done | bytes 912
  2239.5 73.7 %reduce-scatter.56.cloned.1.call-done = bf16[2,1024,256]{2,1,0:T(8,128)(2,1)} async-done(((bf16[2,1024,1024]{2,1,0:T(8,128)(2,1)}), bf16[2,1024,256]{2,1,0:T(8,128)(2,1)}) %reduce-scatter.56.cloned.1.call-update) | async-done | bytes 1048592 | tf_op jit(solution)/shard_map/reduce_scatter | solution.py:514
  2318.3 40.8 %psum.23 = f32[]{:T(128)} all-reduce(f32[]{:T(128)S(6)} %add.510), channel_id=1, replica_groups=mesh['dp'=4,'mp'=8] {'dp','mp'}, use_global_device_ids=true, to_apply=%region_75.78 | all-reduce | flops 1 | bytes 8 | tf_op jit(solution)/shard_map/psum | solution.py:534
  (883 shorter events, 743.0 us)
Async XLA Ops:
  7.2 86.3 %all-gather.18.cloned.1.call-start = ((), (), s32[]{:S(2)}) async-start(), calls=%async_computation.19 | async-start | bytes 5242880 | tf_op jit(solution)/shard_map/all_gather | solution.py:392
  10.1 162.7 %all-gather.24.cloned.1.call-start = ((), (), s32[]{:S(2)}) async-start(), calls=%async_computation.24 | async-start | bytes 5120000 | tf_op jit(solution)/shard_map/all_gather | solution.py:391
  11.2 234.7 %reduce-scatter.22.cloned.1.call-start = ((), (), s32[]{:S(2)}) async-start(), calls=%async_computation.20 | async-start | bytes 9437184 | tf_op jit(solution)/shard_map/reduce_scatter | solution.py:76
  121.5 162.4 %reduce-scatter.26.cloned.1.call-start = ((), (), s32[]{:S(2)}) async-start(), calls=%async_computation.25 | async-start | bytes 589824 | tf_op jit(solution)/shard_map/reduce_scatter | solution.py:76
  178.1 171.2 %all-gather.22.cloned.1.call-start = ((), (), s32[]{:S(2)}) async-start(), calls=%async_computation.22 | async-start | bytes 3932160 | tf_op jit(solution)/shard_map/all_gather | solution.py:389
  179.2 225.5 %all-gather.20.cloned.1.call-start = ((), (), s32[]{:S(2)}) async-start(), calls=%async_computation.21 | async-start | bytes 9437184 | tf_op jit(solution)/shard_map/all_gather | solution.py:70
  219.2 577.1 %copy-start.112 = (f32[1,1024]{1,0:T(1,128)}, f32[1,1024]{1,0:T(1,128)S(1)}, u32[]{:S(2)}) copy-start(f32[1,1024]{1,0:T(1,128)S(1)} %get-tuple-element.523) | copy-start | bytes 12292
  250.0 237.1 %reduce-scatter.28.cloned.1.call-start = ((), (), s32[]{:S(2)}) async-start(), calls=%async_computation.26 | async-start | bytes 589824 | tf_op jit(solution)/shard_map/reduce_scatter | solution.py:76
  356.1 169.5 %all-gather.26.cloned.1.call-start = ((), (), s32[]{:S(2)}) async-start(), calls=%async_computation.27 | async-start | bytes 5242880 | tf_op jit(solution)/shard_map/all_gather | solution.py:390
  357.3 242.0 %reduce-scatter.24.cloned.1.call-start = ((), (), s32[]{:S(2)}) async-start(), calls=%async_computation.23 | async-start | bytes 9437184 | tf_op jit(solution)/shard_map/reduce_scatter | solution.py:76
  487.0 149.9 %reduce-scatter.30.cloned.1.call-start = ((), (), s32[]{:S(2)}) async-start(), calls=%async_computation.28 | async-start | bytes 589824 | tf_op jit(solution)/shard_map/reduce_scatter | solution.py:76
  531.8 162.2 %all-gather.28.cloned.1.call-start = ((), (), s32[]{:S(2)}) async-start(), calls=%async_computation.29 | async-start | bytes 9437184 | tf_op jit(solution)/shard_map/all_gather | solution.py:70
  603.6 190.6 %reduce-scatter.32.cloned.1.call-start = ((), (), s32[]{:S(2)}) async-start(), calls=%async_computation.30 | async-start | bytes 9437184 | tf_op jit(solution)/shard_map/reduce_scatter | solution.py:76
  722.7 129.4 %all-gather.30.cloned.1.call-start = ((), (), s32[]{:S(2)}) async-start(), calls=%async_computation.31 | async-start | bytes 9437184 | tf_op jit(solution)/shard_map/all_gather | solution.py:70
  797.6 161.7 %reduce-scatter.34.cloned.1.call-start = ((), (), s32[]{:S(2)}) async-start(), calls=%async_computation.32 | async-start | bytes 9437184 | tf_op jit(solution)/shard_map/reduce_scatter | solution.py:76
  887.9 130.1 %all-gather.32.cloned.1.call-start = ((), (), s32[]{:S(2)}) async-start(), calls=%async_computation.33 | async-start | bytes 9437184 | tf_op jit(solution)/shard_map/all_gather | solution.py:70
  963.4 210.5 %reduce-scatter.36.cloned.1.call-start = ((), (), s32[]{:S(2)}) async-start(), calls=%async_computation.34 | async-start | bytes 9437184 | tf_op jit(solution)/shard_map/reduce_scatter | solution.py:88
  1105.2 127.7 %all-gather.34.cloned.1.call-start = ((), (), s32[]{:S(2)}) async-start(), calls=%async_computation.35 | async-start | bytes 9437184 | tf_op jit(solution)/shard_map/all_gather | solution.py:82
  1178.3 149.7 %reduce-scatter.38.cloned.1.call-start = ((), (), s32[]{:S(2)}) async-start(), calls=%async_computation.36 | async-start | bytes 9437184 | tf_op jit(solution)/shard_map/reduce_scatter | solution.py:88
  1256.6 132.1 %all-gather.36.cloned.1.call-start = ((), (), s32[]{:S(2)}) async-start(), calls=%async_computation.37 | async-start | bytes 9437184 | tf_op jit(solution)/shard_map/all_gather | solution.py:82
  1334.1 149.8 %reduce-scatter.44.cloned.1.call-start = ((), (), s32[]{:S(2)}) async-start(), calls=%async_computation.40 | async-start | bytes 9437184 | tf_op jit(solution)/shard_map/reduce_scatter | solution.py:88
  1412.5 109.2 %reduce-scatter.40.cloned.1.call-start = ((), (), s32[]{:S(2)}) async-start(), calls=%async_computation.38 | async-start | bytes 589824 | tf_op jit(solution)/shard_map/reduce_scatter | solution.py:88
  1424.6 154.2 %all-gather.38.cloned.1.call-start = ((), (), s32[]{:S(2)}) async-start(), calls=%async_computation.41 | async-start | bytes 9437184 | tf_op jit(solution)/shard_map/all_gather | solution.py:82
  1490.0 225.9 %reduce-scatter.42.cloned.1.call-start = ((), (), s32[]{:S(2)}) async-start(), calls=%async_computation.39 | async-start | bytes 589824 | tf_op jit(solution)/shard_map/reduce_scatter | solution.py:88
  1539.0 247.7 %reduce-scatter.54.cloned.1.call-start = ((), (), s32[]{:S(2)}) async-start(), calls=%async_computation.46 | async-start | bytes 9437184 | tf_op jit(solution)/shard_map/reduce_scatter | solution.py:88
  1715.3 109.5 %reduce-scatter.50.cloned.1.call-start = ((), (), s32[]{:S(2)}) async-start(), calls=%async_computation.44 | async-start | bytes 589824 | tf_op jit(solution)/shard_map/reduce_scatter | solution.py:88
  1736.6 159.0 %all-gather.40.cloned.1.call-start = ((), (), s32[]{:S(2)}) async-start(), calls=%async_computation.47 | async-start | bytes 9437184 | tf_op jit(solution)/shard_map/all_gather | solution.py:82
  1792.6 167.9 %reduce-scatter.48.cloned.1.call-start = ((), (), s32[]{:S(2)}) async-start(), calls=%async_computation.43 | async-start | bytes 5242880 | tf_op jit(solution)/shard_map/reduce_scatter | solution.py:505
  1813.8 224.9 %reduce-scatter.52.cloned.1.call-start = ((), (), s32[]{:S(2)}) async-start(), calls=%async_computation.45 | async-start | bytes 5120000 | tf_op jit(solution)/shard_map/reduce_scatter | solution.py:511
  1849.2 252.5 %reduce-scatter.46.cloned.1.call-start = ((), (), s32[]{:S(2)}) async-start(), calls=%async_computation.42 | async-start | bytes 3932160 | tf_op jit(solution)/shard_map/reduce_scatter | solution.py:499
  1877.3 360.7 %reduce-scatter.58.cloned.1.call-start = ((), (), s32[]{:S(2)}) async-start(), calls=%async_computation.49 | async-start | bytes 540672
  1895.2 417.9 %reduce-scatter.56.cloned.1.call-start = ((), (), s32[]{:S(2)}) async-start(), calls=%async_computation.48 | async-start | bytes 5242880 | tf_op jit(solution)/shard_map/reduce_scatter | solution.py:514
  (205 other events, 7023.5 us)
Sparse Core Ops, SparseCore 0:
  10.2 83.2 all-gather.17
  95.6 77.1 all-gather.23
  176.3 69.5 reduce-scatter.21
  249.7 34.1 reduce-scatter.25
  285.9 63.4 all-gather.21
  351.7 53.0 all-gather.19
  408.4 34.1 reduce-scatter.27
  444.8 80.7 all-gather.25
  529.5 69.8 reduce-scatter.23
  602.8 34.0 reduce-scatter.29
  639.6 54.3 all-gather.27
  722.8 71.3 reduce-scatter.31
  797.7 54.3 all-gather.29
  888.0 71.2 reduce-scatter.33
  963.5 54.3 all-gather.31
  1105.3 68.5 reduce-scatter.35
  1178.5 54.3 all-gather.33
  1256.7 71.2 reduce-scatter.37
  1334.3 54.3 all-gather.35
  1412.6 71.2 reduce-scatter.43
  1487.6 34.1 reduce-scatter.39
  1524.4 54.3 all-gather.37
  1582.8 34.1 reduce-scatter.41
  1715.4 71.2 reduce-scatter.53
  1790.6 34.1 reduce-scatter.49
  1827.1 54.4 all-gather.39
  1883.7 76.7 reduce-scatter.47
  1962.9 75.7 reduce-scatter.51
  2041.0 60.6 reduce-scatter.45
  2104.4 133.5 reduce-scatter.57
  2240.5 72.6 reduce-scatter.55
where the time goes:
time: 2400 us; the launch traced here: 2390 us
  waiting for transfers between devices  1510 us (63%)
  matrix products  355 us (15%)
  other arithmetic  202 us (8%)
  blocking collectives  187 us (8%)
  local copies, waits for them, and re-layouts  109 us (5%)
  between operations  25.3 us (1%)
    reduce_scatter x7, waiting for transfers between devices, collect_forward(): lax.psum_scatter(values.astype(jnp.bfloat16), 'mp', scatter_dimension=0,...  303 us
    reduce_scatter x7, waiting for transfers between devices, collect_backward(): lax.psum_scatter(for_sending(values), 'mp', scatter_dimension=0, tiled=True)  292 us
    all_gather x4, waiting for transfers between devices, spread_forward(): lax.all_gather(for_sending(values), 'mp', axis=0, tiled=True)  196 us
    dot_general x34, matrix products, product(): lax.dot_general(left, right, dims, preferred_element_type=jnp.float32)  157 us
    all_gather x4, waiting for transfers between devices, spread_backward(): return lax.all_gather(values, 'mp', axis=0, tiled=True)  149 us
    unnamed x32, waiting for transfers between devices  133 us
    all_gather x1, waiting for transfers between devices, per_device(): lax.all_gather(code_master.astype(jnp.bfloat16), 'dp', axis=2, tiled=True)  81.3 us
    reduce_scatter x1, waiting for transfers between devices, per_device(): lax.psum_scatter(grad_text.astype(jnp.bfloat16), 'dp', scatter_dimension=...  75.8 us
  transfers between devices with their start and end apart: 31, of which 28 were waited for; matrix products, arithmetic and copies ran while one was open for 19% of the time, Pallas kernels for 0%

commit v1 on v0

v1 whole, which is shorter than its diff:
```python
from functools import partial
import math

import jax
import jax.numpy as jnp
from jax import lax
from jax.experimental import pallas as pl
from jax.experimental.pallas import tpu as pltpu
from jax.sharding import Mesh, PartitionSpec as P

D = 1024
HEAD_DIM = 64
FF = 4096
VC = 8192
VT = 16000


EPS = 1e-06
CLIP = 0.01
MOMENT = 0.9
DECAY = 0.75
SMOOTH = 0.1
Z_WEIGHT = 0.01
NEGATIVE = -1e30
LAST = (((1,), (1,)), ((), ()))
FIRST = (((0,), (0,)), ((), ()))


MESH = pl.DeviceIdType.MESH
ORDERS = ((0, 1, 2), (0, 2, 1), (1, 0, 2), (2, 0, 1))


def sources(n):
    return [(far, bits) for far in range(1 - n, n) for bits in range(4)]


def hops(far, bits):
    return abs(far) + (bits & 1) + (bits >> 1)


def arrival(order, far, bits):
    last = None
    for dim in order:
        if (dim == 0 and far != 0) or (dim > 0 and bits & dim):
            last = dim
    return last


def passes(order, far, bits):
    came = arrival(order, far, bits)
    place = -1 if came is None else order.index(came)
    found = [(0, -1 if far > 0 else 1)] if came == 0 else []
    for dim in order[place + 1 :]:
        found += [(0, 1), (0, -1)] if dim == 0 else [(dim, 0)]
    return found


def cut_slabs(shapes, gap):
    slabs = []
    base = 0.0
    for which, (rows, _) in enumerate(shapes):
        small = max(16, rows // 6 // 16 * 16)
        large = (rows - 2 * small) // 2 // 16 * 16
        begin = 0
        for order, count in zip(ORDERS, (small, small, large, rows - 2 * small - large)):
            slabs.append((which, begin, count, order, base))
            begin += count
        base += gap
    return slabs


def wide(shape, n):
    _, rows, columns = shape
    return (n * rows, 4 * columns) if columns % 128 == 0 else (4 * n * rows, columns)


def placed(whole, shape, z, i, begin, rows):
    if shape[2] % 128 == 0:
        return whole.at[
            :,
            pl.ds(pl.multiple_of(z * shape[1] + begin, 16), rows),
            pl.ds(pl.multiple_of(i * shape[2], 128), shape[2]),
        ]
    return whole.at[:, pl.ds(pl.multiple_of((z * 4 + i) * shape[1] + begin, 16), rows)]


class Here:
    def __init__(self, n):
        self.n = n
        self.z = lax.axis_index("dp")
        self.i = lax.axis_index("img")
        self.t = lax.axis_index("t")

    def device(self, dim, step):
        if dim == 0:
            return (self.z + step, self.i, self.t)
        return (self.z, jnp.bitwise_xor(self.i, dim), self.t)

    def below(self):
        return self.z > 0

    def above(self):
        return self.z < self.n - 1

    def side(self, step):
        return self.above() if step > 0 else self.below()

    def greet(self):
        barrier = pltpu.get_barrier_semaphore()

        def tell(device):
            pl.semaphore_signal(barrier, inc=1, device_id=device, device_id_type=MESH)

        pl.when(self.below())(lambda: tell(self.device(0, -1)))
        pl.when(self.above())(lambda: tell(self.device(0, 1)))
        tell(self.device(1, 0))
        tell(self.device(2, 0))
        pl.semaphore_wait(
            barrier, 2 + jnp.where(self.below(), 1, 0) + jnp.where(self.above(), 1, 0)
        )

    def exists(self, far):
        if far == 0:
            return None
        return (self.z + far >= 0) if far < 0 else (self.z + far < self.n)


def guarded(condition, action):
    if condition is None:
        action()
    else:
        pl.when(condition)(action)


def both(first, second):
    if first is None or second is None:
        return second if first is None else first
    return jnp.logical_and(first, second)


def gather_kernel(n, slabs, count, *refs):
    ins, outs = refs[:count], refs[count : 2 * count]
    send_sem, recv_sem, local_sem = refs[2 * count :]
    here = Here(n)
    here.greet()
    local = []
    for which in range(count):
        shape = ins[which].shape
        copy = pltpu.make_async_copy(
            ins[which], placed(outs[which], shape, here.z, here.i, 0, shape[1]), local_sem.at[which]
        )
        copy.start()
        local.append(copy)

    def block(slab, far, bits):
        which, begin, rows = slabs[slab][:3]
        return placed(
            outs[which], ins[which].shape, here.z + far, jnp.bitwise_xor(here.i, bits), begin, rows
        )

    def name(far, bits):
        return (here.z + far) * 4 + jnp.bitwise_xor(here.i, bits)

    def copy_of(slab, far, bits, dim, step):
        which, begin, rows = slabs[slab][:3]
        target = block(slab, far, bits)
        own = far == 0 and bits == 0
        return pltpu.make_async_remote_copy(
            src_ref=ins[which].at[:, pl.ds(begin, rows)] if own else target,
            dst_ref=target,
            send_sem=send_sem.at[slab, name(far, bits), (1 + step) // 2 if dim == 0 else 1 + dim],
            recv_sem=recv_sem.at[slab, name(far, bits)],
            device_id=here.device(dim, step),
            device_id_type=MESH,
        )

    def arrive(slab, far, bits):
        target = block(slab, far, bits)
        pltpu.make_async_remote_copy(
            src_ref=target,
            dst_ref=target,
            send_sem=send_sem.at[slab, 0, 0],
            recv_sem=recv_sem.at[slab, name(far, bits)],
            device_id=here.device(1, 0),
            device_id_type=MESH,
        ).wait_recv()

    events = sorted(
        (slabs[slab][4] + hops(far, bits), slab, far, bits)
        for slab in range(len(slabs))
        for far, bits in sources(n)
    )
    sent = []
    final = []
    for _, slab, far, bits in events:
        onward = passes(slabs[slab][3], far, bits)
        own = far == 0 and bits == 0
        if not onward:
            final.append((slab, far, bits))
            continue

        def act(slab=slab, far=far, bits=bits, onward=onward, own=own):
            if not own:
                arrive(slab, far, bits)
            for dim, step in onward:
                guarded(
                    here.side(step) if dim == 0 else None,
                    lambda dim=dim, step=step: copy_of(slab, far, bits, dim, step).start(),
                )

        guarded(here.exists(far), act)
        sent += [(slab, far, bits, dim, step) for dim, step in onward]
    for slab, far, bits in final:
        guarded(here.exists(far), lambda at=(slab, far, bits): arrive(*at))
    for slab, far, bits, dim, step in sent:
        guarded(
            both(here.exists(far), here.side(step) if dim == 0 else None),
            lambda at=(slab, far, bits, dim, step): copy_of(*at).wait_send(),
        )
    for copy in local:
        copy.wait()


def gather(arrays, n, gap, collective_id):
    count = len(arrays)
    slabs = cut_slabs([a.shape[1:] for a in arrays], gap)
    size = sum(a.size * a.dtype.itemsize for a in arrays) * 4 * n
    return pl.pallas_call(
        partial(gather_kernel, n, slabs, count),
        out_shape=[
            jax.ShapeDtypeStruct((a.shape[0],) + wide(a.shape, n), a.dtype) for a in arrays
        ],
        in_specs=[pl.BlockSpec(memory_space=pl.ANY)] * count,
        out_specs=[pl.BlockSpec(memory_space=pl.ANY)] * count,
        scratch_shapes=[
            pltpu.SemaphoreType.DMA((len(slabs), 4 * n, 4)),
            pltpu.SemaphoreType.DMA((len(slabs), 4 * n)),
            pltpu.SemaphoreType.DMA((count,)),
        ],
        compiler_params=pltpu.CompilerParams(
            collective_id=collective_id, has_side_effects=True
        ),
        cost_estimate=pl.CostEstimate(flops=0, bytes_accessed=size * 16, transcendentals=0),
        name="gather",
    )(*arrays)


def places(n, order):
    table = {}
    used = 0
    line = [b for b in range(4) if any(dim == 0 for dim, _ in passes(order, 0, b))]
    for rank, bits in enumerate(line):
        for far in range(1 - n, n):
            for dim, step in passes(order, far, bits):
                if dim == 0:
                    second = far == 0 and step < 0
                    table[far, bits, dim, step] = (
                        (used + n, False) if second else (used + far, True)
                    )
        used += n + 1
    for flip in (1, 2):
        pairs = [p for p in sources(n) if (flip, 0) in passes(order, *p)]
        spread = any(far for far, _ in pairs)
        for bits in sorted({b for _, b in pairs}):
            for far, other in pairs:
                if other == bits:
                    table[far, bits, flip, 0] = (used + far, True) if spread else (used, False)
            used += n if spread else 1
    return table, used


def scatter_kernel(n, slabs, members, *refs):
    total = sum(members)
    count = len(members)
    ins, refs = refs[:total], refs[total:]
    outs, owns, gots = refs[:count], refs[count : 2 * count], refs[2 * count : 3 * count]
    send_sem, recv_sem, local_sem = refs[3 * count :]
    here = Here(n)
    tables = {order: places(n, order)[0] for order in ORDERS}
    loads = []
    for which in range(count):
        for member in range(members[which]):
            matrix = ins[sum(members[:which]) + member]
            rows = owns[which].shape[2] // members[which]
            columns = owns[which].shape[3]
            for z in range(n):
                for i in range(4):
                    copy = pltpu.make_async_copy(
                        matrix.at[pl.ds(z * rows, rows), pl.ds(i * columns, columns)]
                        if matrix.shape[0] == n * rows
                        else matrix.at[pl.ds((z * 4 + i) * rows, rows)],
                        owns[which].at[z, i, pl.ds(member * rows, rows)],
                        local_sem.at[len(loads)],
                    )
                    copy.start()
                    loads.append(copy)
    here.greet()
    for copy in loads:
        copy.wait()

    def own(slab, far, bits):
        which, begin, rows = slabs[slab][:3]
        return owns[which].at[
            here.z + far, jnp.bitwise_xor(here.i, bits), pl.ds(begin, rows)
        ]

    def slot(slab, number):
        which, _, rows, _, _, first = slabs[slab]
        return gots[which].at[pl.ds(pl.multiple_of(first + number * rows, 16), rows)]

    def number_at(order, z, key):
        constant, counts = tables[order][key]
        return constant + z if counts else constant

    def copy_of(slab, far, bits):
        order = slabs[slab][3]
        dim = arrival(order, far, bits)
        step = 0 if dim else (1 if far > 0 else -1)
        number = number_at(order, here.z + step, (far - step, bits ^ dim, dim, -step))
        return pltpu.make_async_remote_copy(
            src_ref=own(slab, far, bits),
            dst_ref=slot(slab, number),
            send_sem=send_sem.at[slab, (here.z + far) * 4 + bits],
            recv_sem=recv_sem.at[slab, number],
            device_id=here.device(dim, step),
            device_id_type=MESH,
        )

    events = sorted(
        (slabs[slab][4] + n + 1 - hops(far, bits), slab, far, bits)
        for slab in range(len(slabs))
        for far, bits in sources(n)
    )

    def add_up(slab, far, bits, parts):
        which, begin, rows, order = slabs[slab][:4]
        numbers = [number_at(order, here.z, (far, bits) + part) for part in parts]
        for number in numbers:
            landed = slot(slab, number)
            pltpu.make_async_remote_copy(
                src_ref=landed,
                dst_ref=landed,
                send_sem=send_sem.at[slab, 0],
                recv_sem=recv_sem.at[slab, number],
                device_id=here.device(1, 0),
                device_id_type=MESH,
            ).wait_recv()
        root = far == 0 and bits == 0
        if not parts and not root:
            return
        mine = own(slab, far, bits)
        landed = [slot(slab, number) for number in numbers]

        @pl.loop(0, rows // 16)
        def _(row):
            at = pl.ds(pl.multiple_of(row * 16, 16), 16)
            added = mine[at].astype(jnp.float32)
            for part in landed:
                added = added + part[at].astype(jnp.float32)
            if root:
                outs[which][pl.ds(pl.multiple_of(begin + row * 16, 16), 16)] = added
            else:
                mine[at] = added.astype(jnp.bfloat16)

    for _, slab, far, bits in events:

        def act(slab=slab, far=far, bits=bits):
            parts = passes(slabs[slab][3], far, bits)
            fixed = [p for p in parts if p[0]]
            line = [p for p in parts if not p[0]]
            if not line:
                add_up(slab, far, bits, fixed)
            elif len(line) == 1:
                there = here.side(line[0][1])
                pl.when(there)(lambda: add_up(slab, far, bits, line + fixed))
                pl.when(jnp.logical_not(there))(lambda: add_up(slab, far, bits, fixed))
            else:
                low, high = here.below(), here.above()
                up, down = line
                pl.when(jnp.logical_and(low, high))(
                    lambda: add_up(slab, far, bits, line + fixed)
                )
                pl.when(jnp.logical_not(low))(lambda: add_up(slab, far, bits, [up] + fixed))
                pl.when(jnp.logical_not(high))(lambda: add_up(slab, far, bits, [down] + fixed))
            if far or bits:
                copy_of(slab, far, bits).start()

        guarded(here.exists(far), act)
    for _, slab, far, bits in events:
        if far or bits:
            guarded(
                here.exists(far),
                lambda at=(slab, far, bits): copy_of(*at).wait_send(),
            )


def scatter(groups, shapes, n, gap, collective_id):
    members = [len(group) for group in groups]
    slabs = []
    totals = [0] * len(groups)
    most = 0
    sizes = [(m * rows, columns) for m, (rows, columns) in zip(members, shapes)]
    for which, begin, rows, order, base in cut_slabs(sizes, gap):
        used = places(n, order)[1]
        slabs.append((which, begin, rows, order, base, totals[which]))
        totals[which] += rows * used
        most = max(most, used)
    size = sum(rows * columns for rows, columns in sizes) * 8 * n
    return pl.pallas_call(
        partial(scatter_kernel, n, slabs, members),
        out_shape=[jax.ShapeDtypeStruct(size, jnp.float32) for size in sizes],
        in_specs=[pl.BlockSpec(memory_space=pl.ANY)] * sum(members),
        out_specs=[pl.BlockSpec(memory_space=pltpu.VMEM)] * len(groups),
        scratch_shapes=[pltpu.VMEM((n, 4) + size, jnp.bfloat16) for size in sizes]
        + [pltpu.VMEM((total, size[1]), jnp.bfloat16) for size, total in zip(sizes, totals)]
        + [
            pltpu.SemaphoreType.DMA((len(slabs), 4 * n)),
            pltpu.SemaphoreType.DMA((len(slabs), most)),
            pltpu.SemaphoreType.DMA((4 * n * sum(members),)),
        ],
        compiler_params=pltpu.CompilerParams(
            collective_id=collective_id, has_side_effects=True, vmem_limit_bytes=58 * 2**20
        ),
        cost_estimate=pl.CostEstimate(flops=0, bytes_accessed=size * 16, transcendentals=0),
        name="scatter",
    )(*[matrix for group in groups for matrix in group])


class Row:
    def __init__(self, size):
        self.size = size
        self.parts = size // 4
        self.me = lax.axis_index("img") * self.parts + lax.axis_index("t")

    def other(self, step):
        return lax.rem(self.me + step, self.size)

    def device(self, index):
        return (lax.axis_index("dp"), index // self.parts, lax.rem(index, self.parts))


class Column:
    def __init__(self, size):
        self.size = size
        self.me = lax.axis_index("dp")

    def other(self, step):
        return lax.rem(self.me + step, self.size)

    def device(self, index):
        return (index, lax.axis_index("img"), lax.axis_index("t"))


def greet(*groups):
    barrier = pltpu.get_barrier_semaphore()
    for group in groups:
        for step in range(1, group.size):
            pl.semaphore_signal(
                barrier, inc=1, device_id=group.device(group.other(step)), device_id_type=MESH
            )
    pl.semaphore_wait(barrier, sum(group.size - 1 for group in groups))


def exchange(group, source, target, send_sem, recv_sem):
    def copy_of(step):
        index = group.other(step)
        return pltpu.make_async_remote_copy(
            src_ref=source(index),
            dst_ref=target(group.me),
            send_sem=send_sem.at[step],
            recv_sem=recv_sem.at[group.me],
            device_id=group.device(index),
            device_id_type=MESH,
        )

    for step in range(1, group.size):
        copy_of(step).start()
    for step in range(1, group.size):
        index = group.other(step)
        pltpu.make_async_remote_copy(
            src_ref=target(index),
            dst_ref=target(index),
            send_sem=send_sem.at[step],
            recv_sem=recv_sem.at[index],
            device_id=group.device(index),
            device_id_type=MESH,
        ).wait_recv()
    for step in range(1, group.size):
        copy_of(step).wait_send()


def row_block(ref, rows, index):
    return ref.at[pl.ds(pl.multiple_of(index * rows, 16), rows)]


def small_call(kernel, out_shape, scratch, operands, collective_id, name):
    vmem = pl.BlockSpec(memory_space=pltpu.VMEM)
    return pl.pallas_call(
        kernel,
        out_shape=out_shape,
        in_specs=[vmem] * len(operands),
        out_specs=vmem,
        scratch_shapes=scratch,
        compiler_params=pltpu.CompilerParams(
            collective_id=collective_id, has_side_effects=True
        ),
        cost_estimate=pl.CostEstimate(flops=0, bytes_accessed=2**24, transcendentals=0),
        name=name,
    )(*operands)


def semaphores(size):
    return [pltpu.SemaphoreType.DMA((size,)), pltpu.SemaphoreType.DMA((size,))]


def row_spread_kernel(size, mine, every, send_sem, recv_sem):
    row = Row(size)
    rows = mine.shape[0]
    greet(row)
    row_block(every, rows, row.me)[...] = mine[...]
    exchange(row, lambda _: mine, lambda index: row_block(every, rows, index), send_sem, recv_sem)


def row_spread(values):
    size = lax.axis_size("img") * lax.axis_size("t")
    return small_call(
        partial(row_spread_kernel, size),
        jax.ShapeDtypeStruct((size * values.shape[0], values.shape[1]), values.dtype),
        semaphores(size),
        [values],
        3,
        "row_spread",
    )


def row_sum(row, short, got, result, send_sem, recv_sem):
    rows = result.shape[0]
    row_block(got, rows, row.me)[...] = row_block(short, rows, row.me)[...]
    exchange(
        row,
        lambda index: row_block(short, rows, index),
        lambda index: row_block(got, rows, index),
        send_sem,
        recv_sem,
    )
    total = got[pl.ds(0, rows)].astype(jnp.float32)
    for index in range(1, row.size):
        total = total + got[pl.ds(index * rows, rows)].astype(jnp.float32)
    result[...] = total


def row_collect_kernel(size, values, result, short, got, send_sem, recv_sem):
    row = Row(size)
    short[...] = values[...].astype(jnp.bfloat16)
    greet(row)
    row_sum(row, short, got, result, send_sem, recv_sem)


def row_collect(values):
    size = lax.axis_size("img") * lax.axis_size("t")
    short = pltpu.VMEM(values.shape, jnp.bfloat16)
    return small_call(
        partial(row_collect_kernel, size),
        jax.ShapeDtypeStruct((values.shape[0] // size, values.shape[1]), jnp.float32),
        [short, short] + semaphores(size),
        [values],
        4,
        "row_collect",
    )


def text_in_kernel(n, size, picked, result, short, got, *sems):
    row, column = Row(size), Column(n)
    width = picked.shape[2]
    greet(row, column)

    def columns(index):
        return short.at[:, pl.ds(pl.multiple_of(index * width, 128), width)]

    columns(column.me)[...] = picked[column.me]
    exchange(column, lambda index: picked.at[index], columns, *sems[:2])
    row_sum(row, short, got, result, *sems[2:])


def text_in(picked):
    n, tokens, width = picked.shape
    size = lax.axis_size("img") * lax.axis_size("t")
    short = pltpu.VMEM((tokens, n * width), jnp.bfloat16)
    return small_call(
        partial(text_in_kernel, n, size),
        jax.ShapeDtypeStruct((tokens // size, n * width), jnp.float32),
        [short, short] + semaphores(n) + semaphores(size),
        [picked],
        5,
        "text_in",
    )


def text_back_kernel(n, size, mine, result, every, *sems):
    row, column = Row(size), Column(n)
    rows, width = mine.shape[0], result.shape[2]
    greet(row, column)
    row_block(every, rows, row.me)[...] = mine[...]
    exchange(row, lambda _: mine, lambda index: row_block(every, rows, index), *sems[:2])

    def columns(index):
        return every.at[:, pl.ds(pl.multiple_of(index * width, 128), width)]

    result[column.me] = columns(column.me)[...]
    exchange(column, columns, lambda index: result.at[index], *sems[2:])


def text_back(values):
    n = lax.axis_size("dp")
    size = lax.axis_size("img") * lax.axis_size("t")
    tokens = size * values.shape[0]
    width = values.shape[1] // n
    return small_call(
        partial(text_back_kernel, n, size),
        jax.ShapeDtypeStruct((n, tokens, width), values.dtype),
        [pltpu.VMEM((tokens, n * width), values.dtype)] + semaphores(size) + semaphores(n),
        [values],
        6,
        "text_back",
    )


def share_kernel(n, size, mine, every, *sems):
    row, column = Row(size), Column(n)
    greet(row, column)
    every[column.me, row.me] = mine[...]
    exchange(row, lambda _: mine, lambda index: every.at[column.me, index], *sems[:2])
    exchange(
        column, lambda _: every.at[column.me], lambda index: every.at[index], *sems[2:]
    )


def share(values):
    n = lax.axis_size("dp")
    size = lax.axis_size("img") * lax.axis_size("t")
    return small_call(
        partial(share_kernel, n, size),
        jax.ShapeDtypeStruct((n, size) + values.shape, values.dtype),
        semaphores(size) + semaphores(n),
        [values],
        7,
        "share",
    )


def total_kernel(n, size, mine, result, row_got, column_got, part, *sems):
    row, column = Row(size), Column(n)
    greet(row, column)
    row_got[row.me] = mine[...]
    exchange(row, lambda _: mine, lambda index: row_got.at[index], *sems[:2])
    added = row_got[0]
    for index in range(1, size):
        added = added + row_got[index]
    part[...] = added
    column_got[column.me] = added
    exchange(column, lambda _: part, lambda index: column_got.at[index], *sems[2:])
    added = column_got[0]
    for index in range(1, n):
        added = added + column_got[index]
    result[...] = added


def total_of(values):
    n = lax.axis_size("dp")
    size = lax.axis_size("img") * lax.axis_size("t")
    return small_call(
        partial(total_kernel, n, size),
        jax.ShapeDtypeStruct(values.shape, values.dtype),
        [
            pltpu.VMEM((size,) + values.shape, values.dtype),
            pltpu.VMEM((n,) + values.shape, values.dtype),
            pltpu.VMEM(values.shape, values.dtype),
        ]
        + semaphores(size)
        + semaphores(n),
        [values],
        8,
        "total",
    )


def rms_norm(values, gain):
    return values * lax.rsqrt(jnp.mean(values * values, axis=-1, keepdims=True) + EPS) * gain


def norm_back(values, gain, upstream):
    _, pull = jax.vjp(rms_norm, values, gain)
    return pull(upstream)


def gelu_exact(values):
    return jax.nn.gelu(values, approximate=False)


ROW = ("img", "t")


def spread(values, axis):
    if axis == "t" and lax.axis_size("t") == 2:
        other = lax.ppermute(values, "t", [(0, 1), (1, 0)])
        first = lax.axis_index("t") == 0
        return jnp.concatenate(
            [jnp.where(first, values, other), jnp.where(first, other, values)], axis=0
        )
    if axis == ROW:
        return row_spread(values)
    return lax.all_gather(values, axis, axis=0, tiled=True)


def collect(values, axis):
    if axis == "t" and lax.axis_size("t") == 2:
        half = values.shape[0] // 2
        place = lax.axis_index("t")
        away = lax.dynamic_slice_in_dim(values, (1 - place) * half, half, 0)
        came = lax.ppermute(away.astype(jnp.bfloat16), "t", [(0, 1), (1, 0)])
        return lax.dynamic_slice_in_dim(values, place * half, half, 0) + came.astype(jnp.float32)
    if axis == ROW:
        return row_collect(values)
    return lax.psum_scatter(
        values.astype(jnp.bfloat16), axis, scatter_dimension=0, tiled=True
    ).astype(jnp.float32)


def product(left, right, dims):
    return lax.dot_general(left, right, dims, preferred_element_type=jnp.float32)


def split_heads(values, groups):
    return values.reshape(groups, values.shape[0] // groups, values.shape[1] // HEAD_DIM, HEAD_DIM)


def core_forward(query, key, value, allowed, scale):
    scores = jnp.einsum("bqhe,bkhe->bhqk", query, key, preferred_element_type=jnp.float32) * scale
    scores = jnp.where(allowed[:, None], scores, NEGATIVE)
    highest = jnp.max(scores, axis=-1, keepdims=True)
    weight = jnp.exp(scores - highest)
    totals = jnp.sum(weight, axis=-1, keepdims=True)
    shares = (weight / totals).astype(jnp.bfloat16)
    mixed = jnp.einsum("bhqk,bkhe->bqhe", shares, value, preferred_element_type=jnp.float32)
    return (mixed.astype(jnp.bfloat16), highest + jnp.log(totals))


def core_backward(query, key, value, allowed, scale, partition, upstream):
    scores = jnp.einsum("bqhe,bkhe->bhqk", query, key, preferred_element_type=jnp.float32) * scale
    scores = jnp.where(allowed[:, None], scores, NEGATIVE)
    shares = jnp.exp(scores - partition)
    grad_value = jnp.einsum(
        "bhqk,bqhe->bkhe", shares.astype(jnp.bfloat16), upstream, preferred_element_type=jnp.float32
    )
    grad_shares = jnp.einsum("bqhe,bkhe->bhqk", upstream, value, preferred_element_type=jnp.float32)
    inner = jnp.sum(shares * grad_shares, axis=-1, keepdims=True)
    grad_scores = (shares * (grad_shares - inner)).astype(jnp.bfloat16)
    grad_query = (
        jnp.einsum("bhqk,bkhe->bqhe", grad_scores, key, preferred_element_type=jnp.float32) * scale
    )
    grad_key = (
        jnp.einsum("bhqk,bqhe->bkhe", grad_scores, query, preferred_element_type=jnp.float32)
        * scale
    )
    return (grad_query, grad_key, grad_value)


def causal_forward(parts, scale):
    query, key, value = parts
    length = query.shape[0]
    block = min(512, length)
    places = jnp.arange(length)
    outputs = []
    partitions = []
    for begin in range(0, length, block):
        allowed = begin + places[:block, None] >= places[None, :]
        mixed, partition = core_forward(
            query[None, begin : begin + block], key[None], value[None], allowed[None], scale
        )
        outputs.append(mixed[0])
        partitions.append(partition[0])
    return (jnp.concatenate(outputs, axis=0), jnp.concatenate(partitions, axis=1))


def causal_backward(parts, scale):
    query, key, value, partition, upstream = parts
    length = query.shape[0]
    block = min(512, length)
    places = jnp.arange(length)
    query_parts = []
    grad_key = jnp.zeros(key.shape, jnp.float32)
    grad_value = jnp.zeros(value.shape, jnp.float32)
    for begin in range(0, length, block):
        allowed = begin + places[:block, None] >= places[None, :]
        part_query, part_key, part_value = core_backward(
            query[None, begin : begin + block],
            key[None],
            value[None],
            allowed[None],
            scale,
            partition[None, :, begin : begin + block],
            upstream[None, begin : begin + block],
        )
        query_parts.append(part_query[0])
        grad_key = grad_key + part_key[0]
        grad_value = grad_value + part_value[0]
    return (jnp.concatenate(query_parts, axis=0), grad_key, grad_value)


def mix_forward(query, key, value, kind, context):
    scale = HEAD_DIM ** (-0.5)
    width = query.shape[1]
    query, key, value = (split_heads(part, 1) for part in (query, key, value))
    if kind == "self":
        mixed, partition = causal_forward((query[0], key[0], value[0]), scale)
        partition = partition[None]
    else:
        mixed, partition = core_forward(query, key, value, context["allowed"], scale)
    return (mixed.reshape(-1, width), partition)


def mix_backward(query, key, value, partition, upstream, kind, context):
    scale = HEAD_DIM ** (-0.5)
    width = query.shape[1]
    query, key, value, upstream = (split_heads(part, 1) for part in (query, key, value, upstream))
    if kind == "self":
        grads = causal_backward((query[0], key[0], value[0], partition[0], upstream[0]), scale)
    else:
        grads = core_backward(
            query, key, value, context["allowed"], scale, partition, upstream
        )
    return tuple(grad.reshape(-1, width).astype(jnp.bfloat16) for grad in grads)


def attention_forward(values, gain, weights, kind, axis, context, source=None):
    normed = rms_norm(values, gain).astype(jnp.bfloat16)
    inputs = spread(normed, axis)
    if source is None:
        source = inputs
    query = jnp.dot(inputs, weights[0], preferred_element_type=jnp.float32).astype(jnp.bfloat16)
    key = jnp.dot(source, weights[1], preferred_element_type=jnp.float32).astype(jnp.bfloat16)
    value = jnp.dot(source, weights[2], preferred_element_type=jnp.float32).astype(jnp.bfloat16)
    mixed, partition = mix_forward(query, key, value, kind, context)
    output = collect(product(mixed, weights[3], LAST), axis)
    return (output, (inputs, source, query, key, value, mixed, partition))


def attention_backward(upstream, values, gain, weights, kind, axis, context, kept):
    inputs, source, query, key, value, mixed, partition = kept
    grad_rows = spread(upstream.astype(jnp.bfloat16), axis)
    grad_out = product(grad_rows, mixed, FIRST)
    grad_mixed = jnp.dot(grad_rows, weights[3], preferred_element_type=jnp.float32).astype(
        jnp.bfloat16
    )
    grad_query, grad_key, grad_value = mix_backward(
        query, key, value, partition, grad_mixed, kind, context
    )
    grads = [
        product(inputs, grad_query, FIRST).astype(jnp.bfloat16),
        product(source, grad_key, FIRST).astype(jnp.bfloat16),
        product(source, grad_value, FIRST).astype(jnp.bfloat16),
        grad_out.astype(jnp.bfloat16),
    ]
    from_query = product(grad_query, weights[0], LAST)
    from_source = product(grad_key, weights[1], LAST) + product(grad_value, weights[2], LAST)
    if kind == "cross":
        grad_normed = collect(from_query, axis)
    else:
        grad_normed = collect(from_query + from_source, axis)
    grad_values, grad_gain = norm_back(values, gain, grad_normed)
    return (grad_values, grad_gain, grads, from_source)


def dense_forward(values, gain, weights, axis):
    normed = rms_norm(values, gain).astype(jnp.bfloat16)
    inputs = spread(normed, axis)
    hidden = jnp.dot(inputs, weights[0], preferred_element_type=jnp.float32)
    active = gelu_exact(hidden).astype(jnp.bfloat16)
    output = collect(product(active, weights[1], LAST), axis)
    return (output, (inputs, weights, hidden, active))


def dense_backward(upstream, values, gain, axis, kept):
    inputs, matrices, hidden, active = kept
    grad_rows = spread(upstream.astype(jnp.bfloat16), axis)
    grad_active = jnp.dot(grad_rows, matrices[1], preferred_element_type=jnp.float32)
    _, pull = jax.vjp(gelu_exact, hidden)
    grad_hidden = pull(grad_active)[0].astype(jnp.bfloat16)
    grads = [
        product(inputs, grad_hidden, FIRST).astype(jnp.bfloat16),
        product(grad_rows, active, FIRST).astype(jnp.bfloat16),
    ]
    grad_normed = collect(product(grad_hidden, matrices[0], LAST), axis)
    grad_values, grad_gain = norm_back(values, gain, grad_normed)
    return (grad_values, grad_gain, grads)


def code_hits(token_ids, usable, vocab):
    local = token_ids - lax.axis_index(ROW) * vocab
    places = jnp.arange(vocab, dtype=jnp.int32)
    return ((local[:, None] == places[None, :]) & usable[:, None]).astype(jnp.bfloat16)


def code_forward(token_ids, usable, table):
    hits = code_hits(token_ids, usable, table.shape[0])
    picked = jnp.dot(hits, table, preferred_element_type=jnp.float32).astype(jnp.bfloat16)
    return lax.psum_scatter(picked, ROW, scatter_dimension=0, tiled=True).astype(jnp.float32)


def code_backward(upstream, token_ids, usable, vocab):
    rows = lax.all_gather(upstream.astype(jnp.bfloat16), ROW, axis=0, tiled=True)
    return product(code_hits(token_ids, usable, vocab), rows, FIRST)


def merge_stats(first, second):
    highest = jnp.maximum(first[0], second[0])
    mass = first[1] * jnp.exp(first[0] - highest) + second[1] * jnp.exp(second[0] - highest)
    return (highest, mass, first[2] + second[2], first[3] + second[3])


def joined(stats):
    if lax.axis_size("t") == 2:
        other = lax.ppermute(jnp.stack(stats), "t", [(0, 1), (1, 0)])
        return merge_stats(stats, tuple(other))
    every = lax.all_gather(jnp.stack(stats), "t")
    state = tuple(every[0])
    for place in range(1, every.shape[0]):
        state = merge_stats(state, tuple(every[place]))
    return state


def matrices_of(gathered, n):
    count, rows, columns = gathered.shape
    if rows <= D:
        return gathered
    parts = gathered.reshape(count, n, 4, rows // n // 4, columns)
    return jnp.transpose(parts, (0, 1, 3, 2, 4)).reshape(count, rows // 4, 4 * columns)


def blocks_of(matrix, columns, n):
    if columns % 128 == 0:
        return matrix
    rows = matrix.shape[0]
    parts = matrix.reshape(n, rows // n, 4, columns)
    return jnp.transpose(parts, (0, 2, 1, 3)).reshape(4 * rows, columns)


def update(master, moment, average, gradient, factor, rate):
    clipped = gradient * factor
    moment_new = MOMENT * moment + clipped
    master_new = master - rate * (clipped + MOMENT * moment_new)
    average_new = DECAY * average + (1.0 - DECAY) * master_new
    return (master_new, moment_new, average_new, master_new.astype(jnp.bfloat16))


def per_device(
    code_ids,
    code_mask,
    caption_ids,
    caption_segments,
    image_row,
    attention_master,
    attention_momentum,
    attention_average,
    dense_master,
    dense_momentum,
    dense_average,
    text_master,
    text_momentum,
    text_average,
    code_master,
    code_momentum,
    code_average,
    gain_master,
    gain_momentum,
    gain_average,
):
    n = lax.axis_size("dp")
    z, image, part = lax.axis_index("dp"), lax.axis_index("img"), lax.axis_index("t")
    attention_shape = attention_master.shape[1:]
    dense_shape = dense_master.shape[1:]
    code_shape = code_master.shape[1:]
    images, length = code_ids.shape
    caption_rows, caption_length = caption_ids.shape
    text_rows, text_width = text_master.shape
    text_count = caption_ids.size
    mask = code_mask.astype(jnp.float32)
    gain_width = gain_master.shape[1]
    note = jnp.zeros((16, 128), jnp.float32)
    note = note.at[:7, :gain_width].set(gain_master)
    note = note.at[7, 0].set(jnp.sum(mask))
    note = note.at[8 : 8 + text_count // 128].set(
        caption_ids.astype(jnp.float32).reshape(-1, 128)
    )
    notes = share(note)
    gain_set = (
        jnp.transpose(notes[:, :, :7, :gain_width], (2, 0, 1, 3))
        .reshape(7, D)
    )
    gain_set = lax.reduce_precision(gain_set, exponent_bits=8, mantissa_bits=7)
    count = jnp.sum(notes[:, 0, 7, 0])
    all_text = notes[:, 0, 8 : 8 + text_count // 128].reshape(-1).astype(jnp.int32)
    encoder_attention, encoder_dense, code_table = (
        lax.all_gather(attention_master[0].astype(jnp.bfloat16), "dp", axis=1, tiled=True),
        lax.all_gather(dense_master[0].astype(jnp.bfloat16), "dp", axis=1, tiled=True),
        lax.all_gather(code_master[0].astype(jnp.bfloat16), "dp", axis=1, tiled=True),
    )
    self_weights, cross_weights, dense_weights = gather(
        [
            attention_master[1].astype(jnp.bfloat16),
            attention_master[2].astype(jnp.bfloat16),
            dense_master[1].astype(jnp.bfloat16),
        ],
        n,
        2.0,
        0,
    )
    self_weights, cross_weights, dense_weights = (
        matrices_of(weights, n) for weights in (self_weights, cross_weights, dense_weights)
    )
    out_part, self_weights = lax.optimization_barrier(
        (code_master[1].astype(jnp.bfloat16), self_weights)
    )
    out_table = lax.all_gather(
        lax.all_gather(out_part, "dp", axis=1, tiled=True), "img", axis=0, tiled=True
    )
    segments = caption_segments.reshape(-1)
    encoder_context = {"allowed": (segments[:, None] == segments[None, :])[None]}
    row = jnp.sum(jnp.where(jnp.arange(images) == image, image_row, 0)) - z * caption_rows
    owners = lax.dynamic_index_in_dim(caption_segments, row, 0, False)
    cross_context = {"allowed": (owners == z * images + image)[None, None, :]}
    text_local = all_text - lax.axis_index(ROW) * text_rows
    text_inside = (text_local >= 0) & (text_local < text_rows)
    picked = jnp.take(text_master, jnp.clip(text_local, 0, text_rows - 1), axis=0)
    picked = jnp.where(text_inside[:, None], picked, 0.0).astype(jnp.bfloat16)
    encoder_in = text_in(picked.reshape(n, text_count, text_width))
    branch, encoder_attention_keep = attention_forward(
        encoder_in, gain_set[0], encoder_attention, "encoder", ROW, encoder_context
    )
    encoder_mid = encoder_in + branch
    branch, encoder_dense_keep = dense_forward(encoder_mid, gain_set[1], encoder_dense, ROW)
    encoder_top = encoder_mid + branch
    encoded = spread(rms_norm(encoder_top, gain_set[2]).astype(jnp.bfloat16), ROW)
    caption = lax.dynamic_slice_in_dim(encoded, row * caption_length, caption_length, 0)
    previous = jnp.concatenate(
        [jnp.zeros((images, 1), jnp.int32), code_ids[:, :-1]], axis=1
    ).reshape(-1)
    starting = jnp.broadcast_to(jnp.arange(length) > 0, (images, length)).reshape(-1)
    code_table, encoder_in = lax.optimization_barrier((code_table, encoder_in))
    decoder_in = code_forward(previous, starting, code_table)
    branch, self_keep = attention_forward(
        decoder_in, gain_set[3], self_weights, "self", "t", None
    )
    decoder_one = decoder_in + branch
    branch, cross_keep = attention_forward(
        decoder_one, gain_set[4], cross_weights, "cross", "t", cross_context, caption
    )
    decoder_two = decoder_one + branch
    branch, decoder_dense_keep = dense_forward(decoder_two, gain_set[5], dense_weights, "t")
    decoder_top = decoder_two + branch
    final = spread(rms_norm(decoder_top, gain_set[6]).astype(jnp.bfloat16), "t")
    logits = product(final, out_table, LAST)
    rows = code_shape[0]
    codes = lax.dynamic_index_in_dim(code_ids, image, 0, False)
    held = codes // rows
    local_target = jnp.where(
        held % lax.axis_size("t") == part, held // lax.axis_size("t") * rows + codes % rows, -1
    )
    hits = jnp.arange(logits.shape[1], dtype=jnp.int32)[None, :] == local_target[:, None]
    highest = jnp.max(logits, axis=-1)
    highest, mass, target_logit, logit_total = joined(
        (
            highest,
            jnp.sum(jnp.exp(logits - highest[:, None]), axis=-1),
            jnp.sum(jnp.where(hits, logits, 0.0), axis=-1),
            jnp.sum(logits, axis=-1),
        )
    )
    partition = highest + jnp.log(mass)
    valid = lax.dynamic_index_in_dim(mask, image, 0, False)
    per_token = (
        partition
        - (1.0 - SMOOTH) * target_logit
        - SMOOTH * logit_total / VC
        + Z_WEIGHT * partition * partition
    )
    per_image = lax.all_gather(per_token, "img")
    loss_part = jnp.sum(per_token * valid) / lax.axis_size("t")
    weighting = valid / count
    grad_logits = weighting[:, None] * (
        (1.0 + 2.0 * Z_WEIGHT * partition)[:, None] * jnp.exp(logits - partition[:, None])
        - (1.0 - SMOOTH) * hits.astype(jnp.float32)
        - SMOOTH / VC
    )
    grad_logits = grad_logits.astype(jnp.bfloat16)
    grad_out_table = product(grad_logits, final, FIRST).astype(jnp.bfloat16)
    out_grads = lax.psum_scatter(
        lax.psum_scatter(grad_out_table, "img", scatter_dimension=0, tiled=True),
        "dp",
        scatter_dimension=1,
        tiled=True,
    ).astype(jnp.float32)
    grad_final = collect(
        jnp.dot(grad_logits, out_table, preferred_element_type=jnp.float32), "t"
    )
    grad_top, gain_six = norm_back(decoder_top, gain_set[6], grad_final)
    grad_branch, gain_five, dense_one = dense_backward(
        grad_top, decoder_two, gain_set[5], "t", decoder_dense_keep
    )
    grad_two = grad_top + grad_branch
    grad_branch, gain_four, attention_two, grad_caption = attention_backward(
        grad_two, decoder_one, gain_set[4], cross_weights, "cross", "t", cross_context, cross_keep
    )
    grad_one = grad_two + grad_branch
    grad_branch, gain_three, attention_one, _ = attention_backward(
        grad_one, decoder_in, gain_set[3], self_weights, "self", "t", None, self_keep
    )
    grad_start = grad_one + grad_branch
    narrow = attention_shape[2]
    one_grads, two_grads, dense_one_grads = scatter(
        [
            [blocks_of(matrix, narrow, n) for matrix in attention_one],
            [blocks_of(matrix, narrow, n) for matrix in attention_two],
            dense_one,
        ],
        [attention_shape[1:], attention_shape[1:], dense_shape[1:]],
        n,
        2.0,
        2,
    )
    grad_code_in = code_backward(grad_start, previous, starting, code_shape[0])
    grad_encoded = collect(
        lax.dynamic_update_slice_in_dim(
            jnp.zeros(encoded.shape, jnp.float32), grad_caption, row * caption_length, 0
        ),
        ROW,
    )
    grad_encoder_top, gain_two = norm_back(encoder_top, gain_set[2], grad_encoded)
    grad_branch, gain_one, dense_zero = dense_backward(
        grad_encoder_top, encoder_mid, gain_set[1], ROW, encoder_dense_keep
    )
    grad_encoder_mid = grad_encoder_top + grad_branch
    grad_branch, gain_zero, attention_zero, _ = attention_backward(
        grad_encoder_mid,
        encoder_in,
        gain_set[0],
        encoder_attention,
        "encoder",
        ROW,
        encoder_context,
        encoder_attention_keep,
    )
    text_rows_back = text_back((grad_encoder_mid + grad_branch).astype(jnp.bfloat16))
    text_hits = jnp.arange(text_rows, dtype=jnp.int32)[:, None] == text_local[None, :]
    text_grads = jnp.dot(
        text_hits.astype(jnp.bfloat16),
        text_rows_back.reshape(-1, text_width),
        preferred_element_type=jnp.float32,
    )

    def owned(values, axis):
        return lax.psum_scatter(
            values.astype(jnp.bfloat16), "dp", scatter_dimension=axis, tiled=True
        ).astype(jnp.float32)

    attention_grads = jnp.stack(
        [
            owned(jnp.stack(attention_zero), 1),
            one_grads.reshape(attention_shape),
            two_grads.reshape(attention_shape),
        ]
    )
    dense_grads = jnp.stack([owned(jnp.stack(dense_zero), 1), dense_one_grads.reshape(dense_shape)])
    code_grads = jnp.stack([owned(grad_code_in, 1), out_grads.reshape(code_shape)])
    squares = (
        jnp.sum(attention_grads * attention_grads)
        + jnp.sum(dense_grads * dense_grads)
        + jnp.sum(text_grads * text_grads)
        + jnp.sum(code_grads * code_grads)
    )
    sums = jnp.stack([gain_zero, gain_one, gain_two, gain_three, gain_four, gain_five, gain_six])
    tail = jnp.zeros((1, D), jnp.float32).at[0, 0].set(squares).at[0, 1].set(loss_part)
    sums = total_of(jnp.concatenate([sums, tail], axis=0))
    gain_sums = sums[:7]
    loss = sums[7, 1] / count
    norm = jnp.sqrt(sums[7, 0] + jnp.sum(gain_sums * gain_sums))
    gain_grads = lax.dynamic_slice_in_dim(
        gain_sums, lax.axis_index(("dp",) + ROW) * gain_width, gain_width, 1
    )
    factor = jnp.minimum(1.0, CLIP / norm)
    rate = 0.012 * math.sqrt(12 * D * D + 4 * D * FF + VT * D + 2 * VC * D + 7 * D) / CLIP
    attention_out = update(
        attention_master, attention_momentum, attention_average, attention_grads, factor, rate
    )
    dense_out = update(dense_master, dense_momentum, dense_average, dense_grads, factor, rate)
    text_out = update(text_master, text_momentum, text_average, text_grads, factor, rate)
    code_out = update(code_master, code_momentum, code_average, code_grads, factor, rate)
    gain_out = update(gain_master, gain_momentum, gain_average, gain_grads, factor, rate)
    return (
        loss,
        norm,
        attention_out[0],
        attention_out[1],
        attention_out[2],
        attention_out[3],
        dense_out[0],
        dense_out[1],
        dense_out[2],
        dense_out[3],
        text_out[0],
        text_out[1],
        text_out[2],
        text_out[3],
        code_out[0],
        code_out[1],
        code_out[2],
        code_out[3],
        gain_out[0],
        gain_out[1],
        gain_out[2],
        gain_out[3],
        per_image,
    )


def solution(mesh):
    n, m = mesh.shape["dp"], mesh.shape["mp"]
    view = Mesh(mesh.devices.reshape(n, 4, m // 4), ("dp",) + ROW)
    return jax.shard_map(
        per_device,
        mesh=view,
        in_specs=(
            P("dp", None),
            P("dp", None),
            P("dp", None),
            P("dp", None),
            P("dp"),
            P(None, None, "dp", ROW),
            P(None, None, "dp", ROW),
            P(None, None, "dp", ROW),
            P(None, None, "dp", ROW),
            P(None, None, "dp", ROW),
            P(None, None, "dp", ROW),
            P(ROW, "dp"),
            P(ROW, "dp"),
            P(ROW, "dp"),
            P(None, ROW, "dp"),
            P(None, ROW, "dp"),
            P(None, ROW, "dp"),
            P(None, ("dp",) + ROW),
            P(None, ("dp",) + ROW),
            P(None, ("dp",) + ROW),
        ),
        out_specs=(
            P(),
            P(),
            P(None, None, "dp", ROW),
            P(None, None, "dp", ROW),
            P(None, None, "dp", ROW),
            P(None, None, "dp", ROW),
            P(None, None, "dp", ROW),
            P(None, None, "dp", ROW),
            P(None, None, "dp", ROW),
            P(None, None, "dp", ROW),
            P(ROW, "dp"),
            P(ROW, "dp"),
            P(ROW, "dp"),
            P(ROW, "dp"),
            P(None, ROW, "dp"),
            P(None, ROW, "dp"),
            P(None, ROW, "dp"),
            P(None, ROW, "dp"),
            P(None, ("dp",) + ROW),
            P(None, ("dp",) + ROW),
            P(None, ("dp",) + ROW),
            P(None, ("dp",) + ROW),
            P("dp", None),
        ),
        check_vma=False,
    )
```

time: 2400 us -> 1180 us (0.49)
  waiting for transfers between devices: 1510 us -> 60.9 us
  Pallas kernels: 0 us -> 555 us
  blocking collectives: 187 us -> 8.12 us
  local copies, waits for them, and re-layouts: 109 us -> 42.4 us
  matrix products: 355 us -> 300 us
  other arithmetic: 202 us -> 168 us
    reduce_scatter x18 -> x6, waiting for transfers between devices: 825 us -> 0.1 us  [the longest x3 0.04 us: owned(): lax.psum_scatter(values.astype(jnp.bfloat16), 'dp', scatter_dimension=axi...]
    pallas_call x0 -> x16, Pallas kernels: none -> 555 us  [the longest x14 213 us: small_call(): pl.pallas_call(kernel, out_shape=out_shape, in_specs=[vmem] * len(operand...]
    all_gather x12 -> x6, waiting for transfers between devices: 555 us -> 38.1 us  [the longest x1 35.5 us: per_device(): lax.all_gather(lax.all_gather(out_part, 'dp', axis=1, tiled=True), 'img',...]
    unnamed x32 -> x12, waiting for transfers between devices: 133 us -> 0.2 us
    all_gather x11 -> x1, blocking collectives: 133 us -> 8.12 us  [per_device(): per_image = lax.all_gather(per_token, 'img')]
    psum x2 -> x0, blocking collectives: 53.5 us -> none  [the longest x1 40.8 us: per_device(): norm = jnp.sqrt(lax.psum(squares, ('dp', 'mp')))]
    scatter-add x4 -> x0, other arithmetic: 46.4 us -> none  [the longest x2 44.9 us: embed_backward(): return jnp.zeros((vocab, gathered.shape[1]), jnp.float32).at[local].add(g...]
    dot_general x34 -> x35, matrix products: 157 us -> 122 us  [product(): lax.dot_general(left, right, dims, preferred_element_type=jnp.float32)]
  transfers between devices with their start and end apart: 31 -> 27, of which waited for: 28 -> 13; matrix products, arithmetic and copies ran while one was open for 19% -> 32% of each run, Pallas kernels for 0% -> 46%
where the time goes in v1:
time: 1180 us; the launch traced here: 1170 us
  Pallas kernels  555 us (47%)
  matrix products  300 us (25%)
  other arithmetic  168 us (14%)
  waiting for transfers between devices  60.9 us (5%)
  local copies, waits for them, and re-layouts  42.4 us (4%)
  between operations  27.4 us (2%)
    pallas_call x14, Pallas kernels, small_call(): pl.pallas_call(kernel, out_shape=out_shape, in_specs=[vmem] * len(operand...  213 us
    pallas_call x1, Pallas kernels, scatter(): pl.pallas_call(partial(scatter_kernel, n, slabs, members), out_shape=[jax...  172 us
    pallas_call x1, Pallas kernels, gather(): pl.pallas_call(partial(gather_kernel, n, slabs, count), out_shape=[jax.Sh...  170 us
    dot_general x35, matrix products, product(): lax.dot_general(left, right, dims, preferred_element_type=jnp.float32)  122 us
    all_gather x1, waiting for transfers between devices, per_device(): lax.all_gather(lax.all_gather(out_part, 'dp', axis=1, tiled=True), 'img',...  35.5 us
    dot_general x4, matrix products, core_backward(): jnp.einsum('bqhe,bkhe->bhqk', upstream, value, preferred_element_type=jnp...  31.1 us
    dot_general x2, matrix products, dense_forward(): hidden = jnp.dot(inputs, weights[0], preferred_element_type=jnp.float32)  30 us
    convert_element_type x4, other arithmetic, core_backward(): grad_scores = (shares * (grad_shares - inner)).astype(jnp.bfloat16)  28.1 us
  transfers between devices with their start and end apart: 27, of which 13 were waited for; matrix products, arithmetic and copies ran while one was open for 32% of the time, Pallas kernels for 46%

profile of v1, /device:TPU:0, one launch (start us, length us, event | category | flops | bytes accessed | tf_op | source)
XLA Modules:
  0.0 1169.8 jit_solution(13762835323075954082)
XLA Ops:
  14.6 22.6 %share.1 = f32[4,8,16,128]{3,2,1,0:T(8,128)} custom-call(f32[16,128]{1,0:T(8,128)} %copy-done.162), custom_call_target="tpu_custom_call" | custom-call | bytes 16777216 | tf_op jit(solution)/shard_map/share/pallas_call | solution.py:498
  43.2 29.5 %text_in.1 = f32[32,1024]{1,0:T(8,128)} custom-call(bf16[4,256,256]{2,1,0:T(8,128)(2,1)} %select_convert_fusion.picked), custom_call_target="tpu_custom_call" | custom-call | bytes 16777216 | tf_op jit(solution)/shard_map/text_in/pallas_call | solution.py:498
  75.4 13.7 %fusion.28 = bf16[4096,1024]{1,0:T(8,128)(2,1)} fusion(bf16[1024,1024]{1,0:T(8,128)(2,1)} %bitcast.452, s32[4096]{0:T(1024)S(1)} %bitcast.437, pred[4096]{0:T(1024)(128)(4,1)S(1)} %bitcast.447), kind=kOutput, calls=%fused_computation.54 | convolution fusion | flops 8602517504 | bytes 10506240 | tf_op jit(solution)/shard_map/dot_general | solution.py:906
  92.0 170.3 %gather.11 = (bf16[4,1024,512]{2,1,0:T(8,128)(2,1)}, bf16[4,1024,512]{2,1,0:T(8,128)(2,1)}, bf16[2,1024,2048]{2,1,0:T(8,128)(2,1)}) custom-call(bf16[4,256,128]{2,1,0:T(8,128)(2,1)} %get-tuple-element.189.refs_0_, bf16[4,256,128]{2,1,0:T(8,128)(2,1)} %get-tuple-element.188.refs_1_, bf16[2,256,512]{2,1,0:T(8,128)(2,1)} %get-tuple-element.184.refs_2_), custom_call_target="tpu_custom_call" | custom-call | bytes 268435456 | tf_op jit(solution)/shard_map/gather/pallas_call | solution.py:228
  265.9 10.0 row_spread.5
  289.6 10.4 row_collect.5
  310.6 16.6 %fusion.5 = f32[8,512]{1,0:T(8,128)S(1)} fusion(f32[8,512,1024]{2,1,0:T(8,128)S(1)} %get-tuple-element.211, f32[8,512]{1,0:T(8,128)S(1)} %get-tuple-element.210), kind=kLoop, calls=%fused_computation.21 | loop fusion | flops 8384512 | bytes 16809984 | tf_op jit(solution)/shard_map/reduce_sum | solution.py:742
  351.3 10.1 row_spread.6
  367.4 11.2 row_collect.6
  384.5 10.0 row_spread.7
  418.2 26.2 %multiply_convert_fusion.3 = (bf16[1024,2048]{1,0:T(8,128)(2,1)S(1)}, f32[1024,2048]{1,0:T(8,128)}, f32[1024,2048]{1,0:T(8,128)}) fusion(bf16[2,1024,2048]{2,1,0:T(8,128)(2,1)S(1)} %bitcast.451, bf16[512,1024]{1,0:T(8,128)(2,1)S(1)} %get-tuple-element.175, bf16[512,1024]{1,0:T(8,128)(2,1)S(1)} %get-tuple-element.174), kind=kOutput, calls=%fused_computation.32 | convolution fusion | flops 4435476480 | bytes 27262976 | tf_op jit(solution)/shard_map/dot_general | solution.py:877
  464.4 35.5 %all-gather.13.cloned.1.call-done = bf16[4096,1024]{1,0:T(8,128)(2,1)} async-done(((bf16[1024,1024]{1,0:T(8,128)(2,1)}), bf16[4096,1024]{1,0:T(8,128)(2,1)}) %all-gather.13.cloned.1.call-update) | async-done | bytes 8388624 | tf_op jit(solution)/shard_map/all_gather | solution.py:1024
  499.9 15.1 %fusion.226 = (f32[1024]{0:T(1024)S(1)}, f32[1024,4096]{1,0:T(8,128)}) fusion(bf16[4096,1024]{1,0:T(8,128)(2,1)} %all-gather.13.cloned.1.call-done, bf16[512,1024]{1,0:T(8,128)(2,1)} %get-tuple-element.173, bf16[512,1024]{1,0:T(8,128)(2,1)S(1)} %get-tuple-element.172), kind=kOutput, calls=%fused_computation.486 | convolution fusion | flops 8598322176 | bytes 27267072 | tf_op jit(solution)/shard_map/dot_general | solution.py:730
  515.0 9.8 exponential_reduce_fusion
  528.0 8.4 multiply_convert_fusion.2
  536.4 11.3 fusion.228
  556.3 12.8 %add_convert_fusion = bf16[1024,2048]{1,0:T(8,128)(2,1)} fusion(f32[1024,2048]{1,0:T(8,128)} %get-tuple-element.153, f32[1024,2048]{1,0:T(8,128)} %get-tuple-element.214, bf16[2,1024,2048]{2,1,0:T(8,128)(2,1)} %get-tuple-element.98, bf16[512,1024]{1,0:T(8,128)(2,1)} %get-tuple-element.171, bf16[512,1024]{1,0:T(8,128)(2,1)S(1)} %get-tuple-element.170), kind=kOutput, calls=%fused_computation.31 | convolution fusion | flops 4328521728 | bytes 27262976 | tf_op jit(solution)/shard_map/dot_general | solution.py:886
  596.2 11.4 convolution_convert_fusion
  622.0 16.3 %multiply_reduce_fusion.1 = (f32[8,512]{1,0:T(8,128)S(1)}, f32[8,512,1024]{2,1,0:T(8,128)}) fusion(f32[8,512,1024]{2,1,0:T(8,128)} %copy-done, f32[8,512]{1,0:T(8,128)S(1)} %log_add_fusion.2, bf16[512,8,64]{0,2,1:T(8,128)(2,1)S(1)} %bitcast.360, bf16[1024,8,64]{0,2,1:T(8,128)(2,1)S(1)} %bitcast.369), kind=kOutput, calls=%fused_computation.5 | convolution fusion | flops 549449728 | bytes 35160064 | tf_op jit(solution)/shard_map/bqhe,bkhe->bhqk/dot_general | solution.py:755
  639.5 10.9 multiply_convert_fusion.1
  656.7 12.6 %multiply_reduce_fusion = (f32[8,512]{1,0:T(8,128)}, f32[8,512,1024]{2,1,0:T(8,128)}) fusion(f32[8,512,1024]{2,1,0:T(8,128)} %copy-done.1, f32[8,512]{1,0:T(8,128)} %log_add_fusion.1, bf16[512,8,64]{0,2,1:T(8,128)(2,1)S(1)} %bitcast.362, bf16[1024,8,64]{0,2,1:T(8,128)(2,1)} %bitcast.368), kind=kOutput, calls=%fused_computation.2 | convolution fusion | flops 549449728 | bytes 35160064 | tf_op jit(solution)/shard_map/bqhe,bkhe->bhqk/dot_general | solution.py:755
  669.3 15.9 %multiply_convert_fusion = bf16[8,512,1024]{2,1,0:T(8,128)(2,1)} fusion(f32[8,512,1024]{2,1,0:T(8,128)} %get-tuple-element.222, f32[8,512,1024]{2,1,0:T(8,128)} %copy-done.1, f32[8,512]{1,0:T(8,128)} %get-tuple-element.221, f32[8,512]{1,0:T(8,128)} %log_add_fusion.1), kind=kLoop, calls=%fused_computation.1 | loop fusion | flops 16777216 | bytes 41975808 | tf_op jit(solution)/shard_map/convert_element_type | solution.py:757
  735.7 16.1 %row_collect.7 = f32[32,1024]{1,0:T(8,128)} custom-call(f32[256,1024]{1,0:T(8,128)} %copy-done.47), custom_call_target="tpu_custom_call" | custom-call | bytes 16777216 | tf_op jit(solution)/shard_map/row_collect/pallas_call | solution.py:498
  754.6 15.5 %row_spread.8 = bf16[256,1024]{1,0:T(8,128)(2,1)} custom-call(bf16[32,1024]{1,0:T(8,128)(2,1)} %fusion.155.mine), custom_call_target="tpu_custom_call" | custom-call | bytes 16777216 | tf_op jit(solution)/shard_map/row_spread/pallas_call | solution.py:498
  774.1 17.1 %row_collect.8 = f32[32,1024]{1,0:T(8,128)} custom-call(f32[256,1024]{1,0:T(8,128)} %fusion.115.values), custom_call_target="tpu_custom_call" | custom-call | bytes 16777216 | tf_op jit(solution)/shard_map/row_collect/pallas_call | solution.py:498
  794.1 11.0 row_spread.9
  830.0 8.5 convolution_convert_fusion.1.refs_9_
  846.4 14.5 %fusion.67 = bf16[1024,1024]{1,0:T(8,128)(2,1)} fusion(bf16[4096,1024]{1,0:T(8,128)(2,1)} %all-gather.15.cloned.1.call-done, s32[4096]{0:T(1024)S(1)} %bitcast.438, pred[4096]{0:T(1024)(128)(4,1)S(1)} %bitcast.448), kind=kOutput, calls=%fused_computation.157 | convolution fusion | flops 8599371776 | bytes 10506240 | tf_op jit(solution)/shard_map/dot_general | solution.py:730
  864.5 10.7 row_collect.9
  878.1 25.4 %text_back.1 = bf16[4,256,256]{2,1,0:T(8,128)(2,1)} custom-call(bf16[32,1024]{1,0:T(8,128)(2,1)} %fusion.154.mine), custom_call_target="tpu_custom_call" | custom-call | bytes 16777216 | tf_op jit(solution)/shard_map/text_back/pallas_call | solution.py:498
  927.1 171.9 %scatter.33 = (f32[1024,128]{1,0:T(8,128)}, f32[1024,128]{1,0:T(8,128)}, f32[512,512]{1,0:T(8,128)}) custom-call(bf16[1024,512]{1,0:T(8,128)(2,1)} %convolution_convert_fusion.12.refs_0_, bf16[1024,512]{1,0:T(8,128)(2,1)} %convolution_convert_fusion.11.refs_1_, bf16[1024,512]{1,0:T(8,128)(2,1)} %convolution_convert_fusion.10.refs_2_, ...), custom_call_target="tpu_custom_call" | custom-call | bytes 268435456 | tf_op jit(solution)/shard_map/scatter/pallas_call | solution.py:409
  1116.5 12.9 %total.1 = f32[8,1024]{1,0:T(8,128)} custom-call(f32[8,1024]{1,0:T(8,128)} %concatenate.68.mine), custom_call_target="tpu_custom_call" | custom-call | bytes 16777216 | tf_op jit(solution)/shard_map/total/pallas_call | solution.py:498
  (716 shorter events, 348.0 us)
Async XLA Ops:
  7.2 68.2 %all-gather.17.cloned.1.call-start = ((), (), s32[]{:S(2)}) async-start(), calls=%async_computation.15 | async-start | bytes 2621440 | tf_op jit(solution)/shard_map/all_gather | solution.py:1006
  10.0 267.7 %all-gather.19.cloned.1.call-start = ((), (), s32[]{:S(2)}) async-start(), calls=%async_computation.16 | async-start | bytes 1310720 | tf_op jit(solution)/shard_map/all_gather | solution.py:1004
  12.6 268.6 %reduce-scatter.7.cloned.1.call-start = ((), (), s32[]{:S(2)}) async-start(), calls=%async_computation.6 | async-start | bytes 9437184 | tf_op jit(solution)/shard_map/reduce_scatter | solution.py:907
  89.1 173.6 %copy-start.110 = (f32[4,8,16,128]{3,2,1,0:T(8,128)S(1)}, f32[4,8,16,128]{3,2,1,0:T(8,128)}, u32[]{:S(2)}) copy-start(f32[4,8,16,128]{3,2,1,0:T(8,128)} %share.1) | copy-start | bytes 786436
  89.2 173.6 %copy-start.34 = (f32[32,1024]{1,0:T(8,128)S(1)}, f32[32,1024]{1,0:T(8,128)}, u32[]{:S(2)}) copy-start(f32[32,1024]{1,0:T(8,128)} %text_in.1) | copy-start | bytes 393220
  89.2 173.7 %copy-start.199 = (s32[4]{0:T(128)S(1)}, s32[4]{0:T(128)}, u32[]{:S(2)}) copy-start(s32[4]{0:T(128)} %param.34) | copy-start | bytes 52
  89.2 186.7 %copy-start.187 = (s32[2,128]{1,0:T(2,128)S(1)}, s32[2,128]{1,0:T(2,128)}, u32[]{:S(2)}) copy-start(s32[2,128]{1,0:T(2,128)} %param.33) | copy-start | bytes 3076
  89.2 272.2 %all-gather.21.cloned.1.call-start = ((), (), s32[]{:S(2)}) async-start(), calls=%async_computation.17 | async-start | bytes 2621440 | tf_op jit(solution)/shard_map/all_gather | solution.py:1005
  91.9 317.7 %all-gather.11.cloned.1.call-start = ((), (), s32[]{:S(2)}) async-start(), calls=%async_computation.7 | async-start | bytes 2621440 | tf_op jit(solution)/shard_map/all_gather | solution.py:1025
  262.3 237.6 %all-gather.13.cloned.1.call-start = ((), (), s32[]{:S(2)}) async-start(), calls=%async_computation.8 | async-start | bytes 10485760 | tf_op jit(solution)/shard_map/all_gather | solution.py:1024
  265.1 133.0 %copy-start.141 = (f32[1024]{0:T(1024)}, f32[1024]{0:T(1024)S(1)}, u32[]{:S(2)}) copy-start(f32[1024]{0:T(1024)S(1)} %mul.931) | copy-start | bytes 12292
  285.5 15.7 %collective-permute-start = (bf16[512,1024]{1,0:T(8,128)(2,1)}, bf16[512,1024]{1,0:T(8,128)(2,1)}, u32[]{:S(2)}, u32[]{:S(2)}) collective-permute-start(bf16[512,1024]{1,0:T(8,128)(2,1)} %fusion.52), channel_id=1, source_target_pairs={{0,1},{1,0},{2,3},{3,2},{4,5},{5,4},{6,7},{7,6},{8,9},{9,8},{10,11... | collective-permute-start | bytes 3145736 | tf_op jit(solution)/shard_map/ppermute | solution.py:705
  348.9 29.6 %collective-permute-start.1 = (bf16[512,1024]{1,0:T(8,128)(2,1)S(1)}, bf16[512,1024]{1,0:T(8,128)(2,1)}, u32[]{:S(2)}, u32[]{:S(2)}) collective-permute-start(bf16[512,1024]{1,0:T(8,128)(2,1)S(1)} %dynamic-slice_convert_fusion.6), channel_id=1, source_target_pairs={{0,1},{1,0},{2,3},{3,2},{4,5},{5,4},{6,7},{7,6},{8,9},{9,8},{10,11... | collective-permute-start | bytes 3145736 | tf_op jit(solution)/shard_map/ppermute | solution.py:720
  382.5 15.6 %collective-permute-start.2 = (bf16[512,1024]{1,0:T(8,128)(2,1)}, bf16[512,1024]{1,0:T(8,128)(2,1)}, u32[]{:S(2)}, u32[]{:S(2)}) collective-permute-start(bf16[512,1024]{1,0:T(8,128)(2,1)} %multiply_convert_fusion.9), channel_id=1, source_target_pairs={{0,1},{1,0},{2,3},{3,2},{4,5},{5,4},{6,7},{7,6},{8,9},{9,8},{10,11... | collective-permute-start | bytes 3145736 | tf_op jit(solution)/shard_map/ppermute | solution.py:705
  408.4 3.7 collective-permute-start.3
  409.7 410.8 %reduce-scatter.15.cloned.1.call-start = ((), (), s32[]{:S(2)}) async-start(), calls=%async_computation.13 | async-start | bytes 10485760 | tf_op jit(solution)/shard_map/reduce_scatter | solution.py:1098
  414.8 2.7 collective-permute-start.4
  451.0 2.9 collective-permute-start.5
  458.1 2.9 collective-permute-start.6
  524.9 1.2 collective-permute-start.7
  547.9 2.7 collective-permute-start.8
  552.5 2.7 collective-permute-start.9
  577.0 2.7 collective-permute-start.10
  583.3 2.7 collective-permute-start.11
  596.0 11.7 collective-permute-start.12
  607.6 238.7 %all-gather.15.cloned.1.call-start = ((), (), s32[]{:S(2)}) async-start(), calls=%async_computation.11 | async-start | bytes 9437184 | tf_op jit(solution)/shard_map/all_gather | solution.py:911
  615.7 2.7 collective-permute-start.13
  721.1 2.7 collective-permute-start.14
  726.5 372.7 %reduce-scatter.9.cloned.1.call-start = ((), (), s32[]{:S(2)}) async-start(), calls=%async_computation.9 | async-start | bytes 1310720 | tf_op jit(solution)/shard_map/reduce_scatter | solution.py:1162
  813.7 289.5 %reduce-scatter.11.cloned.1.call-start = ((), (), s32[]{:S(2)}) async-start(), calls=%async_computation.10 | async-start | bytes 2621440 | tf_op jit(solution)/shard_map/reduce_scatter | solution.py:1162
  818.4 290.4 %reduce-scatter.17.cloned.1.call-start = ((), (), s32[]{:S(2)}) async-start(), calls=%async_computation.14 | async-start | bytes 2621440 | tf_op jit(solution)/shard_map/reduce_scatter | solution.py:1097
  820.5 288.3 %reduce-scatter.13.cloned.1.call-start = ((), (), s32[]{:S(2)}) async-start(), calls=%async_computation.12 | async-start | bytes 2621440 | tf_op jit(solution)/shard_map/reduce_scatter | solution.py:1162
  (211 other events, 2297.2 us)
Sparse Core Ops, SparseCore 0:
  10.2 65.1 all-gather.16
  77.5 29.0 all-gather.18
  110.1 109.1 reduce-scatter.6
  221.4 47.5 all-gather.20
  271.0 46.1 all-gather.10
  409.8 90.0 all-gather.12
  607.8 86.4 reduce-scatter.14
  726.6 69.5 all-gather.14
  813.8 28.1 reduce-scatter.8
  844.8 42.5 reduce-scatter.10
  889.7 45.2 reduce-scatter.16
  937.8 77.0 reduce-scatter.12

commit v2 on v1

--- a/solution.py
+++ b/solution.py
@@ -461,32 +461,44 @@
     pl.semaphore_wait(barrier, sum(group.size - 1 for group in groups))
 
 
-def exchange(group, source, target, send_sem, recv_sem):
-    def copy_of(step):
-        index = group.other(step)
+class Exchange:
+    def __init__(self, group, source, target, send_sem, recv_sem):
+        self.group, self.source, self.target = group, source, target
+        self.send_sem, self.recv_sem = send_sem, recv_sem
+
+    def copy_of(self, step):
+        index = self.group.other(step)
         return pltpu.make_async_remote_copy(
-            src_ref=source(index),
-            dst_ref=target(group.me),
-            send_sem=send_sem.at[step],
-            recv_sem=recv_sem.at[group.me],
-            device_id=group.device(index),
+            src_ref=self.source(index),
+            dst_ref=self.target(self.group.me),
+            send_sem=self.send_sem.at[step],
+            recv_sem=self.recv_sem.at[self.group.me],
+            device_id=self.group.device(index),
             device_id_type=MESH,
         )
 
-    for step in range(1, group.size):
-        copy_of(step).start()
-    for step in range(1, group.size):
-        index = group.other(step)
-        pltpu.make_async_remote_copy(
-            src_ref=target(index),
-            dst_ref=target(index),
-            send_sem=send_sem.at[step],
-            recv_sem=recv_sem.at[index],
-            device_id=group.device(index),
-            device_id_type=MESH,
-        ).wait_recv()
-    for step in range(1, group.size):
-        copy_of(step).wait_send()
+    def start(self):
+        for step in range(1, self.group.size):
+            self.copy_of(step).start()
+        return self
+
+    def finish(self):
+        for step in range(1, self.group.size):
+            index = self.group.other(step)
+            pltpu.make_async_remote_copy(
+                src_ref=self.target(index),
+                dst_ref=self.target(index),
+                send_sem=self.send_sem.at[step],
+                recv_sem=self.recv_sem.at[index],
+                device_id=self.group.device(index),
+                device_id_type=MESH,
+            ).wait_recv()
+        for step in range(1, self.group.size):
+            self.copy_of(step).wait_send()
+
+
+def exchange(*parts):
+    Exchange(*parts).start().finish()
 
 
 def row_block(ref, rows, index):
@@ -513,65 +525,72 @@
     return [pltpu.SemaphoreType.DMA((size,)), pltpu.SemaphoreType.DMA((size,))]
 
 
-def row_spread_kernel(size, mine, every, send_sem, recv_sem):
-    row = Row(size)
-    rows = mine.shape[0]
-    greet(row)
-    row_block(every, rows, row.me)[...] = mine[...]
-    exchange(row, lambda _: mine, lambda index: row_block(every, rows, index), send_sem, recv_sem)
-
-
-def row_spread(values):
-    size = lax.axis_size("img") * lax.axis_size("t")
-    return small_call(
-        partial(row_spread_kernel, size),
-        jax.ShapeDtypeStruct((size * values.shape[0], values.shape[1]), values.dtype),
-        semaphores(size),
-        [values],
-        3,
-        "row_spread",
-    )
-
-
-def row_sum(row, short, got, result, send_sem, recv_sem):
-    rows = result.shape[0]
-    row_block(got, rows, row.me)[...] = row_block(short, rows, row.me)[...]
-    exchange(
-        row,
-        lambda index: row_block(short, rows, index),
-        lambda index: row_block(got, rows, index),
-        send_sem,
-        recv_sem,
-    )
-    total = got[pl.ds(0, rows)].astype(jnp.float32)
-    for index in range(1, row.size):
-        total = total + got[pl.ds(index * rows, rows)].astype(jnp.float32)
-    result[...] = total
-
-
-def row_collect_kernel(size, values, result, short, got, send_sem, recv_sem):
-    row = Row(size)
-    short[...] = values[...].astype(jnp.bfloat16)
-    greet(row)
-    row_sum(row, short, got, result, send_sem, recv_sem)
-
-
-def row_collect(values):
-    size = lax.axis_size("img") * lax.axis_size("t")
-    short = pltpu.VMEM(values.shape, jnp.bfloat16)
-    return small_call(
-        partial(row_collect_kernel, size),
-        jax.ShapeDtypeStruct((values.shape[0] // size, values.shape[1]), jnp.float32),
-        [short, short] + semaphores(size),
-        [values],
-        4,
-        "row_collect",
-    )
-
-
-def text_in_kernel(n, size, picked, result, short, got, *sems):
+class RowSpread:
+    def __init__(self, row, mine, every, *sems):
+        self.mine, self.every, self.rows, self.me = mine, every, mine.shape[0], row.me
+        self.work = Exchange(row, lambda _: mine, self.block, *sems)
+
+    def block(self, index):
+        return row_block(self.every, self.rows, index)
+
+    def start(self, values):
+        self.mine[...] = values
+        self.block(self.me)[...] = values
+        self.work.start()
+
+    def finish(self):
+        self.work.finish()
+        return self.every[...]
+
+
+class RowSum:
+    def __init__(self, row, short, got, rows, *sems):
+        self.short, self.got, self.rows, self.row = short, got, rows, row
+        self.work = Exchange(
+            row,
+            lambda index: row_block(short, rows, index),
+            lambda index: row_block(got, rows, index),
+            *sems,
+        )
+
+    def start(self, values=None):
+        if values is not None:
+            self.short[...] = values.astype(jnp.bfloat16)
+        mine = row_block(self.short, self.rows, self.row.me)
+        row_block(self.got, self.rows, self.row.me)[...] = mine[...]
+        self.work.start()
+
+    def finish(self):
+        self.work.finish()
+        total = self.got[pl.ds(0, self.rows)].astype(jnp.float32)
+        for index in range(1, self.row.size):
+            total = total + self.got[pl.ds(index * self.rows, self.rows)].astype(jnp.float32)
+        return total
+
+
+def head_lanes(width):
+    lanes = lax.broadcasted_iota(jnp.int32, (1, width), 1) // HEAD_DIM
+    return [lanes == head for head in range(width // HEAD_DIM)]
+
+
+def only(lanes, values):
+    return jnp.where(lanes, values, jnp.zeros_like(values))
+
+
+def full_shares(query, key, allowed, lanes):
+    scores = product(only(lanes, query), key, LAST) * HEAD_DIM ** (-0.5)
+    scores = jnp.where(allowed > 0, scores, NEGATIVE)
+    weight = jnp.exp(scores - jnp.max(scores, axis=-1, keepdims=True))
+    return weight / jnp.sum(weight, axis=-1, keepdims=True)
+
+
+def encoder_kernel(
+    n, size, picked, gains, attention, dense, allowed,
+    encoded, first, middle, top, inputs, query, key, value, mixed, dense_in, hidden, active,
+    short, mine, got_text, got_mixed, got_dense, *sems,
+):
     row, column = Row(size), Column(n)
-    width = picked.shape[2]
+    rows, width = first.shape[0], picked.shape[2]
     greet(row, column)
 
     def columns(index):
@@ -579,50 +598,292 @@
 
     columns(column.me)[...] = picked[column.me]
     exchange(column, lambda index: picked.at[index], columns, *sems[:2])
-    row_sum(row, short, got, result, *sems[2:])
-
-
-def text_in(picked):
-    n, tokens, width = picked.shape
+    text = RowSum(row, short, got_text, rows, *sems[2:4])
+    text.start()
+    values = text.finish()
+    first[...] = values
+    spread_one = RowSpread(row, mine, inputs, *sems[4:6])
+    spread_one.start(rms_norm(values, gains[0:1]).astype(jnp.bfloat16))
+    every = spread_one.finish()
+    query[...] = jnp.dot(
+        every, attention[0], preferred_element_type=jnp.float32
+    ).astype(jnp.bfloat16)
+    key[...] = jnp.dot(every, attention[1], preferred_element_type=jnp.float32).astype(jnp.bfloat16)
+    value[...] = jnp.dot(
+        every, attention[2], preferred_element_type=jnp.float32
+    ).astype(jnp.bfloat16)
+    out = jnp.zeros(query.shape, jnp.float32)
+    for lanes in head_lanes(query.shape[1]):
+        shares = full_shares(query[...], key[...], allowed[...], lanes).astype(jnp.bfloat16)
+        out = out + jnp.dot(shares, only(lanes, value[...]), preferred_element_type=jnp.float32)
+    mixed[...] = out.astype(jnp.bfloat16)
+    branch = RowSum(row, short, got_mixed, rows, *sems[6:8])
+    branch.start(product(mixed[...], attention[3], LAST))
+    values = values + branch.finish()
+    middle[...] = values
+    spread_two = RowSpread(row, mine, dense_in, *sems[8:10])
+    spread_two.start(rms_norm(values, gains[1:2]).astype(jnp.bfloat16))
+    every = spread_two.finish()
+    hidden[...] = jnp.dot(every, dense[0], preferred_element_type=jnp.float32)
+    inner = hidden[...]
+    active[...] = (0.5 * inner * (1.0 + lax.erf(inner * math.sqrt(0.5)))).astype(jnp.bfloat16)
+    branch = RowSum(row, short, got_dense, rows, *sems[10:12])
+    branch.start(product(active[...], dense[1], LAST))
+    values = values + branch.finish()
+    top[...] = values
+    spread_three = RowSpread(row, mine, encoded, *sems[12:14])
+    spread_three.start(rms_norm(values, gains[2:3]).astype(jnp.bfloat16))
+    spread_three.finish()
+
+
+def encoder_call(kernel, out_shape, scratch, operands, collective_id, name):
+    vmem = pl.BlockSpec(memory_space=pltpu.VMEM)
+    return pl.pallas_call(
+        kernel,
+        out_shape=out_shape,
+        in_specs=[vmem] * len(operands),
+        out_specs=[vmem] * len(out_shape),
+        scratch_shapes=scratch,
+        compiler_params=pltpu.CompilerParams(
+            collective_id=collective_id, has_side_effects=True, vmem_limit_bytes=48 * 2**20
+        ),
+        cost_estimate=pl.CostEstimate(flops=0, bytes_accessed=2**27, transcendentals=0),
+        name=name,
+    )(*operands)
+
+
+def encoder_forward(picked, gains, attention, dense, allowed):
+    n, tokens, _ = picked.shape
     size = lax.axis_size("img") * lax.axis_size("t")
-    short = pltpu.VMEM((tokens, n * width), jnp.bfloat16)
-    return small_call(
-        partial(text_in_kernel, n, size),
-        jax.ShapeDtypeStruct((tokens // size, n * width), jnp.float32),
-        [short, short] + semaphores(n) + semaphores(size),
-        [picked],
-        5,
-        "text_in",
-    )
-
-
-def text_back_kernel(n, size, mine, result, every, *sems):
+    width, inner = attention.shape[2], dense.shape[2]
+    own = jax.ShapeDtypeStruct((tokens // size, D), jnp.float32)
+    every = jax.ShapeDtypeStruct((tokens, D), jnp.bfloat16)
+    head = jax.ShapeDtypeStruct((tokens, width), jnp.bfloat16)
+    wide_out = [jax.ShapeDtypeStruct((tokens, inner), kind) for kind in (jnp.float32, jnp.bfloat16)]
+    whole = pltpu.VMEM((tokens, D), jnp.bfloat16)
+    outs = encoder_call(
+        partial(encoder_kernel, n, size),
+        [every, own, own, own, every, head, head, head, head, every] + wide_out,
+        [whole, pltpu.VMEM((tokens // size, D), jnp.bfloat16), whole, whole, whole]
+        + semaphores(n)
+        + semaphores(size) * 6,
+        [picked, gains, attention, dense, allowed],
+        3,
+        "encoder",
+    )
+    return outs[0], outs[1:]
+
+
+def norm_back_sums(values, gain, upstream):
+    scale = lax.rsqrt(jnp.mean(values * values, axis=-1, keepdims=True) + EPS)
+    unit = values * scale
+    inner = upstream * gain
+    grad = scale * (inner - unit * jnp.mean(inner * unit, axis=-1, keepdims=True))
+    return grad, jnp.sum(upstream * unit, axis=0, keepdims=True)
+
+
+def encoder_back_kernel(
+    n, size, grad_encoded, gains, attention, dense, allowed,
+    first, middle, top, inputs, query, key, value, mixed, dense_in, hidden, active,
+    text_rows, gain_grads, attention_grads, dense_grads,
+    short, mine, got_encoded, got_dense, got_mixed, every_dense, every_mixed, every_text, *sems,
+):
     row, column = Row(size), Column(n)
-    rows, width = mine.shape[0], result.shape[2]
+    rows, width = first.shape[0], text_rows.shape[2]
+    short[...] = grad_encoded[...].astype(jnp.bfloat16)
     greet(row, column)
-    row_block(every, rows, row.me)[...] = mine[...]
-    exchange(row, lambda _: mine, lambda index: row_block(every, rows, index), *sems[:2])
+    gain_grads[...] = jnp.zeros(gain_grads.shape, jnp.float32)
+    work = RowSum(row, short, got_encoded, rows, *sems[:2])
+    work.start()
+    grad, gain = norm_back_sums(top[...], gains[2:3], work.finish())
+    gain_grads[2:3] = gain
+    work = RowSpread(row, mine, every_dense, *sems[2:4])
+    work.start(grad.astype(jnp.bfloat16))
+    upstream = work.finish()
+    inner = hidden[...]
+    share = 0.5 * (1.0 + lax.erf(inner * math.sqrt(0.5)))
+    slope = share + inner * jnp.exp(-0.5 * inner * inner) * (1.0 / math.sqrt(2.0 * math.pi))
+    grad_hidden = (
+        slope * jnp.dot(upstream, dense[1], preferred_element_type=jnp.float32)
+    ).astype(jnp.bfloat16)
+    work = RowSum(row, short, got_dense, rows, *sems[4:6])
+    work.start(product(grad_hidden, dense[0], LAST))
+    dense_grads[0] = product(dense_in[...], grad_hidden, FIRST).astype(jnp.bfloat16)
+    dense_grads[1] = product(upstream, active[...], FIRST).astype(jnp.bfloat16)
+    part, gain = norm_back_sums(middle[...], gains[1:2], work.finish())
+    gain_grads[1:2] = gain
+    grad = grad + part
+    work = RowSpread(row, mine, every_mixed, *sems[6:8])
+    work.start(grad.astype(jnp.bfloat16))
+    upstream = work.finish()
+    grad_mixed = jnp.dot(upstream, attention[3], preferred_element_type=jnp.float32).astype(
+        jnp.bfloat16
+    )
+    scale = HEAD_DIM ** (-0.5)
+    grad_query = grad_key = grad_value = jnp.zeros(query.shape, jnp.float32)
+    for lanes in head_lanes(query.shape[1]):
+        shares = full_shares(query[...], key[...], allowed[...], lanes)
+        head_up = only(lanes, grad_mixed)
+        grad_value = grad_value + product(shares.astype(jnp.bfloat16), head_up, FIRST)
+        grad_shares = product(head_up, value[...], LAST)
+        delta = jnp.sum(shares * grad_shares, axis=-1, keepdims=True)
+        grad_scores = (shares * (grad_shares - delta)).astype(jnp.bfloat16)
+        grad_query = grad_query + scale * jnp.dot(
+            grad_scores, only(lanes, key[...]), preferred_element_type=jnp.float32
+        )
+        grad_key = grad_key + scale * product(grad_scores, only(lanes, query[...]), FIRST)
+    grad_query = grad_query.astype(jnp.bfloat16)
+    grad_key = grad_key.astype(jnp.bfloat16)
+    grad_value = grad_value.astype(jnp.bfloat16)
+    work = RowSum(row, short, got_mixed, rows, *sems[8:10])
+    work.start(
+        product(grad_query, attention[0], LAST)
+        + product(grad_key, attention[1], LAST)
+        + product(grad_value, attention[2], LAST)
+    )
+    for which, part in enumerate((grad_query, grad_key, grad_value)):
+        attention_grads[which] = product(inputs[...], part, FIRST).astype(jnp.bfloat16)
+    attention_grads[3] = product(upstream, mixed[...], FIRST).astype(jnp.bfloat16)
+    part, gain = norm_back_sums(first[...], gains[0:1], work.finish())
+    gain_grads[0:1] = gain
+    work = RowSpread(row, mine, every_text, *sems[10:12])
+    work.start((grad + part).astype(jnp.bfloat16))
+    work.finish()
 
     def columns(index):
-        return every.at[:, pl.ds(pl.multiple_of(index * width, 128), width)]
-
-    result[column.me] = columns(column.me)[...]
-    exchange(column, columns, lambda index: result.at[index], *sems[2:])
-
-
-def text_back(values):
+        return every_text.at[:, pl.ds(pl.multiple_of(index * width, 128), width)]
+
+    text_rows[column.me] = columns(column.me)[...]
+    exchange(column, columns, lambda index: text_rows.at[index], *sems[12:14])
+
+
+def encoder_backward(grad_encoded, gains, attention, dense, allowed, kept):
     n = lax.axis_size("dp")
+    tokens = grad_encoded.shape[0]
     size = lax.axis_size("img") * lax.axis_size("t")
-    tokens = size * values.shape[0]
-    width = values.shape[1] // n
-    return small_call(
-        partial(text_back_kernel, n, size),
-        jax.ShapeDtypeStruct((n, tokens, width), values.dtype),
-        [pltpu.VMEM((tokens, n * width), values.dtype)] + semaphores(size) + semaphores(n),
-        [values],
-        6,
-        "text_back",
-    )
+    whole = pltpu.VMEM((tokens, D), jnp.bfloat16)
+    return encoder_call(
+        partial(encoder_back_kernel, n, size),
+        [
+            jax.ShapeDtypeStruct((n, tokens, D // n), jnp.bfloat16),
+            jax.ShapeDtypeStruct((8, D), jnp.float32),
+            jax.ShapeDtypeStruct(attention.shape, jnp.bfloat16),
+            jax.ShapeDtypeStruct(dense.shape, jnp.bfloat16),
+        ],
+        [whole, pltpu.VMEM((tokens // size, D), jnp.bfloat16)]
+        + [whole] * 6
+        + semaphores(size) * 6
+        + semaphores(n),
+        [grad_encoded, gains, attention, dense, allowed, *kept],
+        4,
+        "encoder_back",
+    )
+
+
+def causal_kernel(query, key, value, mixed, partition):
+    length = query.shape[0]
+    block = min(256, length)
+    scale = HEAD_DIM ** (-0.5)
+    halves = head_lanes(query.shape[1])
+    for begin in range(0, length, block):
+        at, end = pl.ds(begin, block), begin + block
+        ahead = lax.broadcasted_iota(jnp.int32, (block, end), 1) > begin + (
+            lax.broadcasted_iota(jnp.int32, (block, end), 0)
+        )
+        out = jnp.zeros((block, query.shape[1]), jnp.float32)
+        logs = jnp.zeros((block, query.shape[1]), jnp.float32)
+        for lanes in halves:
+            scores = product(only(lanes, query[at]), key[:end], LAST) * scale
+            scores = jnp.where(ahead, NEGATIVE, scores)
+            highest = jnp.max(scores, axis=-1, keepdims=True)
+            weight = jnp.exp(scores - highest)
+            total = jnp.sum(weight, axis=-1, keepdims=True)
+            shares = (weight * (1.0 / total)).astype(jnp.bfloat16)
+            out = out + jnp.dot(
+                shares, only(lanes, value[:end]), preferred_element_type=jnp.float32
+            )
+            logs = jnp.where(lanes, highest + jnp.log(total), logs)
+        mixed[at] = out.astype(jnp.bfloat16)
+        partition[at] = logs
+
+
+def causal_back_kernel(
+    query, key, value, upstream, partition, out_query, out_key, out_value, grad_key, grad_value
+):
+    length = query.shape[0]
+    block = min(256, length)
+    scale = HEAD_DIM ** (-0.5)
+    halves = head_lanes(query.shape[1])
+    grad_key[...] = jnp.zeros(grad_key.shape, jnp.float32)
+    grad_value[...] = jnp.zeros(grad_value.shape, jnp.float32)
+    for begin in range(0, length, block):
+        at, end = pl.ds(begin, block), begin + block
+        ahead = lax.broadcasted_iota(jnp.int32, (block, end), 1) > begin + (
+            lax.broadcasted_iota(jnp.int32, (block, end), 0)
+        )
+        grad_query = jnp.zeros((block, query.shape[1]), jnp.float32)
+        for head, lanes in enumerate(halves):
+            head_query, head_up = only(lanes, query[at]), only(lanes, upstream[at])
+            log = partition[at, head * HEAD_DIM : head * HEAD_DIM + 1]
+            scores = product(head_query, key[:end], LAST) * scale
+            shares = jnp.exp(jnp.where(ahead, NEGATIVE, scores) - log)
+            grad_value[:end] += product(shares.astype(jnp.bfloat16), head_up, FIRST)
+            grad_shares = product(head_up, value[:end], LAST)
+            delta = jnp.sum(shares * grad_shares, axis=-1, keepdims=True)
+            grad_scores = (shares * (grad_shares - delta)).astype(jnp.bfloat16)
+            grad_query = grad_query + jnp.dot(
+                grad_scores, only(lanes, key[:end]), preferred_element_type=jnp.float32
+            )
+            grad_key[:end] += product(grad_scores, head_query, FIRST)
+        out_query[at] = (grad_query * scale).astype(jnp.bfloat16)
+    out_key[...] = (grad_key[...] * scale).astype(jnp.bfloat16)
+    out_value[...] = grad_value[...].astype(jnp.bfloat16)
+
+
+def by_heads(kernel, operands, kinds, scratch):
+    length, width = operands[0].shape
+    lanes = min(128, width)
+    spec = pl.BlockSpec((length, lanes), lambda pair: (0, pair))
+    return pl.pallas_call(
+        kernel,
+        grid=(width // lanes,),
+        out_shape=[jax.ShapeDtypeStruct((length, width), kind) for kind in kinds],
+        in_specs=[spec] * len(operands),
+        out_specs=[spec] * len(kinds),
+        scratch_shapes=[pltpu.VMEM((length, lanes), jnp.float32)] * scratch,
+        compiler_params=pltpu.CompilerParams(vmem_limit_bytes=40 * 2**20),
+        cost_estimate=pl.CostEstimate(
+            flops=4 * length * length * width, bytes_accessed=2**25, transcendentals=length * length
+        ),
+        name="causal",
+    )(*operands)
+
+
+def causal_forward(query, key, value):
+    return by_heads(causal_kernel, (query, key, value), (jnp.bfloat16, jnp.float32), 0)
+
+
+def causal_backward(query, key, value, partition, upstream):
+    return by_heads(
+        causal_back_kernel, (query, key, value, upstream, partition), (jnp.bfloat16,) * 3, 2
+    )
+
+
+def table_kernel(blocks, table):
+    table[...] = blocks[0, 0]
+
+
+def table_of(blocks):
+    n, images, rows, columns = blocks.shape
+    return pl.pallas_call(
+        table_kernel,
+        grid=(images, n),
+        out_shape=jax.ShapeDtypeStruct((images * rows, n * columns), blocks.dtype),
+        in_specs=[pl.BlockSpec((1, 1, rows, columns), lambda i, z: (z, i, 0, 0))],
+        out_specs=pl.BlockSpec((rows, columns), lambda i, z: (i, z)),
+        cost_estimate=pl.CostEstimate(flops=0, bytes_accessed=2**24, transcendentals=0),
+        name="table",
+    )(blocks)
 
 
 def share_kernel(n, size, mine, every, *sems):
@@ -707,8 +968,6 @@
         return jnp.concatenate(
             [jnp.where(first, values, other), jnp.where(first, other, values)], axis=0
         )
-    if axis == ROW:
-        return row_spread(values)
     return lax.all_gather(values, axis, axis=0, tiled=True)
 
 
@@ -719,8 +978,6 @@
         away = lax.dynamic_slice_in_dim(values, (1 - place) * half, half, 0)
         came = lax.ppermute(away.astype(jnp.bfloat16), "t", [(0, 1), (1, 0)])
         return lax.dynamic_slice_in_dim(values, place * half, half, 0) + came.astype(jnp.float32)
-    if axis == ROW:
-        return row_collect(values)
     return lax.psum_scatter(
         values.astype(jnp.bfloat16), axis, scatter_dimension=0, tiled=True
     ).astype(jnp.float32)
@@ -765,70 +1022,23 @@
     return (grad_query, grad_key, grad_value)
 
 
-def causal_forward(parts, scale):
-    query, key, value = parts
-    length = query.shape[0]
-    block = min(512, length)
-    places = jnp.arange(length)
-    outputs = []
-    partitions = []
-    for begin in range(0, length, block):
-        allowed = begin + places[:block, None] >= places[None, :]
-        mixed, partition = core_forward(
-            query[None, begin : begin + block], key[None], value[None], allowed[None], scale
-        )
-        outputs.append(mixed[0])
-        partitions.append(partition[0])
-    return (jnp.concatenate(outputs, axis=0), jnp.concatenate(partitions, axis=1))
-
-
-def causal_backward(parts, scale):
-    query, key, value, partition, upstream = parts
-    length = query.shape[0]
-    block = min(512, length)
-    places = jnp.arange(length)
-    query_parts = []
-    grad_key = jnp.zeros(key.shape, jnp.float32)
-    grad_value = jnp.zeros(value.shape, jnp.float32)
-    for begin in range(0, length, block):
-        allowed = begin + places[:block, None] >= places[None, :]
-        part_query, part_key, part_value = core_backward(
-            query[None, begin : begin + block],
-            key[None],
-            value[None],
-            allowed[None],
-            scale,
-            partition[None, :, begin : begin + block],
-            upstream[None, begin : begin + block],
-        )
-        query_parts.append(part_query[0])
-        grad_key = grad_key + part_key[0]
-        grad_value = grad_value + part_value[0]
-    return (jnp.concatenate(query_parts, axis=0), grad_key, grad_value)
-
-
 def mix_forward(query, key, value, kind, context):
     scale = HEAD_DIM ** (-0.5)
     width = query.shape[1]
+    if kind == "self":
+        return causal_forward(query, key, value)
     query, key, value = (split_heads(part, 1) for part in (query, key, value))
-    if kind == "self":
-        mixed, partition = causal_forward((query[0], key[0], value[0]), scale)
-        partition = partition[None]
-    else:
-        mixed, partition = core_forward(query, key, value, context["allowed"], scale)
+    mixed, partition = core_forward(query, key, value, context["allowed"], scale)
     return (mixed.reshape(-1, width), partition)
 
 
 def mix_backward(query, key, value, partition, upstream, kind, context):
     scale = HEAD_DIM ** (-0.5)
     width = query.shape[1]
+    if kind == "self":
+        return causal_backward(query, key, value, partition, upstream)
     query, key, value, upstream = (split_heads(part, 1) for part in (query, key, value, upstream))
-    if kind == "self":
-        grads = causal_backward((query[0], key[0], value[0], partition[0], upstream[0]), scale)
-    else:
-        grads = core_backward(
-            query, key, value, context["allowed"], scale, partition, upstream
-        )
+    grads = core_backward(query, key, value, context["allowed"], scale, partition, upstream)
     return tuple(grad.reshape(-1, width).astype(jnp.bfloat16) for grad in grads)
 
 
@@ -985,21 +1195,6 @@
     text_rows, text_width = text_master.shape
     text_count = caption_ids.size
     mask = code_mask.astype(jnp.float32)
-    gain_width = gain_master.shape[1]
-    note = jnp.zeros((16, 128), jnp.float32)
-    note = note.at[:7, :gain_width].set(gain_master)
-    note = note.at[7, 0].set(jnp.sum(mask))
-    note = note.at[8 : 8 + text_count // 128].set(
-        caption_ids.astype(jnp.float32).reshape(-1, 128)
-    )
-    notes = share(note)
-    gain_set = (
-        jnp.transpose(notes[:, :, :7, :gain_width], (2, 0, 1, 3))
-        .reshape(7, D)
-    )
-    gain_set = lax.reduce_precision(gain_set, exponent_bits=8, mantissa_bits=7)
-    count = jnp.sum(notes[:, 0, 7, 0])
-    all_text = notes[:, 0, 8 : 8 + text_count // 128].reshape(-1).astype(jnp.int32)
     encoder_attention, encoder_dense, code_table = (
         lax.all_gather(attention_master[0].astype(jnp.bfloat16), "dp", axis=1, tiled=True),
         lax.all_gather(dense_master[0].astype(jnp.bfloat16), "dp", axis=1, tiled=True),
@@ -1018,14 +1213,37 @@
     self_weights, cross_weights, dense_weights = (
         matrices_of(weights, n) for weights in (self_weights, cross_weights, dense_weights)
     )
-    out_part, self_weights = lax.optimization_barrier(
-        (code_master[1].astype(jnp.bfloat16), self_weights)
-    )
-    out_table = lax.all_gather(
-        lax.all_gather(out_part, "dp", axis=1, tiled=True), "img", axis=0, tiled=True
-    )
+    previous = jnp.concatenate(
+        [jnp.zeros((images, 1), jnp.int32), code_ids[:, :-1]], axis=1
+    ).reshape(-1)
+    starting = jnp.broadcast_to(jnp.arange(length) > 0, (images, length)).reshape(-1)
+    code_table, self_weights, mask, encoder_attention, encoder_dense = lax.optimization_barrier(
+        (code_table, self_weights, mask, encoder_attention, encoder_dense)
+    )
+    decoder_in = code_forward(previous, starting, code_table)
+    out_part, decoder_in = lax.optimization_barrier(
+        (code_master[1].astype(jnp.bfloat16), decoder_in)
+    )
+    out_table = table_of(
+        lax.all_gather(out_part, ("dp", "img")).reshape((n, 4) + code_shape)
+    )
+    gain_width = gain_master.shape[1]
+    note = jnp.zeros((16, 128), jnp.float32)
+    note = note.at[:7, :gain_width].set(gain_master)
+    note = note.at[7, 0].set(jnp.sum(mask))
+    note = note.at[8 : 8 + text_count // 128].set(
+        caption_ids.astype(jnp.float32).reshape(-1, 128)
+    )
+    notes = share(note)
+    gain_set = (
+        jnp.transpose(notes[:, :, :7, :gain_width], (2, 0, 1, 3))
+        .reshape(7, D)
+    )
+    gain_set = lax.reduce_precision(gain_set, exponent_bits=8, mantissa_bits=7)
+    count = jnp.sum(notes[:, 0, 7, 0])
+    all_text = notes[:, 0, 8 : 8 + text_count // 128].reshape(-1).astype(jnp.int32)
     segments = caption_segments.reshape(-1)
-    encoder_context = {"allowed": (segments[:, None] == segments[None, :])[None]}
+    same = (segments[:, None] == segments[None, :]).astype(jnp.float32)
     row = jnp.sum(jnp.where(jnp.arange(images) == image, image_row, 0)) - z * caption_rows
     owners = lax.dynamic_index_in_dim(caption_segments, row, 0, False)
     cross_context = {"allowed": (owners == z * images + image)[None, None, :]}
@@ -1033,21 +1251,15 @@
     text_inside = (text_local >= 0) & (text_local < text_rows)
     picked = jnp.take(text_master, jnp.clip(text_local, 0, text_rows - 1), axis=0)
     picked = jnp.where(text_inside[:, None], picked, 0.0).astype(jnp.bfloat16)
-    encoder_in = text_in(picked.reshape(n, text_count, text_width))
-    branch, encoder_attention_keep = attention_forward(
-        encoder_in, gain_set[0], encoder_attention, "encoder", ROW, encoder_context
-    )
-    encoder_mid = encoder_in + branch
-    branch, encoder_dense_keep = dense_forward(encoder_mid, gain_set[1], encoder_dense, ROW)
-    encoder_top = encoder_mid + branch
-    encoded = spread(rms_norm(encoder_top, gain_set[2]).astype(jnp.bfloat16), ROW)
+    encoder_gains = jnp.concatenate([gain_set, jnp.zeros((1, D), jnp.float32)])
+    encoded, encoder_keep = encoder_forward(
+        picked.reshape(n, text_count, text_width),
+        encoder_gains,
+        encoder_attention,
+        encoder_dense,
+        same,
+    )
     caption = lax.dynamic_slice_in_dim(encoded, row * caption_length, caption_length, 0)
-    previous = jnp.concatenate(
-        [jnp.zeros((images, 1), jnp.int32), code_ids[:, :-1]], axis=1
-    ).reshape(-1)
-    starting = jnp.broadcast_to(jnp.arange(length) > 0, (images, length)).reshape(-1)
-    code_table, encoder_in = lax.optimization_barrier((code_table, encoder_in))
-    decoder_in = code_forward(previous, starting, code_table)
     branch, self_keep = attention_forward(
         decoder_in, gain_set[3], self_weights, "self", "t", None
     )
@@ -1129,28 +1341,12 @@
         2,
     )
     grad_code_in = code_backward(grad_start, previous, starting, code_shape[0])
-    grad_encoded = collect(
-        lax.dynamic_update_slice_in_dim(
-            jnp.zeros(encoded.shape, jnp.float32), grad_caption, row * caption_length, 0
-        ),
-        ROW,
-    )
-    grad_encoder_top, gain_two = norm_back(encoder_top, gain_set[2], grad_encoded)
-    grad_branch, gain_one, dense_zero = dense_backward(
-        grad_encoder_top, encoder_mid, gain_set[1], ROW, encoder_dense_keep
-    )
-    grad_encoder_mid = grad_encoder_top + grad_branch
-    grad_branch, gain_zero, attention_zero, _ = attention_backward(
-        grad_encoder_mid,
-        encoder_in,
-        gain_set[0],
-        encoder_attention,
-        "encoder",
-        ROW,
-        encoder_context,
-        encoder_attention_keep,
-    )
-    text_rows_back = text_back((grad_encoder_mid + grad_branch).astype(jnp.bfloat16))
+    grad_encoded = lax.dynamic_update_slice_in_dim(
+        jnp.zeros(encoded.shape, jnp.float32), grad_caption, row * caption_length, 0
+    )
+    text_rows_back, encoder_gain_grads, attention_zero, dense_zero = encoder_backward(
+        grad_encoded, encoder_gains, encoder_attention, encoder_dense, same, encoder_keep
+    )
     text_hits = jnp.arange(text_rows, dtype=jnp.int32)[:, None] == text_local[None, :]
     text_grads = jnp.dot(
         text_hits.astype(jnp.bfloat16),
@@ -1165,12 +1361,12 @@
 
     attention_grads = jnp.stack(
         [
-            owned(jnp.stack(attention_zero), 1),
+            owned(attention_zero, 1),
             one_grads.reshape(attention_shape),
             two_grads.reshape(attention_shape),
         ]
     )
-    dense_grads = jnp.stack([owned(jnp.stack(dense_zero), 1), dense_one_grads.reshape(dense_shape)])
+    dense_grads = jnp.stack([owned(dense_zero, 1), dense_one_grads.reshape(dense_shape)])
     code_grads = jnp.stack([owned(grad_code_in, 1), out_grads.reshape(code_shape)])
     squares = (
         jnp.sum(attention_grads * attention_grads)
@@ -1178,7 +1374,12 @@
         + jnp.sum(text_grads * text_grads)
         + jnp.sum(code_grads * code_grads)
     )
-    sums = jnp.stack([gain_zero, gain_one, gain_two, gain_three, gain_four, gain_five, gain_six])
+    sums = jnp.concatenate(
+        [
+            encoder_gain_grads[:3],
+            jnp.stack([gain_three, gain_four, gain_five, gain_six]),
+        ]
+    )
     tail = jnp.zeros((1, D), jnp.float32).at[0, 0].set(squares).at[0, 1].set(loss_part)
     sums = total_of(jnp.concatenate([sums, tail], axis=0))
     gain_sums = sums[:7]

time: 1180 us -> 1150 us (0.975)
  matrix products: 300 us -> 183 us
  Pallas kernels: 555 us -> 648 us
  other arithmetic: 168 us -> 96.7 us
  waiting for transfers between devices: 60.9 us -> 124 us
    pallas_call x0 -> x5, Pallas kernels: none -> 198 us  [the longest x2 149 us: encoder_call(): pl.pallas_call(kernel, out_shape=out_shape, in_specs=[vmem] * len(operand...]
    pallas_call x14 -> x2, Pallas kernels: 213 us -> 29.2 us  [small_call(): pl.pallas_call(kernel, out_shape=out_shape, in_specs=[vmem] * len(operand...]
    reduce_scatter x1, waiting for transfers between devices: 0.02 us -> 52.4 us  [code_forward(): lax.psum_scatter(picked, ROW, scatter_dimension=0, tiled=True)]
    pallas_call x1, Pallas kernels: 170 us -> 222 us  [gather(): pl.pallas_call(partial(gather_kernel, n, slabs, count), out_shape=[jax.Sh...]
    dot_general x4 -> x1, matrix products: 31.1 us -> 1.04 us  [core_backward(): jnp.einsum('bqhe,bkhe->bhqk', upstream, value, preferred_element_type=jnp...]
    convert_element_type x4 -> x1, other arithmetic: 28.1 us -> 1.25 us  [core_backward(): grad_scores = (shares * (grad_shares - inner)).astype(jnp.bfloat16)]
    pallas_call x1, Pallas kernels: 172 us -> 199 us  [scatter(): pl.pallas_call(partial(scatter_kernel, n, slabs, members), out_shape=[jax...]
    dot_general x35 -> x23, matrix products: 122 us -> 96.9 us  [product(): lax.dot_general(left, right, dims, preferred_element_type=jnp.float32)]
  transfers between devices with their start and end apart: 27 -> 26, of which waited for: 13 -> 13; matrix products, arithmetic and copies ran while one was open for 32% -> 17% of each run, Pallas kernels for 46% -> 53%
where the time goes in v2:
time: 1150 us; the launch traced here: 1140 us
  Pallas kernels  648 us (56%)
  matrix products  183 us (16%)
  waiting for transfers between devices  124 us (11%)
  other arithmetic  96.7 us (8%)
  local copies, waits for them, and re-layouts  48.8 us (4%)
  between operations  26 us (2%)
    pallas_call x1, Pallas kernels, gather(): pl.pallas_call(partial(gather_kernel, n, slabs, count), out_shape=[jax.Sh...  222 us
    pallas_call x1, Pallas kernels, scatter(): pl.pallas_call(partial(scatter_kernel, n, slabs, members), out_shape=[jax...  199 us
    pallas_call x2, Pallas kernels, encoder_call(): pl.pallas_call(kernel, out_shape=out_shape, in_specs=[vmem] * len(operand...  149 us
    dot_general x23, matrix products, product(): lax.dot_general(left, right, dims, preferred_element_type=jnp.float32)  96.9 us
    reduce_scatter x1, waiting for transfers between devices, code_forward(): lax.psum_scatter(picked, ROW, scatter_dimension=0, tiled=True)  52.4 us
    all_gather x1, waiting for transfers between devices, per_device(): lax.all_gather(out_part, ('dp', 'img')).reshape((n, 4) + code_shape)  45.8 us
    pallas_call x2, Pallas kernels, by_heads(): pl.pallas_call(kernel, grid=(width // lanes,), out_shape=[jax.ShapeDtypeS...  37.1 us
    unnamed x337, local copies, waits for them, and re-layouts  30.9 us
  transfers between devices with their start and end apart: 26, of which 13 were waited for; matrix products, arithmetic and copies ran while one was open for 17% of the time, Pallas kernels for 53%

profile of v2, /device:TPU:0, one launch (start us, length us, event | category | flops | bytes accessed | tf_op | source)
XLA Modules:
  0.0 1141.3 jit_solution(17417610617366557948)
XLA Ops:
  13.5 222.4 %gather.11 = (bf16[4,1024,512]{2,1,0:T(8,128)(2,1)}, bf16[4,1024,512]{2,1,0:T(8,128)(2,1)}, bf16[2,1024,2048]{2,1,0:T(8,128)(2,1)}) custom-call(bf16[4,256,128]{2,1,0:T(8,128)(2,1)} %get-tuple-element.217.refs_0_, bf16[4,256,128]{2,1,0:T(8,128)(2,1)} %get-tuple-element.216.refs_1_, bf16[2,256,512]{2,1,0:T(8,128)(2,1)} %get-tuple-element.212.refs_2_), custom_call_target="tpu_custom_call" | custom-call | bytes 268435456 | tf_op jit(solution)/shard_map/gather/pallas_call | solution.py:228
  236.0 13.8 %fusion.16 = bf16[4096,1024]{1,0:T(8,128)(2,1)} fusion(bf16[1024,1024]{1,0:T(8,128)(2,1)} %bitcast.266, s32[4096]{0:T(1024)S(1)} %bitcast.249, pred[4096]{0:T(1024)(128)(4,1)S(1)} %bitcast.259), kind=kOutput, calls=%fused_computation.32 | convolution fusion | flops 8602517504 | bytes 10506240 | tf_op jit(solution)/shard_map/dot_general | solution.py:1116
  252.6 13.6 %share.1 = f32[4,8,16,128]{3,2,1,0:T(8,128)} custom-call(f32[16,128]{1,0:T(8,128)} %copy-done.131), custom_call_target="tpu_custom_call" | custom-call | bytes 16777216 | tf_op jit(solution)/shard_map/share/pallas_call | solution.py:510
  268.1 52.4 %reduce-scatter.7.cloned.1.call-done = bf16[512,1024]{1,0:T(8,128)(2,1)} async-done(((bf16[4096,1024]{1,0:T(8,128)(2,1)}), bf16[512,1024]{1,0:T(8,128)(2,1)}) %reduce-scatter.7.cloned.1.call-update) | async-done | bytes 1048592 | tf_op jit(solution)/shard_map/reduce_scatter | solution.py:1117
  330.8 14.1 %causal.2 = (bf16[1024,512]{1,0:T(8,128)(2,1)S(1)}, f32[1024,512]{1,0:T(8,128)S(1)}) custom-call(bf16[1024,512]{1,0:T(8,128)(2,1)S(1)} %convolution_convert_fusion.16.query, bf16[1024,512]{1,0:T(8,128)(2,1)S(1)} %convolution_convert_fusion.15.key, bf16[1024,512]{1,0:T(8,128)(2,1)S(1)} %convolution_convert_fusion.14.value), custom_call_target="tpu_custom_call" | custom-call | flops 2147483648 | bytes 33554432 | tf_op jit(solution)/shard_map/causal/pallas_call | solution.py:847
  357.8 4.6 gather_fusion
  363.8 61.6 %encoder.1 = (bf16[256,1024]{1,0:T(8,128)(2,1)S(1)}, f32[32,1024]{1,0:T(8,128)S(1)}, f32[32,1024]{1,0:T(8,128)S(1)}, f32[32,1024]{1,0:T(8,128)S(1)}, bf16[256,10...) custom-call(bf16[4,256,256]{2,1,0:T(8,128)(2,1)S(1)} %select_convert, ...), custom_call_target="tpu_custom_call" | custom-call | bytes 134217728 | tf_op jit(solution)/shard_map/encoder/pallas_call | solution.py:641
  449.4 3.1 multiply_reduce_fusion.11
  456.2 26.0 %multiply_convert_fusion.1 = (bf16[1024,2048]{1,0:T(8,128)(2,1)S(1)}, f32[1024,2048]{1,0:T(8,128)}, f32[1024,2048]{1,0:T(8,128)}) fusion(bf16[2,1024,2048]{2,1,0:T(8,128)(2,1)S(1)} %bitcast.263, bf16[512,1024]{1,0:T(8,128)(2,1)S(1)} %get-tuple-element.206, bf16[512,1024]{1,0:T(8,128)(2,1)S(1)} %get-tuple-element.205), kind=kOutput, calls=%fused_computation.12 | convolution fusion | flops 4435476480 | bytes 27262976 | tf_op jit(solution)/shard_map/dot_general | solution.py:1087
  482.1 4.5 fusion.21
  499.1 3.4 broadcast_select_fusion.7
  502.5 45.8 %all-gather.19.cloned.1.call-done = bf16[16384,256]{1,0:T(8,128)(2,1)} async-done(((bf16[1024,256]{1,0:T(8,128)(2,1)}), bf16[16384,256]{1,0:T(8,128)(2,1)}) %all-gather.19.cloned.1.call-update) | async-done | bytes 8388624 | tf_op jit(solution)/shard_map/all_gather | solution.py:1228
  548.3 11.9 %table.1 = bf16[4096,1024]{1,0:T(8,128)(2,1)} custom-call(bf16[4,4,1024,256]{3,2,1,0:T(8,128)(2,1)} %bitcast.203), custom_call_target="tpu_custom_call" | custom-call | bytes 16777216 | tf_op jit(solution)/shard_map/table/pallas_call | solution.py:878
  560.2 15.1 %fusion.159 = (f32[1024]{0:T(1024)S(1)}, f32[1024,4096]{1,0:T(8,128)}) fusion(bf16[4096,1024]{1,0:T(8,128)(2,1)} %table.1, bf16[512,1024]{1,0:T(8,128)(2,1)} %get-tuple-element.204, bf16[512,1024]{1,0:T(8,128)(2,1)S(1)} %get-tuple-element.203), kind=kOutput, calls=%fused_computation.335 | convolution fusion | flops 8598322176 | bytes 27267072 | tf_op jit(solution)/shard_map/dot_general | solution.py:987
  575.4 10.2 exponential_reduce_fusion
  588.3 8.8 multiply_convert_fusion
  597.1 8.8 fusion.161
  612.0 11.3 convolution_convert_fusion
  625.3 15.0 %add_convert_fusion = bf16[1024,2048]{1,0:T(8,128)(2,1)S(1)} fusion(f32[1024,2048]{1,0:T(8,128)} %get-tuple-element.190, f32[1024,2048]{1,0:T(8,128)} %get-tuple-element.232, bf16[2,1024,2048]{2,1,0:T(8,128)(2,1)} %get-tuple-element.127, bf16[512,1024]{1,0:T(8,128)(2,1)S(1)} %get-tuple-element.202, bf16[512,1024]{1,0:T(8,128)(2,1)S(1)} %get-tuple-element.201), kind=kOutput, calls=%fused_computation.11 | convolution fusion | flops 4328521728 | bytes 27262976 | tf_op jit(solution)/shard_map/dot_general | solution.py:1096
  640.4 4.5 fusion.23
  671.4 23.0 %causal.3 = (bf16[1024,512]{1,0:T(8,128)(2,1)S(1)}, bf16[1024,512]{1,0:T(8,128)(2,1)S(1)}, bf16[1024,512]{1,0:T(8,128)(2,1)S(1)}) custom-call(bf16[1024,512]{1,0:T(8,128)(2,1)S(1)} %copy-done.32, bf16[1024,512]{1,0:T(8,128)(2,1)S(1)} %copy-done.30, bf16[1024,512]{1,0:T(8,128)(2,1)S(1)} %copy-done.28, ...), custom_call_target="tpu_custom_call" | custom-call | flops 2147483648 | bytes 33554432 | tf_op jit(solution)/shard_map/causal/pallas_call | solution.py:847
  713.5 87.1 %encoder_back.1 = (bf16[4,256,256]{2,1,0:T(8,128)(2,1)S(1)}, f32[8,1024]{1,0:T(8,128)S(1)}, bf16[4,1024,128]{2,1,0:T(8,128)(2,1)}, bf16[2,1024,512]{2,1,0:T(8,128)(2,1)}) custom-call(f32[256,1024]{1,0:T(8,128)S(1)} %fusion.54.grad_encoded, f32[8,1024]{1,0:T(8,128)S(1)} %concatenate.43.gains, bf16[4,1024,128]{2,1,0:T(8,128)(2,1)} %bitcast.200, ...), custom_call_target="tpu_custom_call" | custom-call | bytes 134217728 | tf_op jit(solution)/shard_map/encoder_back/pallas_call | solution.py:641
  804.8 8.2 all-gather.4
  814.2 9.2 convolution_convert_fusion.1.refs_9_
  823.4 14.6 %fusion.49 = bf16[1024,1024]{1,0:T(8,128)(2,1)} fusion(bf16[4096,1024]{1,0:T(8,128)(2,1)} %all-gather.11.cloned.1.call-done, s32[4096]{0:T(1024)S(1)} %bitcast.250, pred[4096]{0:T(1024)(128)(4,1)S(1)} %bitcast.260), kind=kOutput, calls=%fused_computation.124 | convolution fusion | flops 8599371776 | bytes 10506240 | tf_op jit(solution)/shard_map/dot_general | solution.py:987
  839.3 9.2 convolution_convert_fusion.2.refs_8_
  851.4 3.5 multiply_reduce_fusion.14
  869.1 198.6 %scatter.33 = (f32[1024,128]{1,0:T(8,128)}, f32[1024,128]{1,0:T(8,128)}, f32[512,512]{1,0:T(8,128)}) custom-call(bf16[1024,512]{1,0:T(8,128)(2,1)} %convolution_convert_fusion.10.refs_0_, bf16[1024,512]{1,0:T(8,128)(2,1)} %convolution_convert_fusion.9.refs_1_, bf16[1024,512]{1,0:T(8,128)(2,1)} %convolution_convert_fusion.8.refs_2_, ...), custom_call_target="tpu_custom_call" | custom-call | bytes 268435456 | tf_op jit(solution)/shard_map/scatter/pallas_call | solution.py:409
  1083.7 15.6 %total.1 = f32[8,1024]{1,0:T(8,128)} custom-call(f32[8,1024]{1,0:T(8,128)} %concatenate.49.mine), custom_call_target="tpu_custom_call" | custom-call | bytes 16777216 | tf_op jit(solution)/shard_map/total/pallas_call | solution.py:510
  1103.4 4.9 fusion.142
  1108.4 3.4 fusion.146
  1118.3 3.3 multiply_add_fusion
  (536 shorter events, 183.7 us)
Async XLA Ops:
  7.2 228.7 %all-gather.15.cloned.1.call-start = ((), (), s32[]{:S(2)}) async-start(), calls=%async_computation.14 | async-start | bytes 1310720 | tf_op jit(solution)/shard_map/all_gather | solution.py:1199
  9.9 226.1 %all-gather.13.cloned.1.call-start = ((), (), s32[]{:S(2)}) async-start(), calls=%async_computation.13 | async-start | bytes 2621440 | tf_op jit(solution)/shard_map/all_gather | solution.py:1201
  11.1 224.9 %all-gather.17.cloned.1.call-start = ((), (), s32[]{:S(2)}) async-start(), calls=%async_computation.15 | async-start | bytes 2621440 | tf_op jit(solution)/shard_map/all_gather | solution.py:1200
  13.2 307.2 %reduce-scatter.7.cloned.1.call-start = ((), (), s32[]{:S(2)}) async-start(), calls=%async_computation.6 | async-start | bytes 9437184 | tf_op jit(solution)/shard_map/reduce_scatter | solution.py:1117
  13.4 236.4 %copy-start.143 = (s32[1,8,4,128]{3,1,2,0:T(8,128)}, s32[1,8,4,128]{3,1,2,0:T(8,128)S(1)}, u32[]{:S(2)}) copy-start(s32[1,8,4,128]{3,1,2,0:T(8,128)S(1)} %copy.82) | copy-start | bytes 49156
  13.4 237.1 %copy-start.122 = (f32[4,1024]{1,0:T(4,128)}, f32[4,1024]{1,0:T(4,128)S(1)}, u32[]{:S(2)}) copy-start(f32[4,1024]{1,0:T(4,128)S(1)} %convert_element_type.296) | copy-start | bytes 49156
  13.5 236.3 %copy-start.150 = (pred[1,8,4,128]{3,1,2,0:T(8,128)(4,1)}, pred[1,8,4,128]{3,1,2,0:T(8,128)(4,1)S(1)}, u32[]{:S(2)}) copy-start(pred[1,8,4,128]{3,1,2,0:T(8,128)(4,1)S(1)} %copy.84) | copy-start | bytes 12292
  249.8 298.5 %all-gather.19.cloned.1.call-start = ((), (), s32[]{:S(2)}) async-start(), calls=%async_computation.16 | async-start | bytes 8912896 | tf_op jit(solution)/shard_map/all_gather | solution.py:1228
  322.4 2.9 collective-permute-start
  348.7 3.7 collective-permute-start.1
  351.6 82.4 %copy-start.118 = (f32[1024]{0:T(1024)}, f32[1024]{0:T(1024)S(1)}, u32[]{:S(2)}) copy-start(f32[1024]{0:T(1024)S(1)} %mul.626) | copy-start | bytes 12292
  354.7 79.3 %copy-start.127 = (f32[512]{0:T(512)}, f32[512]{0:T(512)S(1)}, u32[]{:S(2)}) copy-start(f32[512]{0:T(512)S(1)} %fusion.123) | copy-start | bytes 6148
  357.2 76.7 %collective-permute-start.2 = (bf16[512,1024]{1,0:T(8,128)(2,1)}, bf16[512,1024]{1,0:T(8,128)(2,1)}, u32[]{:S(2)}, u32[]{:S(2)}) collective-permute-start(bf16[512,1024]{1,0:T(8,128)(2,1)} %multiply_convert_fusion.6), channel_id=1, source_target_pairs={{0,1},{1,0},{2,3},{3,2},{4,5},{5,4},{6,7},{7,6},{8,9},{9,8},{10,11... | collective-permute-start | bytes 3145736 | tf_op jit(solution)/shard_map/ppermute | solution.py:966
  433.5 368.7 %reduce-scatter.15.cloned.1.call-start = ((), (), s32[]{:S(2)}) async-start(), calls=%async_computation.11 | async-start | bytes 10485760 | tf_op jit(solution)/shard_map/reduce_scatter | solution.py:1310
  446.0 3.5 collective-permute-start.3
  452.9 2.7 collective-permute-start.4
  488.9 2.9 collective-permute-start.5
  496.3 2.9 collective-permute-start.6
  502.5 57.7 %copy-start.105 = (bf16[512,1024]{1,0:T(8,128)(2,1)}, bf16[512,1024]{1,0:T(8,128)(2,1)S(1)}, u32[]{:S(2)}) copy-start(bf16[512,1024]{1,0:T(8,128)(2,1)S(1)} %get-tuple-element.203) | copy-start | bytes 3145732
  585.6 1.3 collective-permute-start.7
  606.1 2.7 collective-permute-start.8
  611.9 11.5 %collective-permute-start.9 = (bf16[512,1024]{1,0:T(8,128)(2,1)}, bf16[512,1024]{1,0:T(8,128)(2,1)}, u32[]{:S(2)}, u32[]{:S(2)}) collective-permute-start(bf16[512,1024]{1,0:T(8,128)(2,1)} %fusion.140), channel_id=1, source_target_pairs={{0,1},{1,0},{2,3},{3,2},{4,5},{5,4},{6,7},{7,6},{8,9},{9,8},{10,11... | collective-permute-start | bytes 3145736 | tf_op jit(solution)/shard_map/ppermute | solution.py:966
  623.4 200.1 %all-gather.11.cloned.1.call-start = ((), (), s32[]{:S(2)}) async-start(), calls=%async_computation.9 | async-start | bytes 9437184 | tf_op jit(solution)/shard_map/all_gather | solution.py:1121
  645.2 2.8 collective-permute-start.10
  650.4 2.7 collective-permute-start.11
  661.1 2.7 collective-permute-start.12
  665.3 2.7 collective-permute-start.13
  698.7 2.8 collective-permute-start.14
  704.0 363.7 %reduce-scatter.9.cloned.1.call-start = ((), (), s32[]{:S(2)}) async-start(), calls=%async_computation.7 | async-start | bytes 1310720 | tf_op jit(solution)/shard_map/reduce_scatter | solution.py:1358
  801.4 270.4 %reduce-scatter.11.cloned.1.call-start = ((), (), s32[]{:S(2)}) async-start(), calls=%async_computation.8 | async-start | bytes 2621440 | tf_op jit(solution)/shard_map/reduce_scatter | solution.py:1358
  802.1 274.0 %reduce-scatter.17.cloned.1.call-start = ((), (), s32[]{:S(2)}) async-start(), calls=%async_computation.12 | async-start | bytes 2621440 | tf_op jit(solution)/shard_map/reduce_scatter | solution.py:1309
  802.7 273.4 %reduce-scatter.13.cloned.1.call-start = ((), (), s32[]{:S(2)}) async-start(), calls=%async_computation.10 | async-start | bytes 2621440 | tf_op jit(solution)/shard_map/reduce_scatter | solution.py:1358
  (160 other events, 727.1 us)
Sparse Core Ops, SparseCore 0:
  10.2 39.7 all-gather.14
  52.1 61.6 all-gather.12
  116.0 61.9 all-gather.16
  249.9 70.4 reduce-scatter.6
  433.6 114.6 all-gather.18
  623.5 84.6 reduce-scatter.14
  710.6 80.0 all-gather.10
  801.5 28.9 reduce-scatter.8
  832.9 42.5 reduce-scatter.10
  877.6 74.6 reduce-scatter.16
  955.4 76.6 reduce-scatter.12

commit v3 on v2

--- a/solution.py
+++ b/solution.py
@@ -27,7 +27,7 @@
 
 
 MESH = pl.DeviceIdType.MESH
-ORDERS = ((0, 1, 2), (0, 2, 1), (1, 0, 2), (2, 0, 1))
+ORDERS = ((0, 1, 2), (0, 2, 1))
 
 
 def sources(n):
@@ -59,27 +59,29 @@
     slabs = []
     base = 0.0
     for which, (rows, _) in enumerate(shapes):
-        small = max(16, rows // 6 // 16 * 16)
-        large = (rows - 2 * small) // 2 // 16 * 16
-        begin = 0
-        for order, count in zip(ORDERS, (small, small, large, rows - 2 * small - large)):
-            slabs.append((which, begin, count, order, base))
-            begin += count
-        base += gap
+        count = 4 if rows % 64 == 0 else 2
+        for part in range(count):
+            size = rows // count
+            order = ORDERS[part % len(ORDERS)]
+            slabs.append((which, part * size, size, order, base + gap * (part // 2)))
+        base += gap * (count // 2)
     return slabs
 
 
-def wide(shape, n):
+def wide(shape, table, n):
     _, rows, columns = shape
+    if table:
+        return (4 * rows, n * columns)
     return (n * rows, 4 * columns) if columns % 128 == 0 else (4 * n * rows, columns)
 
 
-def placed(whole, shape, z, i, begin, rows):
-    if shape[2] % 128 == 0:
+def placed(whole, shape, table, z, i, begin, rows):
+    if table or shape[2] % 128 == 0:
+        down, right = (i, z) if table else (z, i)
         return whole.at[
             :,
-            pl.ds(pl.multiple_of(z * shape[1] + begin, 16), rows),
-            pl.ds(pl.multiple_of(i * shape[2], 128), shape[2]),
+            pl.ds(pl.multiple_of(down * shape[1] + begin, 16), rows),
+            pl.ds(pl.multiple_of(right * shape[2], 128), shape[2]),
         ]
     return whole.at[:, pl.ds(pl.multiple_of((z * 4 + i) * shape[1] + begin, 16), rows)]
 
@@ -138,7 +140,8 @@
     return jnp.logical_and(first, second)
 
 
-def gather_kernel(n, slabs, count, *refs):
+def gather_kernel(n, slabs, tables, *refs):
+    count = len(tables)
     ins, outs = refs[:count], refs[count : 2 * count]
     send_sem, recv_sem, local_sem = refs[2 * count :]
     here = Here(n)
@@ -147,16 +150,17 @@
     for which in range(count):
         shape = ins[which].shape
         copy = pltpu.make_async_copy(
-            ins[which], placed(outs[which], shape, here.z, here.i, 0, shape[1]), local_sem.at[which]
+            ins[which],
+            placed(outs[which], shape, tables[which], here.z, here.i, 0, shape[1]),
+            local_sem.at[which],
         )
         copy.start()
         local.append(copy)
 
     def block(slab, far, bits):
         which, begin, rows = slabs[slab][:3]
-        return placed(
-            outs[which], ins[which].shape, here.z + far, jnp.bitwise_xor(here.i, bits), begin, rows
-        )
+        z, i = here.z + far, jnp.bitwise_xor(here.i, bits)
+        return placed(outs[which], ins[which].shape, tables[which], z, i, begin, rows)
 
     def name(far, bits):
         return (here.z + far) * 4 + jnp.bitwise_xor(here.i, bits)
@@ -221,14 +225,15 @@
         copy.wait()
 
 
-def gather(arrays, n, gap, collective_id):
+def gather(arrays, tables, n, gap, collective_id):
     count = len(arrays)
     slabs = cut_slabs([a.shape[1:] for a in arrays], gap)
     size = sum(a.size * a.dtype.itemsize for a in arrays) * 4 * n
     return pl.pallas_call(
-        partial(gather_kernel, n, slabs, count),
+        partial(gather_kernel, n, slabs, tables),
         out_shape=[
-            jax.ShapeDtypeStruct((a.shape[0],) + wide(a.shape, n), a.dtype) for a in arrays
+            jax.ShapeDtypeStruct((a.shape[0],) + wide(a.shape, table, n), a.dtype)
+            for a, table in zip(arrays, tables)
         ],
         in_specs=[pl.BlockSpec(memory_space=pl.ANY)] * count,
         out_specs=[pl.BlockSpec(memory_space=pl.ANY)] * count,
@@ -511,7 +516,7 @@
         kernel,
         out_shape=out_shape,
         in_specs=[vmem] * len(operands),
-        out_specs=vmem,
+        out_specs=[vmem] * len(out_shape) if isinstance(out_shape, list) else vmem,
         scratch_shapes=scratch,
         compiler_params=pltpu.CompilerParams(
             collective_id=collective_id, has_side_effects=True
@@ -869,23 +874,6 @@
     )
 
 
-def table_kernel(blocks, table):
-    table[...] = blocks[0, 0]
-
-
-def table_of(blocks):
-    n, images, rows, columns = blocks.shape
-    return pl.pallas_call(
-        table_kernel,
-        grid=(images, n),
-        out_shape=jax.ShapeDtypeStruct((images * rows, n * columns), blocks.dtype),
-        in_specs=[pl.BlockSpec((1, 1, rows, columns), lambda i, z: (z, i, 0, 0))],
-        out_specs=pl.BlockSpec((rows, columns), lambda i, z: (i, z)),
-        cost_estimate=pl.CostEstimate(flops=0, bytes_accessed=2**24, transcendentals=0),
-        name="table",
-    )(blocks)
-
-
 def share_kernel(n, size, mine, every, *sems):
     row, column = Row(size), Column(n)
     greet(row, column)
@@ -909,7 +897,7 @@
     )
 
 
-def total_kernel(n, size, mine, result, row_got, column_got, part, *sems):
+def total_kernel(n, size, mine, result, row_result, row_got, column_got, part, *sems):
     row, column = Row(size), Column(n)
     greet(row, column)
     row_got[row.me] = mine[...]
@@ -924,6 +912,7 @@
     for index in range(1, n):
         added = added + column_got[index]
     result[...] = added
+    row_result[...] = part[...]
 
 
 def total_of(values):
@@ -931,7 +920,7 @@
     size = lax.axis_size("img") * lax.axis_size("t")
     return small_call(
         partial(total_kernel, n, size),
-        jax.ShapeDtypeStruct(values.shape, values.dtype),
+        [jax.ShapeDtypeStruct(values.shape, values.dtype)] * 2,
         [
             pltpu.VMEM((size,) + values.shape, values.dtype),
             pltpu.VMEM((n,) + values.shape, values.dtype),
@@ -1200,16 +1189,19 @@
         lax.all_gather(dense_master[0].astype(jnp.bfloat16), "dp", axis=1, tiled=True),
         lax.all_gather(code_master[0].astype(jnp.bfloat16), "dp", axis=1, tiled=True),
     )
-    self_weights, cross_weights, dense_weights = gather(
+    self_weights, cross_weights, dense_weights, out_table = gather(
         [
             attention_master[1].astype(jnp.bfloat16),
             attention_master[2].astype(jnp.bfloat16),
             dense_master[1].astype(jnp.bfloat16),
+            code_master[1:2].astype(jnp.bfloat16),
         ],
+        [False, False, False, True],
         n,
-        2.0,
+        1.0,
         0,
     )
+    out_table = out_table[0]
     self_weights, cross_weights, dense_weights = (
         matrices_of(weights, n) for weights in (self_weights, cross_weights, dense_weights)
     )
@@ -1221,12 +1213,6 @@
         (code_table, self_weights, mask, encoder_attention, encoder_dense)
     )
     decoder_in = code_forward(previous, starting, code_table)
-    out_part, decoder_in = lax.optimization_barrier(
-        (code_master[1].astype(jnp.bfloat16), decoder_in)
-    )
-    out_table = table_of(
-        lax.all_gather(out_part, ("dp", "img")).reshape((n, 4) + code_shape)
-    )
     gain_width = gain_master.shape[1]
     note = jnp.zeros((16, 128), jnp.float32)
     note = note.at[:7, :gain_width].set(gain_master)
@@ -1259,6 +1245,7 @@
         encoder_dense,
         same,
     )
+    decoder_in, encoded = lax.optimization_barrier((decoder_in, encoded))
     caption = lax.dynamic_slice_in_dim(encoded, row * caption_length, caption_length, 0)
     branch, self_keep = attention_forward(
         decoder_in, gain_set[3], self_weights, "self", "t", None
@@ -1296,7 +1283,9 @@
         - SMOOTH * logit_total / VC
         + Z_WEIGHT * partition * partition
     )
-    per_image = lax.all_gather(per_token, "img")
+    own_tokens = jnp.where(
+        (jnp.arange(images)[:, None] == image) & (part == 0), per_token[None, :], 0.0
+    )
     loss_part = jnp.sum(per_token * valid) / lax.axis_size("t")
     weighting = valid / count
     grad_logits = weighting[:, None] * (
@@ -1337,7 +1326,7 @@
         ],
         [attention_shape[1:], attention_shape[1:], dense_shape[1:]],
         n,
-        2.0,
+        1.0,
         2,
     )
     grad_code_in = code_backward(grad_start, previous, starting, code_shape[0])
@@ -1381,7 +1370,9 @@
         ]
     )
     tail = jnp.zeros((1, D), jnp.float32).at[0, 0].set(squares).at[0, 1].set(loss_part)
-    sums = total_of(jnp.concatenate([sums, tail], axis=0))
+    own_tokens = jnp.concatenate([own_tokens, jnp.zeros((8 - images, D), jnp.float32)])
+    sums, row_sums = total_of(jnp.concatenate([sums, tail, own_tokens], axis=0))
+    per_image = row_sums[8 : 8 + images]
     gain_sums = sums[:7]
     loss = sums[7, 1] / count
     norm = jnp.sqrt(sums[7, 0] + jnp.sum(gain_sums * gain_sums))

time: 1150 us -> 1020 us (0.89)
  waiting for transfers between devices: 124 us -> 28.6 us
  Pallas kernels: 648 us -> 624 us
    reduce_scatter x1, waiting for transfers between devices: 52.4 us -> 0.01 us  [code_forward(): lax.psum_scatter(picked, ROW, scatter_dimension=0, tiled=True)]
    all_gather x1 -> x0, waiting for transfers between devices: 45.8 us -> none  [per_device(): lax.all_gather(out_part, ('dp', 'img')).reshape((n, 4) + code_shape)]
    pallas_call x1, Pallas kernels: 199 us -> 155 us  [scatter(): pl.pallas_call(partial(scatter_kernel, n, slabs, members), out_shape=[jax...]
    pallas_call x2, Pallas kernels: 149 us -> 163 us  [encoder_call(): pl.pallas_call(kernel, out_shape=out_shape, in_specs=[vmem] * len(operand...]
    unnamed x337 -> x324, local copies, waits for them, and re-layouts: 30.9 us -> 32.5 us
    pallas_call x2 -> x1, Pallas kernels: 234 us -> 234 us  [gather(): pl.pallas_call(partial(gather_kernel, n, slabs, tables), out_shape=[jax.S...]
  transfers between devices with their start and end apart: 26 -> 25, of which waited for: 13 -> 13; matrix products, arithmetic and copies ran while one was open for 17% -> 14% of each run, Pallas kernels for 53% -> 58%
where the time goes in v3:
time: 1020 us
  Pallas kernels  624 us (61%)
  matrix products  183 us (18%)
  other arithmetic  97 us (10%)
  local copies, waits for them, and re-layouts  51.1 us (5%)
  waiting for transfers between devices  28.6 us (3%)
  between operations  26.2 us (3%)
    pallas_call x1, Pallas kernels, gather(): pl.pallas_call(partial(gather_kernel, n, slabs, tables), out_shape=[jax.S...  234 us
    pallas_call x2, Pallas kernels, encoder_call(): pl.pallas_call(kernel, out_shape=out_shape, in_specs=[vmem] * len(operand...  163 us
    pallas_call x1, Pallas kernels, scatter(): pl.pallas_call(partial(scatter_kernel, n, slabs, members), out_shape=[jax...  155 us
    dot_general x23, matrix products, product(): lax.dot_general(left, right, dims, preferred_element_type=jnp.float32)  96.4 us
    pallas_call x2, Pallas kernels, by_heads(): pl.pallas_call(kernel, grid=(width // lanes,), out_shape=[jax.ShapeDtypeS...  37.5 us
    pallas_call x2, Pallas kernels, small_call(): pl.pallas_call(kernel, out_shape=out_shape, in_specs=[vmem] * len(operand...  34 us
    unnamed x324, local copies, waits for them, and re-layouts  32.5 us
    dot_general x1, matrix products, dense_forward(): hidden = jnp.dot(inputs, weights[0], preferred_element_type=jnp.float32)  26 us
  transfers between devices with their start and end apart: 25, of which 13 were waited for; matrix products, arithmetic and copies ran while one was open for 14% of the time, Pallas kernels for 58%

profile of v3, /device:TPU:0, one launch (start us, length us, event | category | flops | bytes accessed | tf_op | source)
XLA Modules:
  0.0 1015.4 jit_solution(16548537333642547002)
XLA Ops:
  13.5 233.7 %gather.11 = (bf16[4,1024,512]{2,1,0:T(8,128)(2,1)}, bf16[4,1024,512]{2,1,0:T(8,128)(2,1)}, bf16[2,1024,2048]{2,1,0:T(8,128)(2,1)}, bf16[1,4096,1024]{2,1,0:T(8,128)(2,1)}) custom-call(bf16[4,256,128]{2,1,0:T(8,128)(2,1)} %get-tuple-element.223.refs_0_, bf16[4,256,128]{2,1,0:T(8,128)(2,1)} %get-tuple-element.222.refs_1_, ...), custom_call_target="tpu_custom_call" | custom-call | bytes 402653184 | tf_op jit(solution)/shard_map/gather/pallas_call | solution.py:232
  247.2 13.8 %fusion.20 = bf16[4096,1024]{1,0:T(8,128)(2,1)} fusion(bf16[1024,1024]{1,0:T(8,128)(2,1)} %bitcast.263, s32[4096]{0:T(1024)S(1)} %bitcast.244, pred[4096]{0:T(1024)(128)(4,1)S(1)} %bitcast.254), kind=kOutput, calls=%fused_computation.36 | convolution fusion | flops 8602517504 | bytes 10506240 | tf_op jit(solution)/shard_map/dot_general | solution.py:1105
  264.0 13.1 %share.1 = f32[4,8,16,128]{3,2,1,0:T(8,128)} custom-call(f32[16,128]{1,0:T(8,128)} %copy-done.126), custom_call_target="tpu_custom_call" | custom-call | bytes 16777216 | tf_op jit(solution)/shard_map/share/pallas_call | solution.py:515
  279.9 4.6 gather_fusion
  286.0 76.2 %encoder.1 = (bf16[256,1024]{1,0:T(8,128)(2,1)S(1)}, f32[32,1024]{1,0:T(8,128)S(1)}, f32[32,1024]{1,0:T(8,128)S(1)}, f32[32,1024]{1,0:T(8,128)S(1)}, bf16[256,10...) custom-call(bf16[4,256,256]{2,1,0:T(8,128)(2,1)S(1)} %select_convert, ...), custom_call_target="tpu_custom_call" | custom-call | bytes 134217728 | tf_op jit(solution)/shard_map/encoder/pallas_call | solution.py:646
  379.5 14.5 %causal.2 = (bf16[1024,512]{1,0:T(8,128)(2,1)S(1)}, f32[1024,512]{1,0:T(8,128)S(1)}) custom-call(bf16[1024,512]{1,0:T(8,128)(2,1)S(1)} %convolution_convert_fusion.16.query, bf16[1024,512]{1,0:T(8,128)(2,1)S(1)} %convolution_convert_fusion.15.key, bf16[1024,512]{1,0:T(8,128)(2,1)S(1)} %convolution_convert_fusion.14.value), custom_call_target="tpu_custom_call" | custom-call | flops 2147483648 | bytes 33554432 | tf_op jit(solution)/shard_map/causal/pallas_call | solution.py:852
  400.5 3.0 multiply_reduce_fusion.12
  427.0 3.1 multiply_reduce_fusion.11
  433.8 26.0 %multiply_convert_fusion.1 = (bf16[1024,2048]{1,0:T(8,128)(2,1)S(1)}, f32[1024,2048]{1,0:T(8,128)}, f32[1024,2048]{1,0:T(8,128)}) fusion(bf16[2,1024,2048]{2,1,0:T(8,128)(2,1)S(1)} %bitcast.258, bf16[512,1024]{1,0:T(8,128)(2,1)S(1)} %get-tuple-element.212, bf16[512,1024]{1,0:T(8,128)(2,1)S(1)} %get-tuple-element.211), kind=kOutput, calls=%fused_computation.16 | convolution fusion | flops 4435476480 | bytes 27262976 | tf_op jit(solution)/shard_map/dot_general | solution.py:1076
  459.7 4.5 fusion.25
  466.7 2.6 collective-permute-done.5
  469.3 3.0 multiply_reduce_fusion.10
  479.1 14.8 %fusion.161 = (f32[1024]{0:T(1024)S(1)}, f32[1024,4096]{1,0:T(8,128)}) fusion(bf16[1,4096,1024]{2,1,0:T(8,128)(2,1)} %get-tuple-element.132, bf16[512,1024]{1,0:T(8,128)(2,1)S(1)} %get-tuple-element.210, bf16[512,1024]{1,0:T(8,128)(2,1)S(1)} %get-tuple-element.209), kind=kOutput, calls=%fused_computation.337 | convolution fusion | flops 8598322176 | bytes 27267072 | tf_op jit(solution)/shard_map/dot_general | solution.py:976
  493.9 10.2 %exponential_reduce_fusion = (f32[1024]{0:T(1024)S(1)}, f32[1024]{0:T(1024)S(1)}, f32[1024]{0:T(1024)S(1)}) fusion(f32[1024,4096]{1,0:T(8,128)} %get-tuple-element.240, f32[1024]{0:T(1024)S(1)} %get-tuple-element.239, s32[1024]{0:T(1024)S(1)} %fusion.112), kind=kLoop, calls=%fused_computation.4 | loop fusion | flops 25162752 | bytes 16797696 | tf_op jit(solution)/shard_map/reduce_sum | solution.py:1273
  506.7 8.8 multiply_convert_fusion
  515.5 8.8 fusion.6
  530.5 11.3 %convolution_convert_fusion = bf16[4096,1024]{1,0:T(8,128)(2,1)} fusion(bf16[1024,4096]{1,0:T(8,128)(2,1)S(1)} %multiply_convert_fusion, bf16[512,1024]{1,0:T(8,128)(2,1)S(1)} %get-tuple-element.210, bf16[512,1024]{1,0:T(8,128)(2,1)S(1)} %get-tuple-element.209), kind=kOutput, calls=%fused_computation.37 | convolution fusion | flops 8598323200 | bytes 18874368 | tf_op jit(solution)/shard_map/dot_general | solution.py:976
  543.8 15.0 %add_convert_fusion = bf16[1024,2048]{1,0:T(8,128)(2,1)S(1)} fusion(f32[1024,2048]{1,0:T(8,128)} %get-tuple-element.196, f32[1024,2048]{1,0:T(8,128)} %get-tuple-element.238, bf16[2,1024,2048]{2,1,0:T(8,128)(2,1)} %get-tuple-element.131, bf16[512,1024]{1,0:T(8,128)(2,1)S(1)} %get-tuple-element.208, bf16[512,1024]{1,0:T(8,128)(2,1)S(1)} %get-tuple-element.207), kind=kOutput, calls=%fused_computation.15 | convolution fusion | flops 4328521728 | bytes 27262976 | tf_op jit(solution)/shard_map/dot_general | solution.py:1085
  558.9 4.5 fusion.27
  589.9 23.0 %causal.3 = (bf16[1024,512]{1,0:T(8,128)(2,1)S(1)}, bf16[1024,512]{1,0:T(8,128)(2,1)S(1)}, bf16[1024,512]{1,0:T(8,128)(2,1)S(1)}) custom-call(bf16[1024,512]{1,0:T(8,128)(2,1)S(1)} %copy-done.32, bf16[1024,512]{1,0:T(8,128)(2,1)S(1)} %copy-done.30, bf16[1024,512]{1,0:T(8,128)(2,1)S(1)} %copy-done.28, ...), custom_call_target="tpu_custom_call" | custom-call | flops 2147483648 | bytes 33554432 | tf_op jit(solution)/shard_map/causal/pallas_call | solution.py:852
  623.0 2.9 fusion.61
  631.8 87.0 %encoder_back.1 = (bf16[4,256,256]{2,1,0:T(8,128)(2,1)S(1)}, f32[8,1024]{1,0:T(8,128)S(1)}, bf16[4,1024,128]{2,1,0:T(8,128)(2,1)}, bf16[2,1024,512]{2,1,0:T(8,128)(2,1)}) custom-call(f32[256,1024]{1,0:T(8,128)S(1)} %fusion.57.grad_encoded, f32[8,1024]{1,0:T(8,128)S(1)} %concatenate.41.gains, bf16[4,1024,128]{2,1,0:T(8,128)(2,1)} %bitcast.198, ...), custom_call_target="tpu_custom_call" | custom-call | bytes 134217728 | tf_op jit(solution)/shard_map/encoder_back/pallas_call | solution.py:646
  724.0 9.1 convolution_convert_fusion.1.refs_9_
  733.1 14.6 %fusion.53 = bf16[1024,1024]{1,0:T(8,128)(2,1)} fusion(bf16[4096,1024]{1,0:T(8,128)(2,1)} %all-gather.8.cloned.1.call-done, s32[4096]{0:T(1024)S(1)} %bitcast.245, pred[4096]{0:T(1024)(128)(4,1)S(1)} %bitcast.255), kind=kOutput, calls=%fused_computation.128 | convolution fusion | flops 8599371776 | bytes 10506240 | tf_op jit(solution)/shard_map/dot_general | solution.py:976
  749.0 9.2 convolution_convert_fusion.2.refs_8_
  761.1 3.5 multiply_reduce_fusion.14
  769.3 2.7 convolution_convert_fusion.7.refs_3_
  778.8 155.2 %scatter.33 = (f32[1024,128]{1,0:T(8,128)}, f32[1024,128]{1,0:T(8,128)}, f32[512,512]{1,0:T(8,128)}) custom-call(bf16[1024,512]{1,0:T(8,128)(2,1)} %convolution_convert_fusion.10.refs_0_, bf16[1024,512]{1,0:T(8,128)(2,1)} %convolution_convert_fusion.9.refs_1_, bf16[1024,512]{1,0:T(8,128)(2,1)} %convolution_convert_fusion.8.refs_2_, ...), custom_call_target="tpu_custom_call" | custom-call | bytes 268435456 | tf_op jit(solution)/shard_map/scatter/pallas_call | solution.py:414
  950.8 20.9 %total.1 = (f32[16,1024]{1,0:T(8,128)}, f32[16,1024]{1,0:T(8,128)}) custom-call(f32[16,1024]{1,0:T(8,128)} %concatenate.49.mine), custom_call_target="tpu_custom_call" | custom-call | bytes 16777216 | tf_op jit(solution)/shard_map/total/pallas_call | solution.py:515
  975.8 4.9 fusion.144
  980.8 3.4 fusion.148
  992.1 3.3 multiply_add_fusion
  (522 shorter events, 177.9 us)
Async XLA Ops:
  7.2 240.0 %all-gather.12.cloned.1.call-start = ((), (), s32[]{:S(2)}) async-start(), calls=%async_computation.14 | async-start | bytes 1310720 | tf_op jit(solution)/shard_map/all_gather | solution.py:1188
  9.9 237.4 %all-gather.10.cloned.1.call-start = ((), (), s32[]{:S(2)}) async-start(), calls=%async_computation.13 | async-start | bytes 2621440 | tf_op jit(solution)/shard_map/all_gather | solution.py:1190
  11.1 236.1 %all-gather.14.cloned.1.call-start = ((), (), s32[]{:S(2)}) async-start(), calls=%async_computation.15 | async-start | bytes 2621440 | tf_op jit(solution)/shard_map/all_gather | solution.py:1189
  13.2 353.6 %reduce-scatter.7.cloned.1.call-start = ((), (), s32[]{:S(2)}) async-start(), calls=%async_computation.6 | async-start | bytes 9437184 | tf_op jit(solution)/shard_map/reduce_scatter | solution.py:1106
  13.4 247.6 %copy-start.138 = (s32[1,8,4,128]{3,1,2,0:T(8,128)}, s32[1,8,4,128]{3,1,2,0:T(8,128)S(1)}, u32[]{:S(2)}) copy-start(s32[1,8,4,128]{3,1,2,0:T(8,128)S(1)} %copy.73) | copy-start | bytes 49156
  13.4 247.6 %copy-start.145 = (pred[1,8,4,128]{3,1,2,0:T(8,128)(4,1)}, pred[1,8,4,128]{3,1,2,0:T(8,128)(4,1)S(1)}, u32[]{:S(2)}) copy-start(pred[1,8,4,128]{3,1,2,0:T(8,128)(4,1)S(1)} %copy.74) | copy-start | bytes 12292
  261.1 459.3 %reduce-scatter.15.cloned.1.call-start = ((), (), s32[]{:S(2)}) async-start(), calls=%async_computation.11 | async-start | bytes 10485760 | tf_op jit(solution)/shard_map/reduce_scatter | solution.py:1299
  279.8 93.4 %copy-start.113 = (f32[1024]{0:T(1024)}, f32[1024]{0:T(1024)S(1)}, u32[]{:S(2)}) copy-start(f32[1024]{0:T(1024)S(1)} %mul.619) | copy-start | bytes 12292
  366.8 42.6 %copy-start.1 = (bf16[256,1024]{1,0:T(8,128)(2,1)}, bf16[256,1024]{1,0:T(8,128)(2,1)S(1)}, u32[]{:S(2)}) copy-start(bf16[256,1024]{1,0:T(8,128)(2,1)S(1)} %get-tuple-element.130) | copy-start | bytes 1572868
  369.8 3.4 collective-permute-start
  397.7 2.8 collective-permute-start.1
  406.0 5.1 collective-permute-start.2
  424.2 2.9 collective-permute-start.3
  430.4 2.7 collective-permute-start.4
  433.7 26.0 %copy-start.102 = (bf16[512,1024]{1,0:T(8,128)(2,1)}, bf16[512,1024]{1,0:T(8,128)(2,1)S(1)}, u32[]{:S(2)}) copy-start(bf16[512,1024]{1,0:T(8,128)(2,1)S(1)} %get-tuple-element.211) | copy-start | bytes 3145732
  433.7 26.0 %copy-start.104 = (bf16[512,1024]{1,0:T(8,128)(2,1)}, bf16[512,1024]{1,0:T(8,128)(2,1)S(1)}, u32[]{:S(2)}) copy-start(bf16[512,1024]{1,0:T(8,128)(2,1)S(1)} %get-tuple-element.212) | copy-start | bytes 3145732
  466.5 2.9 collective-permute-start.5
  473.8 2.9 collective-permute-start.6
  493.9 21.6 %slice-start.4 = ((s8[8388608]{0:T(1024)(128)(4,1)}), s8[4194304]{0:T(1024)(128)(4,1)S(1)}, s32[]{:S(2)}) async-start(s8[8388608]{0:T(1024)(128)(4,1)} %bitcast.261), calls=%async_computation.20 | async-start | bytes 8388608
  504.1 1.2 collective-permute-start.7
  524.5 2.7 collective-permute-start.8
  530.3 11.6 %collective-permute-start.9 = (bf16[512,1024]{1,0:T(8,128)(2,1)}, bf16[512,1024]{1,0:T(8,128)(2,1)}, u32[]{:S(2)}, u32[]{:S(2)}) collective-permute-start(bf16[512,1024]{1,0:T(8,128)(2,1)} %fusion.142), channel_id=1, source_target_pairs={{0,1},{1,0},{2,3},{3,2},{4,5},{5,4},{6,7},{7,6},{8,9},{9,8},{10,11... | collective-permute-start | bytes 3145736 | tf_op jit(solution)/shard_map/ppermute | solution.py:955
  541.9 191.3 %all-gather.8.cloned.1.call-start = ((), (), s32[]{:S(2)}) async-start(), calls=%async_computation.9 | async-start | bytes 9437184 | tf_op jit(solution)/shard_map/all_gather | solution.py:1110
  563.6 2.7 collective-permute-start.10
  568.8 2.7 collective-permute-start.11
  579.4 2.8 collective-permute-start.12
  583.7 2.7 collective-permute-start.13
  617.2 2.7 collective-permute-start.14
  622.4 311.6 %reduce-scatter.9.cloned.1.call-start = ((), (), s32[]{:S(2)}) async-start(), calls=%async_computation.7 | async-start | bytes 1310720 | tf_op jit(solution)/shard_map/reduce_scatter | solution.py:1347
  719.6 218.5 %reduce-scatter.11.cloned.1.call-start = ((), (), s32[]{:S(2)}) async-start(), calls=%async_computation.8 | async-start | bytes 2621440 | tf_op jit(solution)/shard_map/reduce_scatter | solution.py:1347
  720.4 222.1 %reduce-scatter.17.cloned.1.call-start = ((), (), s32[]{:S(2)}) async-start(), calls=%async_computation.12 | async-start | bytes 2621440 | tf_op jit(solution)/shard_map/reduce_scatter | solution.py:1298
  721.1 221.4 %reduce-scatter.13.cloned.1.call-start = ((), (), s32[]{:S(2)}) async-start(), calls=%async_computation.10 | async-start | bytes 2621440 | tf_op jit(solution)/shard_map/reduce_scatter | solution.py:1347
  (153 other events, 585.1 us)
Sparse Core Ops, SparseCore 0:
  10.2 39.4 all-gather.11
  51.9 64.1 all-gather.9
  118.2 59.5 all-gather.13
  261.2 86.6 reduce-scatter.6
  542.0 86.4 reduce-scatter.14
  630.7 79.8 all-gather.7
  719.7 30.1 reduce-scatter.8
  752.3 42.5 reduce-scatter.10
  797.1 74.1 reduce-scatter.16
  874.1 67.6 reduce-scatter.12

commit v4 on v3

--- a/solution.py
+++ b/solution.py
@@ -444,16 +444,22 @@
         return (lax.axis_index("dp"), index // self.parts, lax.rem(index, self.parts))
 
 
-class Column:
-    def __init__(self, size):
-        self.size = size
-        self.me = lax.axis_index("dp")
+class Along:
+    def __init__(self, axis, size):
+        self.axis, self.size = axis, size
+        self.me = lax.axis_index(axis)
 
     def other(self, step):
         return lax.rem(self.me + step, self.size)
 
     def device(self, index):
-        return (index, lax.axis_index("img"), lax.axis_index("t"))
+        return tuple(
+            index if axis == self.axis else lax.axis_index(axis) for axis in ("dp",) + ROW
+        )
+
+
+def Column(size):
+    return Along("dp", size)
 
 
 def greet(*groups):
@@ -897,37 +903,43 @@
     )
 
 
-def total_kernel(n, size, mine, result, row_result, row_got, column_got, part, *sems):
-    row, column = Row(size), Column(n)
-    greet(row, column)
-    row_got[row.me] = mine[...]
-    exchange(row, lambda _: mine, lambda index: row_got.at[index], *sems[:2])
-    added = row_got[0]
-    for index in range(1, size):
-        added = added + row_got[index]
-    part[...] = added
-    column_got[column.me] = added
-    exchange(column, lambda _: part, lambda index: column_got.at[index], *sems[2:])
-    added = column_got[0]
-    for index in range(1, n):
-        added = added + column_got[index]
-    result[...] = added
-    row_result[...] = part[...]
-
-
-def total_of(values):
-    n = lax.axis_size("dp")
-    size = lax.axis_size("img") * lax.axis_size("t")
+def total_kernel(sizes, mine, result, row_result, *refs):
+    groups = [Along(axis, size) for axis, size in sizes]
+    parts, gots, sems = refs[:3], refs[3:6], refs[6:]
+    greet(*groups)
+    parts[0][...] = mine[...]
+    for turn, group in enumerate(groups):
+        rows = gots[turn].shape[1]
+        source = parts[turn].at[pl.ds(0, rows)]
+        got = gots[turn]
+        got[group.me] = source[...]
+        exchange(
+            group,
+            lambda _, source=source: source,
+            lambda index, got=got: got.at[index],
+            *sems[2 * turn : 2 * turn + 2],
+        )
+        added = got[0]
+        for index in range(1, group.size):
+            added = added + got[index]
+        if turn < 2:
+            parts[turn + 1][...] = added
+        else:
+            result[...] = added
+    row_result[...] = parts[2][...]
+
+
+def total_of(values, rows):
+    sizes = [(axis, lax.axis_size(axis)) for axis in ("t", "img", "dp")]
+    shape = values.shape
+    short = (rows, shape[1])
+    shapes = [shape, shape, short]
     return small_call(
-        partial(total_kernel, n, size),
-        [jax.ShapeDtypeStruct(values.shape, values.dtype)] * 2,
-        [
-            pltpu.VMEM((size,) + values.shape, values.dtype),
-            pltpu.VMEM((n,) + values.shape, values.dtype),
-            pltpu.VMEM(values.shape, values.dtype),
-        ]
-        + semaphores(size)
-        + semaphores(n),
+        partial(total_kernel, sizes),
+        [jax.ShapeDtypeStruct(short, values.dtype), jax.ShapeDtypeStruct(shape, values.dtype)],
+        [pltpu.VMEM(shape, values.dtype)] * 3
+        + [pltpu.VMEM((size,) + part, values.dtype) for (_, size), part in zip(sizes, shapes)]
+        + [sem for _, size in sizes for sem in semaphores(size)],
         [values],
         8,
         "total",
@@ -941,10 +953,6 @@
 def norm_back(values, gain, upstream):
     _, pull = jax.vjp(rms_norm, values, gain)
     return pull(upstream)
-
-
-def gelu_exact(values):
-    return jax.nn.gelu(values, approximate=False)
 
 
 ROW = ("img", "t")
@@ -1074,17 +1082,20 @@
     normed = rms_norm(values, gain).astype(jnp.bfloat16)
     inputs = spread(normed, axis)
     hidden = jnp.dot(inputs, weights[0], preferred_element_type=jnp.float32)
-    active = gelu_exact(hidden).astype(jnp.bfloat16)
+    share_below = 0.5 * (1.0 + lax.erf(hidden * math.sqrt(0.5)))
+    active = (hidden * share_below).astype(jnp.bfloat16)
+    slope = share_below + hidden * jnp.exp(-0.5 * hidden * hidden) * (
+        1.0 / math.sqrt(2.0 * math.pi)
+    )
     output = collect(product(active, weights[1], LAST), axis)
-    return (output, (inputs, weights, hidden, active))
+    return (output, (inputs, weights, slope, active))
 
 
 def dense_backward(upstream, values, gain, axis, kept):
-    inputs, matrices, hidden, active = kept
+    inputs, matrices, slope, active = kept
     grad_rows = spread(upstream.astype(jnp.bfloat16), axis)
     grad_active = jnp.dot(grad_rows, matrices[1], preferred_element_type=jnp.float32)
-    _, pull = jax.vjp(gelu_exact, hidden)
-    grad_hidden = pull(grad_active)[0].astype(jnp.bfloat16)
+    grad_hidden = (grad_active * slope).astype(jnp.bfloat16)
     grads = [
         product(inputs, grad_hidden, FIRST).astype(jnp.bfloat16),
         product(grad_rows, active, FIRST).astype(jnp.bfloat16),
@@ -1209,8 +1220,8 @@
         [jnp.zeros((images, 1), jnp.int32), code_ids[:, :-1]], axis=1
     ).reshape(-1)
     starting = jnp.broadcast_to(jnp.arange(length) > 0, (images, length)).reshape(-1)
-    code_table, self_weights, mask, encoder_attention, encoder_dense = lax.optimization_barrier(
-        (code_table, self_weights, mask, encoder_attention, encoder_dense)
+    code_table, self_weights, encoder_attention, encoder_dense = lax.optimization_barrier(
+        (code_table, self_weights, encoder_attention, encoder_dense)
     )
     decoder_in = code_forward(previous, starting, code_table)
     gain_width = gain_master.shape[1]
@@ -1371,7 +1382,7 @@
     )
     tail = jnp.zeros((1, D), jnp.float32).at[0, 0].set(squares).at[0, 1].set(loss_part)
     own_tokens = jnp.concatenate([own_tokens, jnp.zeros((8 - images, D), jnp.float32)])
-    sums, row_sums = total_of(jnp.concatenate([sums, tail, own_tokens], axis=0))
+    sums, row_sums = total_of(jnp.concatenate([sums, tail, own_tokens], axis=0), 8)
     per_image = row_sums[8 : 8 + images]
     gain_sums = sums[:7]
     loss = sums[7, 1] / count

time: 1020 us -> 997 us (0.977)
  matrix products: 183 us -> 162 us
    dot_general x1, matrix products: 26 us -> 7.3 us  [dense_forward(): hidden = jnp.dot(inputs, weights[0], preferred_element_type=jnp.float32)]
    unnamed x324 -> x284, local copies, waits for them, and re-layouts: 32.5 us -> 31.8 us
  transfers between devices with their start and end apart: 25 -> 25, of which waited for: 13 -> 13; matrix products, arithmetic and copies ran while one was open for 14% -> 14% of each run, Pallas kernels for 58% -> 59%
where the time goes in v4:
time: 997 us; the launch traced here: 988 us
  Pallas kernels  618 us (62%)
  matrix products  162 us (16%)
  other arithmetic  96.7 us (10%)
  local copies, waits for them, and re-layouts  50.5 us (5%)
  waiting for transfers between devices  28.7 us (3%)
  between operations  26 us (3%)
    pallas_call x1, Pallas kernels, gather(): pl.pallas_call(partial(gather_kernel, n, slabs, tables), out_shape=[jax.S...  234 us
    pallas_call x2, Pallas kernels, encoder_call(): pl.pallas_call(kernel, out_shape=out_shape, in_specs=[vmem] * len(operand...  161 us
    pallas_call x1, Pallas kernels, scatter(): pl.pallas_call(partial(scatter_kernel, n, slabs, members), out_shape=[jax...  154 us
    dot_general x23, matrix products, product(): lax.dot_general(left, right, dims, preferred_element_type=jnp.float32)  100 us
    pallas_call x2, Pallas kernels, by_heads(): pl.pallas_call(kernel, grid=(width // lanes,), out_shape=[jax.ShapeDtypeS...  37.3 us
    pallas_call x2, Pallas kernels, small_call(): pl.pallas_call(kernel, out_shape=out_shape, in_specs=[vmem] * len(operand...  31.9 us
    unnamed x284, local copies, waits for them, and re-layouts  31.8 us
  transfers between devices with their start and end apart: 25, of which 13 were waited for; matrix products, arithmetic and copies ran while one was open for 14% of the time, Pallas kernels for 59%

profile of v4, /device:TPU:0, one launch (start us, length us, event | category | flops | bytes accessed | tf_op | source)
XLA Modules:
  0.0 987.9 jit_solution(2010979170480615252)
XLA Ops:
  13.4 233.7 %gather.11 = (bf16[4,1024,512]{2,1,0:T(8,128)(2,1)}, bf16[4,1024,512]{2,1,0:T(8,128)(2,1)}, bf16[2,1024,2048]{2,1,0:T(8,128)(2,1)}, bf16[1,4096,1024]{2,1,0:T(8,128)(2,1)}) custom-call(bf16[4,256,128]{2,1,0:T(8,128)(2,1)} %get-tuple-element.219.refs_0_, bf16[4,256,128]{2,1,0:T(8,128)(2,1)} %get-tuple-element.218.refs_1_, ...), custom_call_target="tpu_custom_call" | custom-call | bytes 402653184 | tf_op jit(solution)/shard_map/gather/pallas_call | solution.py:232
  247.2 13.8 %fusion.20 = bf16[4096,1024]{1,0:T(8,128)(2,1)} fusion(bf16[1024,1024]{1,0:T(8,128)(2,1)} %bitcast.259, s32[4096]{0:T(1024)S(1)} %bitcast.242, pred[4096]{0:T(1024)(128)(4,1)S(1)} %bitcast.252), kind=kOutput, calls=%fused_computation.28 | convolution fusion | flops 8602517504 | bytes 10506240 | tf_op jit(solution)/shard_map/dot_general | solution.py:1116
  264.2 13.2 %share.1 = f32[4,8,16,128]{3,2,1,0:T(8,128)} custom-call(f32[16,128]{1,0:T(8,128)} %copy-done.111), custom_call_target="tpu_custom_call" | custom-call | bytes 16777216 | tf_op jit(solution)/shard_map/share/pallas_call | solution.py:521
  280.2 4.6 gather_fusion
  286.5 75.9 %encoder.1 = (bf16[256,1024]{1,0:T(8,128)(2,1)S(1)}, f32[32,1024]{1,0:T(8,128)S(1)}, f32[32,1024]{1,0:T(8,128)S(1)}, f32[32,1024]{1,0:T(8,128)S(1)}, bf16[256,10...) custom-call(bf16[4,256,256]{2,1,0:T(8,128)(2,1)S(1)} %select_convert, ...), custom_call_target="tpu_custom_call" | custom-call | bytes 134217728 | tf_op jit(solution)/shard_map/encoder/pallas_call | solution.py:652
  378.9 14.3 %causal.2 = (bf16[1024,512]{1,0:T(8,128)(2,1)S(1)}, f32[1024,512]{1,0:T(8,128)S(1)}) custom-call(bf16[1024,512]{1,0:T(8,128)(2,1)S(1)} %convolution_convert_fusion.16.query, bf16[1024,512]{1,0:T(8,128)(2,1)S(1)} %convolution_convert_fusion.15.key, bf16[1024,512]{1,0:T(8,128)(2,1)S(1)} %convolution_convert_fusion.14.value), custom_call_target="tpu_custom_call" | custom-call | flops 2147483648 | bytes 33554432 | tf_op jit(solution)/shard_map/causal/pallas_call | solution.py:858
  399.6 3.0 multiply_reduce_fusion.12
  410.1 2.6 broadcast_select_fusion.11
  424.8 3.1 multiply_reduce_fusion.11
  431.5 7.3 multiply_convert_fusion.1
  438.8 4.5 fusion.24
  448.4 3.0 multiply_reduce_fusion.10
  458.2 14.7 %fusion.157 = (f32[1024]{0:T(1024)S(1)}, f32[1024,4096]{1,0:T(8,128)}) fusion(bf16[1,4096,1024]{2,1,0:T(8,128)(2,1)} %get-tuple-element.130, bf16[512,1024]{1,0:T(8,128)(2,1)S(1)} %get-tuple-element.206, bf16[512,1024]{1,0:T(8,128)(2,1)S(1)} %get-tuple-element.205), kind=kOutput, calls=%fused_computation.329 | convolution fusion | flops 8598322176 | bytes 27267072 | tf_op jit(solution)/shard_map/dot_general | solution.py:984
  472.9 10.2 %exponential_reduce_fusion = (f32[1024]{0:T(1024)S(1)}, f32[1024]{0:T(1024)S(1)}, f32[1024]{0:T(1024)S(1)}) fusion(f32[1024,4096]{1,0:T(8,128)} %get-tuple-element.237, f32[1024]{0:T(1024)S(1)} %get-tuple-element.236, s32[1024]{0:T(1024)S(1)} %fusion.109), kind=kLoop, calls=%fused_computation.4 | loop fusion | flops 25162752 | bytes 16797696 | tf_op jit(solution)/shard_map/reduce_sum | solution.py:1284
  485.7 8.8 multiply_convert_fusion
  494.5 8.8 fusion.11
  509.5 11.5 %convolution_convert_fusion = bf16[4096,1024]{1,0:T(8,128)(2,1)} fusion(bf16[1024,4096]{1,0:T(8,128)(2,1)S(1)} %multiply_convert_fusion, bf16[512,1024]{1,0:T(8,128)(2,1)S(1)} %get-tuple-element.206, bf16[512,1024]{1,0:T(8,128)(2,1)S(1)} %get-tuple-element.205), kind=kOutput, calls=%fused_computation.29 | convolution fusion | flops 8598323200 | bytes 18874368 | tf_op jit(solution)/shard_map/dot_general | solution.py:984
  524.1 9.5 fusion.10
  533.6 8.0 fusion.26
  568.0 23.0 %causal.3 = (bf16[1024,512]{1,0:T(8,128)(2,1)S(1)}, bf16[1024,512]{1,0:T(8,128)(2,1)S(1)}, bf16[1024,512]{1,0:T(8,128)(2,1)S(1)}) custom-call(bf16[1024,512]{1,0:T(8,128)(2,1)S(1)} %copy-done.32, bf16[1024,512]{1,0:T(8,128)(2,1)S(1)} %copy-done.30, bf16[1024,512]{1,0:T(8,128)(2,1)S(1)} %copy-done.28, ...), custom_call_target="tpu_custom_call" | custom-call | flops 2147483648 | bytes 33554432 | tf_op jit(solution)/shard_map/causal/pallas_call | solution.py:858
  601.0 3.0 fusion.58
  609.9 85.6 %encoder_back.1 = (bf16[4,256,256]{2,1,0:T(8,128)(2,1)S(1)}, f32[8,1024]{1,0:T(8,128)S(1)}, bf16[4,1024,128]{2,1,0:T(8,128)(2,1)}, bf16[2,1024,512]{2,1,0:T(8,128)(2,1)}) custom-call(f32[256,1024]{1,0:T(8,128)S(1)} %fusion.54.grad_encoded, f32[8,1024]{1,0:T(8,128)S(1)} %concatenate.41.gains, bf16[4,1024,128]{2,1,0:T(8,128)(2,1)} %bitcast.196, ...), custom_call_target="tpu_custom_call" | custom-call | bytes 134217728 | tf_op jit(solution)/shard_map/encoder_back/pallas_call | solution.py:652
  700.7 9.1 convolution_convert_fusion.1.refs_9_
  709.8 14.7 %fusion.50 = bf16[1024,1024]{1,0:T(8,128)(2,1)} fusion(bf16[4096,1024]{1,0:T(8,128)(2,1)} %all-gather.8.cloned.1.call-done, s32[4096]{0:T(1024)S(1)} %bitcast.243, pred[4096]{0:T(1024)(128)(4,1)S(1)} %bitcast.253), kind=kOutput, calls=%fused_computation.119 | convolution fusion | flops 8599371776 | bytes 10506240 | tf_op jit(solution)/shard_map/dot_general | solution.py:984
  725.7 9.2 convolution_convert_fusion.2.refs_8_
  737.8 3.5 multiply_reduce_fusion.14
  746.0 2.7 convolution_convert_fusion.7.refs_3_
  755.4 153.6 %scatter.33 = (f32[1024,128]{1,0:T(8,128)}, f32[1024,128]{1,0:T(8,128)}, f32[512,512]{1,0:T(8,128)}) custom-call(bf16[1024,512]{1,0:T(8,128)(2,1)} %convolution_convert_fusion.10.refs_0_, bf16[1024,512]{1,0:T(8,128)(2,1)} %convolution_convert_fusion.9.refs_1_, bf16[1024,512]{1,0:T(8,128)(2,1)} %convolution_convert_fusion.8.refs_2_, ...), custom_call_target="tpu_custom_call" | custom-call | bytes 268435456 | tf_op jit(solution)/shard_map/scatter/pallas_call | solution.py:414
  925.6 18.6 %total.1 = (f32[8,1024]{1,0:T(8,128)}, f32[16,1024]{1,0:T(8,128)}) custom-call(f32[16,1024]{1,0:T(8,128)} %concatenate.49.mine), custom_call_target="tpu_custom_call" | custom-call | bytes 16777216 | tf_op jit(solution)/shard_map/total/pallas_call | solution.py:521
  948.4 4.9 fusion.141
  953.4 3.4 fusion.145
  964.6 3.3 multiply_add_fusion
  (481 shorter events, 176.9 us)
Async XLA Ops:
  7.2 240.0 %all-gather.12.cloned.1.call-start = ((), (), s32[]{:S(2)}) async-start(), calls=%async_computation.14 | async-start | bytes 1310720 | tf_op jit(solution)/shard_map/all_gather | solution.py:1199
  9.9 237.4 %all-gather.10.cloned.1.call-start = ((), (), s32[]{:S(2)}) async-start(), calls=%async_computation.13 | async-start | bytes 2621440 | tf_op jit(solution)/shard_map/all_gather | solution.py:1201
  11.1 236.1 %all-gather.14.cloned.1.call-start = ((), (), s32[]{:S(2)}) async-start(), calls=%async_computation.15 | async-start | bytes 2621440 | tf_op jit(solution)/shard_map/all_gather | solution.py:1200
  13.2 353.0 %reduce-scatter.7.cloned.1.call-start = ((), (), s32[]{:S(2)}) async-start(), calls=%async_computation.6 | async-start | bytes 9437184 | tf_op jit(solution)/shard_map/reduce_scatter | solution.py:1117
  13.4 247.7 %copy-start.120 = (s32[1,8,4,128]{3,1,2,0:T(8,128)}, s32[1,8,4,128]{3,1,2,0:T(8,128)S(1)}, u32[]{:S(2)}) copy-start(s32[1,8,4,128]{3,1,2,0:T(8,128)S(1)} %copy.73) | copy-start | bytes 49156
  13.4 247.7 %copy-start.127 = (pred[1,8,4,128]{3,1,2,0:T(8,128)(4,1)}, pred[1,8,4,128]{3,1,2,0:T(8,128)(4,1)S(1)}, u32[]{:S(2)}) copy-start(pred[1,8,4,128]{3,1,2,0:T(8,128)(4,1)S(1)} %copy.74) | copy-start | bytes 12292
  261.1 19.1 %copy-start.46 = (f32[2000,256]{1,0:T(8,128)S(1)}, f32[2000,256]{1,0:T(8,128)}, u32[]{:S(2)}) copy-start(f32[2000,256]{1,0:T(8,128)} %param.41) | copy-start | bytes 6144004
  261.1 436.1 %reduce-scatter.15.cloned.1.call-start = ((), (), s32[]{:S(2)}) async-start(), calls=%async_computation.11 | async-start | bytes 10485760 | tf_op jit(solution)/shard_map/reduce_scatter | solution.py:1310
  280.1 92.4 %copy-start.105 = (f32[1024]{0:T(1024)}, f32[1024]{0:T(1024)S(1)}, u32[]{:S(2)}) copy-start(f32[1024]{0:T(1024)S(1)} %mul.623) | copy-start | bytes 12292
  366.2 42.2 %copy-start.3 = (bf16[256,1024]{1,0:T(8,128)(2,1)}, bf16[256,1024]{1,0:T(8,128)(2,1)S(1)}, u32[]{:S(2)}) copy-start(bf16[256,1024]{1,0:T(8,128)(2,1)S(1)} %get-tuple-element.128) | copy-start | bytes 1572868
  369.2 3.4 collective-permute-start
  378.9 14.3 %copy-start.31 = (bf16[1024,512]{1,0:T(8,128)(2,1)}, bf16[1024,512]{1,0:T(8,128)(2,1)S(1)}, u32[]{:S(2)}) copy-start(bf16[1024,512]{1,0:T(8,128)(2,1)S(1)} %convolution_convert_fusion.16.query) | copy-start | bytes 3145732
  396.8 2.8 collective-permute-start.1
  405.1 5.0 collective-permute-start.2
  422.0 2.9 collective-permute-start.3
  428.2 2.7 collective-permute-start.4
  445.6 2.9 collective-permute-start.5
  453.0 2.9 collective-permute-start.6
  472.9 21.6 %slice-start.2 = ((s8[8388608]{0:T(1024)(128)(4,1)}), s8[4194304]{0:T(1024)(128)(4,1)S(1)}, s32[]{:S(2)}) async-start(s8[8388608]{0:T(1024)(128)(4,1)} %bitcast.257), calls=%async_computation.18 | async-start | bytes 8388608
  483.1 1.2 collective-permute-start.7
  503.5 2.7 collective-permute-start.8
  509.3 11.7 %collective-permute-start.9 = (bf16[512,1024]{1,0:T(8,128)(2,1)}, bf16[512,1024]{1,0:T(8,128)(2,1)}, u32[]{:S(2)}, u32[]{:S(2)}) collective-permute-start(bf16[512,1024]{1,0:T(8,128)(2,1)} %fusion.139), channel_id=1, source_target_pairs={{0,1},{1,0},{2,3},{3,2},{4,5},{5,4},{6,7},{7,6},{8,9},{9,8},{10,11... | collective-permute-start | bytes 3145736 | tf_op jit(solution)/shard_map/ppermute | solution.py:963
  521.0 188.8 %all-gather.8.cloned.1.call-start = ((), (), s32[]{:S(2)}) async-start(), calls=%async_computation.9 | async-start | bytes 9437184 | tf_op jit(solution)/shard_map/all_gather | solution.py:1121
  541.8 2.7 collective-permute-start.10
  546.9 2.7 collective-permute-start.11
  557.6 2.7 collective-permute-start.12
  561.8 2.7 collective-permute-start.13
  595.3 2.7 collective-permute-start.14
  600.5 308.7 %reduce-scatter.9.cloned.1.call-start = ((), (), s32[]{:S(2)}) async-start(), calls=%async_computation.7 | async-start | bytes 1310720 | tf_op jit(solution)/shard_map/reduce_scatter | solution.py:1358
  696.4 216.8 %reduce-scatter.11.cloned.1.call-start = ((), (), s32[]{:S(2)}) async-start(), calls=%async_computation.8 | async-start | bytes 2621440 | tf_op jit(solution)/shard_map/reduce_scatter | solution.py:1358
  697.1 220.4 %reduce-scatter.17.cloned.1.call-start = ((), (), s32[]{:S(2)}) async-start(), calls=%async_computation.12 | async-start | bytes 2621440 | tf_op jit(solution)/shard_map/reduce_scatter | solution.py:1309
  697.9 219.7 %reduce-scatter.13.cloned.1.call-start = ((), (), s32[]{:S(2)}) async-start(), calls=%async_computation.10 | async-start | bytes 2621440 | tf_op jit(solution)/shard_map/reduce_scatter | solution.py:1358
  (133 other events, 436.1 us)
Sparse Core Ops, SparseCore 0:
  10.2 39.5 all-gather.11
  51.9 64.1 all-gather.9
  118.2 59.5 all-gather.13
  261.3 86.6 reduce-scatter.6
  521.1 86.4 reduce-scatter.14
  609.9 79.5 all-gather.7
  696.5 29.4 reduce-scatter.8
  728.4 42.5 reduce-scatter.10
  773.2 74.0 reduce-scatter.16
  850.1 67.3 reduce-scatter.12

commit v5 on v4

--- a/solution.py
+++ b/solution.py
@@ -59,12 +59,10 @@
     slabs = []
     base = 0.0
     for which, (rows, _) in enumerate(shapes):
-        count = 4 if rows % 64 == 0 else 2
-        for part in range(count):
-            size = rows // count
-            order = ORDERS[part % len(ORDERS)]
-            slabs.append((which, part * size, size, order, base + gap * (part // 2)))
-        base += gap * (count // 2)
+        size = rows // len(ORDERS)
+        for part, order in enumerate(ORDERS):
+            slabs.append((which, part * size, size, order, base))
+        base += gap
     return slabs
 
 

time: 997 us -> 991 us (level)
  no operation moved by 1% of the time
where the time goes in v5:
time: 991 us; the launch traced here: 984 us
  Pallas kernels  614 us (62%)
  matrix products  162 us (16%)
  other arithmetic  96.6 us (10%)
  local copies, waits for them, and re-layouts  50.5 us (5%)
  waiting for transfers between devices  28.8 us (3%)
  between operations  26 us (3%)
    pallas_call x1, Pallas kernels, gather(): pl.pallas_call(partial(gather_kernel, n, slabs, tables), out_shape=[jax.S...  230 us
    pallas_call x2, Pallas kernels, encoder_call(): pl.pallas_call(kernel, out_shape=out_shape, in_specs=[vmem] * len(operand...  161 us
    pallas_call x1, Pallas kernels, scatter(): pl.pallas_call(partial(scatter_kernel, n, slabs, members), out_shape=[jax...  154 us
    dot_general x23, matrix products, product(): lax.dot_general(left, right, dims, preferred_element_type=jnp.float32)  100 us
    pallas_call x2, Pallas kernels, by_heads(): pl.pallas_call(kernel, grid=(width // lanes,), out_shape=[jax.ShapeDtypeS...  37.6 us
    unnamed x284, local copies, waits for them, and re-layouts  31.8 us
    pallas_call x2, Pallas kernels, small_call(): pl.pallas_call(kernel, out_shape=out_shape, in_specs=[vmem] * len(operand...  31.7 us
  transfers between devices with their start and end apart: 25, of which 13 were waited for; matrix products, arithmetic and copies ran while one was open for 14% of the time, Pallas kernels for 59%

profile of v5, /device:TPU:0, one launch (start us, length us, event | category | flops | bytes accessed | tf_op | source)
XLA Modules:
  0.0 984.3 jit_solution(8986246507456995512)
XLA Ops:
  13.4 229.9 %gather.11 = (bf16[4,1024,512]{2,1,0:T(8,128)(2,1)}, bf16[4,1024,512]{2,1,0:T(8,128)(2,1)}, bf16[2,1024,2048]{2,1,0:T(8,128)(2,1)}, bf16[1,4096,1024]{2,1,0:T(8,128)(2,1)}) custom-call(bf16[4,256,128]{2,1,0:T(8,128)(2,1)} %get-tuple-element.219.refs_0_, bf16[4,256,128]{2,1,0:T(8,128)(2,1)} %get-tuple-element.218.refs_1_, ...), custom_call_target="tpu_custom_call" | custom-call | bytes 402653184 | tf_op jit(solution)/shard_map/gather/pallas_call | solution.py:230
  243.4 13.8 %fusion.20 = bf16[4096,1024]{1,0:T(8,128)(2,1)} fusion(bf16[1024,1024]{1,0:T(8,128)(2,1)} %bitcast.259, s32[4096]{0:T(1024)S(1)} %bitcast.242, pred[4096]{0:T(1024)(128)(4,1)S(1)} %bitcast.252), kind=kOutput, calls=%fused_computation.28 | convolution fusion | flops 8602517504 | bytes 10506240 | tf_op jit(solution)/shard_map/dot_general | solution.py:1114
  260.2 15.9 %share.1 = f32[4,8,16,128]{3,2,1,0:T(8,128)} custom-call(f32[16,128]{1,0:T(8,128)} %copy-done.111), custom_call_target="tpu_custom_call" | custom-call | bytes 16777216 | tf_op jit(solution)/shard_map/share/pallas_call | solution.py:519
  278.8 4.6 gather_fusion
  285.2 76.0 %encoder.1 = (bf16[256,1024]{1,0:T(8,128)(2,1)S(1)}, f32[32,1024]{1,0:T(8,128)S(1)}, f32[32,1024]{1,0:T(8,128)S(1)}, f32[32,1024]{1,0:T(8,128)S(1)}, bf16[256,10...) custom-call(bf16[4,256,256]{2,1,0:T(8,128)(2,1)S(1)} %select_convert, ...), custom_call_target="tpu_custom_call" | custom-call | bytes 134217728 | tf_op jit(solution)/shard_map/encoder/pallas_call | solution.py:650
  377.7 14.6 %causal.2 = (bf16[1024,512]{1,0:T(8,128)(2,1)S(1)}, f32[1024,512]{1,0:T(8,128)S(1)}) custom-call(bf16[1024,512]{1,0:T(8,128)(2,1)S(1)} %convolution_convert_fusion.16.query, bf16[1024,512]{1,0:T(8,128)(2,1)S(1)} %convolution_convert_fusion.15.key, bf16[1024,512]{1,0:T(8,128)(2,1)S(1)} %convolution_convert_fusion.14.value), custom_call_target="tpu_custom_call" | custom-call | flops 2147483648 | bytes 33554432 | tf_op jit(solution)/shard_map/causal/pallas_call | solution.py:856
  398.8 3.0 multiply_reduce_fusion.12
  424.0 3.1 multiply_reduce_fusion.11
  430.7 7.3 multiply_convert_fusion.1
  438.0 4.5 fusion.24
  445.0 2.6 collective-permute-done.5
  447.6 3.0 multiply_reduce_fusion.10
  457.4 14.7 %fusion.157 = (f32[1024]{0:T(1024)S(1)}, f32[1024,4096]{1,0:T(8,128)}) fusion(bf16[1,4096,1024]{2,1,0:T(8,128)(2,1)} %get-tuple-element.130, bf16[512,1024]{1,0:T(8,128)(2,1)S(1)} %get-tuple-element.206, bf16[512,1024]{1,0:T(8,128)(2,1)S(1)} %get-tuple-element.205), kind=kOutput, calls=%fused_computation.329 | convolution fusion | flops 8598322176 | bytes 27267072 | tf_op jit(solution)/shard_map/dot_general | solution.py:982
  472.0 10.2 %exponential_reduce_fusion = (f32[1024]{0:T(1024)S(1)}, f32[1024]{0:T(1024)S(1)}, f32[1024]{0:T(1024)S(1)}) fusion(f32[1024,4096]{1,0:T(8,128)} %get-tuple-element.237, f32[1024]{0:T(1024)S(1)} %get-tuple-element.236, s32[1024]{0:T(1024)S(1)} %fusion.109), kind=kLoop, calls=%fused_computation.4 | loop fusion | flops 25162752 | bytes 16797696 | tf_op jit(solution)/shard_map/reduce_sum | solution.py:1282
  484.8 8.6 multiply_convert_fusion
  493.4 8.8 fusion.11
  508.4 11.7 %convolution_convert_fusion = bf16[4096,1024]{1,0:T(8,128)(2,1)} fusion(bf16[1024,4096]{1,0:T(8,128)(2,1)S(1)} %multiply_convert_fusion, bf16[512,1024]{1,0:T(8,128)(2,1)S(1)} %get-tuple-element.206, bf16[512,1024]{1,0:T(8,128)(2,1)S(1)} %get-tuple-element.205), kind=kOutput, calls=%fused_computation.29 | convolution fusion | flops 8598323200 | bytes 18874368 | tf_op jit(solution)/shard_map/dot_general | solution.py:982
  523.3 9.5 fusion.10
  532.8 8.0 fusion.26
  567.1 23.0 %causal.3 = (bf16[1024,512]{1,0:T(8,128)(2,1)S(1)}, bf16[1024,512]{1,0:T(8,128)(2,1)S(1)}, bf16[1024,512]{1,0:T(8,128)(2,1)S(1)}) custom-call(bf16[1024,512]{1,0:T(8,128)(2,1)S(1)} %copy-done.32, bf16[1024,512]{1,0:T(8,128)(2,1)S(1)} %copy-done.30, bf16[1024,512]{1,0:T(8,128)(2,1)S(1)} %copy-done.28, ...), custom_call_target="tpu_custom_call" | custom-call | flops 2147483648 | bytes 33554432 | tf_op jit(solution)/shard_map/causal/pallas_call | solution.py:856
  600.0 3.0 fusion.58
  609.0 84.8 %encoder_back.1 = (bf16[4,256,256]{2,1,0:T(8,128)(2,1)S(1)}, f32[8,1024]{1,0:T(8,128)S(1)}, bf16[4,1024,128]{2,1,0:T(8,128)(2,1)}, bf16[2,1024,512]{2,1,0:T(8,128)(2,1)}) custom-call(f32[256,1024]{1,0:T(8,128)S(1)} %fusion.54.grad_encoded, f32[8,1024]{1,0:T(8,128)S(1)} %concatenate.41.gains, bf16[4,1024,128]{2,1,0:T(8,128)(2,1)} %bitcast.196, ...), custom_call_target="tpu_custom_call" | custom-call | bytes 134217728 | tf_op jit(solution)/shard_map/encoder_back/pallas_call | solution.py:650
  698.9 9.1 convolution_convert_fusion.1.refs_9_
  708.0 14.7 %fusion.50 = bf16[1024,1024]{1,0:T(8,128)(2,1)} fusion(bf16[4096,1024]{1,0:T(8,128)(2,1)} %all-gather.8.cloned.1.call-done, s32[4096]{0:T(1024)S(1)} %bitcast.243, pred[4096]{0:T(1024)(128)(4,1)S(1)} %bitcast.253), kind=kOutput, calls=%fused_computation.119 | convolution fusion | flops 8599371776 | bytes 10506240 | tf_op jit(solution)/shard_map/dot_general | solution.py:982
  723.9 9.2 convolution_convert_fusion.2.refs_8_
  736.1 3.5 multiply_reduce_fusion.14
  744.3 2.7 convolution_convert_fusion.7.refs_3_
  753.7 154.3 %scatter.33 = (f32[1024,128]{1,0:T(8,128)}, f32[1024,128]{1,0:T(8,128)}, f32[512,512]{1,0:T(8,128)}) custom-call(bf16[1024,512]{1,0:T(8,128)(2,1)} %convolution_convert_fusion.10.refs_0_, bf16[1024,512]{1,0:T(8,128)(2,1)} %convolution_convert_fusion.9.refs_1_, bf16[1024,512]{1,0:T(8,128)(2,1)} %convolution_convert_fusion.8.refs_2_, ...), custom_call_target="tpu_custom_call" | custom-call | bytes 268435456 | tf_op jit(solution)/shard_map/scatter/pallas_call | solution.py:412
  924.7 15.8 %total.1 = (f32[8,1024]{1,0:T(8,128)}, f32[16,1024]{1,0:T(8,128)}) custom-call(f32[16,1024]{1,0:T(8,128)} %concatenate.49.mine), custom_call_target="tpu_custom_call" | custom-call | bytes 16777216 | tf_op jit(solution)/shard_map/total/pallas_call | solution.py:519
  944.7 4.9 fusion.141
  949.7 3.4 fusion.145
  961.0 3.3 multiply_add_fusion
  (481 shorter events, 176.9 us)
Async XLA Ops:
  7.2 236.1 %all-gather.12.cloned.1.call-start = ((), (), s32[]{:S(2)}) async-start(), calls=%async_computation.14 | async-start | bytes 1310720 | tf_op jit(solution)/shard_map/all_gather | solution.py:1197
  9.9 233.5 %all-gather.10.cloned.1.call-start = ((), (), s32[]{:S(2)}) async-start(), calls=%async_computation.13 | async-start | bytes 2621440 | tf_op jit(solution)/shard_map/all_gather | solution.py:1199
  11.1 232.3 %all-gather.14.cloned.1.call-start = ((), (), s32[]{:S(2)}) async-start(), calls=%async_computation.15 | async-start | bytes 2621440 | tf_op jit(solution)/shard_map/all_gather | solution.py:1198
  13.2 351.8 %reduce-scatter.7.cloned.1.call-start = ((), (), s32[]{:S(2)}) async-start(), calls=%async_computation.6 | async-start | bytes 9437184 | tf_op jit(solution)/shard_map/reduce_scatter | solution.py:1115
  13.4 243.8 %copy-start.120 = (s32[1,8,4,128]{3,1,2,0:T(8,128)}, s32[1,8,4,128]{3,1,2,0:T(8,128)S(1)}, u32[]{:S(2)}) copy-start(s32[1,8,4,128]{3,1,2,0:T(8,128)S(1)} %copy.73) | copy-start | bytes 49156
  13.4 243.8 %copy-start.127 = (pred[1,8,4,128]{3,1,2,0:T(8,128)(4,1)}, pred[1,8,4,128]{3,1,2,0:T(8,128)(4,1)S(1)}, u32[]{:S(2)}) copy-start(pred[1,8,4,128]{3,1,2,0:T(8,128)(4,1)S(1)} %copy.74) | copy-start | bytes 12292
  257.2 21.6 %copy-start.46 = (f32[2000,256]{1,0:T(8,128)S(1)}, f32[2000,256]{1,0:T(8,128)}, u32[]{:S(2)}) copy-start(f32[2000,256]{1,0:T(8,128)} %param.41) | copy-start | bytes 6144004
  257.3 438.2 %reduce-scatter.15.cloned.1.call-start = ((), (), s32[]{:S(2)}) async-start(), calls=%async_computation.11 | async-start | bytes 10485760 | tf_op jit(solution)/shard_map/reduce_scatter | solution.py:1308
  278.7 92.7 %copy-start.105 = (f32[1024]{0:T(1024)}, f32[1024]{0:T(1024)S(1)}, u32[]{:S(2)}) copy-start(f32[1024]{0:T(1024)S(1)} %mul.623) | copy-start | bytes 12292
  365.0 42.6 %copy-start.3 = (bf16[256,1024]{1,0:T(8,128)(2,1)}, bf16[256,1024]{1,0:T(8,128)(2,1)S(1)}, u32[]{:S(2)}) copy-start(bf16[256,1024]{1,0:T(8,128)(2,1)S(1)} %get-tuple-element.128) | copy-start | bytes 1572868
  368.0 3.4 collective-permute-start
  377.7 14.7 %copy-start.31 = (bf16[1024,512]{1,0:T(8,128)(2,1)}, bf16[1024,512]{1,0:T(8,128)(2,1)S(1)}, u32[]{:S(2)}) copy-start(bf16[1024,512]{1,0:T(8,128)(2,1)S(1)} %convolution_convert_fusion.16.query) | copy-start | bytes 3145732
  396.0 2.8 collective-permute-start.1
  404.3 5.0 collective-permute-start.2
  421.2 2.9 collective-permute-start.3
  427.4 2.7 collective-permute-start.4
  444.7 2.9 collective-permute-start.5
  452.1 2.9 collective-permute-start.6
  472.0 21.4 %slice-start.2 = ((s8[8388608]{0:T(1024)(128)(4,1)}), s8[4194304]{0:T(1024)(128)(4,1)S(1)}, s32[]{:S(2)}) async-start(s8[8388608]{0:T(1024)(128)(4,1)} %bitcast.257), calls=%async_computation.18 | async-start | bytes 8388608
  482.2 1.2 collective-permute-start.7
  502.4 2.7 collective-permute-start.8
  508.2 12.0 %collective-permute-start.9 = (bf16[512,1024]{1,0:T(8,128)(2,1)}, bf16[512,1024]{1,0:T(8,128)(2,1)}, u32[]{:S(2)}, u32[]{:S(2)}) collective-permute-start(bf16[512,1024]{1,0:T(8,128)(2,1)} %fusion.139), channel_id=1, source_target_pairs={{0,1},{1,0},{2,3},{3,2},{4,5},{5,4},{6,7},{7,6},{8,9},{9,8},{10,11... | collective-permute-start | bytes 3145736 | tf_op jit(solution)/shard_map/ppermute | solution.py:961
  520.2 187.9 %all-gather.8.cloned.1.call-start = ((), (), s32[]{:S(2)}) async-start(), calls=%async_computation.9 | async-start | bytes 9437184 | tf_op jit(solution)/shard_map/all_gather | solution.py:1119
  541.0 2.7 collective-permute-start.10
  546.0 2.7 collective-permute-start.11
  556.7 2.7 collective-permute-start.12
  560.9 2.7 collective-permute-start.13
  594.4 2.7 collective-permute-start.14
  599.6 308.5 %reduce-scatter.9.cloned.1.call-start = ((), (), s32[]{:S(2)}) async-start(), calls=%async_computation.7 | async-start | bytes 1310720 | tf_op jit(solution)/shard_map/reduce_scatter | solution.py:1356
  694.6 217.6 %reduce-scatter.11.cloned.1.call-start = ((), (), s32[]{:S(2)}) async-start(), calls=%async_computation.8 | async-start | bytes 2621440 | tf_op jit(solution)/shard_map/reduce_scatter | solution.py:1356
  695.4 221.1 %reduce-scatter.17.cloned.1.call-start = ((), (), s32[]{:S(2)}) async-start(), calls=%async_computation.12 | async-start | bytes 2621440 | tf_op jit(solution)/shard_map/reduce_scatter | solution.py:1307
  696.1 220.4 %reduce-scatter.13.cloned.1.call-start = ((), (), s32[]{:S(2)}) async-start(), calls=%async_computation.10 | async-start | bytes 2621440 | tf_op jit(solution)/shard_map/reduce_scatter | solution.py:1356
  (133 other events, 436.0 us)
Sparse Core Ops, SparseCore 0:
  10.2 39.7 all-gather.11
  52.1 61.5 all-gather.9
  115.9 63.1 all-gather.13
  257.4 89.3 reduce-scatter.6
  520.3 86.4 reduce-scatter.14
  609.1 79.3 all-gather.7
  694.8 29.7 reduce-scatter.8
  726.9 42.5 reduce-scatter.10
  771.8 73.0 reduce-scatter.16
  847.7 68.3 reduce-scatter.12

commit v6 on v5

--- a/solution.py
+++ b/solution.py
@@ -1338,7 +1338,8 @@
         1.0,
         2,
     )
-    grad_code_in = code_backward(grad_start, previous, starting, code_shape[0])
+    grad_start_late, out_grads = lax.optimization_barrier((grad_start, out_grads))
+    grad_code_in = code_backward(grad_start_late, previous, starting, code_shape[0])
     grad_encoded = lax.dynamic_update_slice_in_dim(
         jnp.zeros(encoded.shape, jnp.float32), grad_caption, row * caption_length, 0
     )

time: 991 us -> 1030 us (1.039)
  waiting for transfers between devices: 28.8 us -> 66.6 us
    reduce_scatter x1, waiting for transfers between devices: 0.02 us -> 27.9 us  [per_device(): lax.psum_scatter(grad_out_table, 'img', scatter_dimension=0, tiled=True)]
  transfers between devices with their start and end apart: 25 -> 25, of which waited for: 13 -> 15; matrix products, arithmetic and copies ran while one was open for 14% -> 14% of each run, Pallas kernels for 59% -> 57%
where the time goes in v6:
time: 1030 us
  Pallas kernels  611 us (59%)
  matrix products  165 us (16%)
  other arithmetic  99.8 us (10%)
  waiting for transfers between devices  66.6 us (6%)
  local copies, waits for them, and re-layouts  53.1 us (5%)
  between operations  26 us (3%)
    pallas_call x1, Pallas kernels, gather(): pl.pallas_call(partial(gather_kernel, n, slabs, tables), out_shape=[jax.S...  230 us
    pallas_call x2, Pallas kernels, encoder_call(): pl.pallas_call(kernel, out_shape=out_shape, in_specs=[vmem] * len(operand...  163 us
    pallas_call x1, Pallas kernels, scatter(): pl.pallas_call(partial(scatter_kernel, n, slabs, members), out_shape=[jax...  149 us
    dot_general x23, matrix products, product(): lax.dot_general(left, right, dims, preferred_element_type=jnp.float32)  96.3 us
    pallas_call x2, Pallas kernels, by_heads(): pl.pallas_call(kernel, grid=(width // lanes,), out_shape=[jax.ShapeDtypeS...  37.4 us
    unnamed x284, local copies, waits for them, and re-layouts  32.4 us
    pallas_call x2, Pallas kernels, small_call(): pl.pallas_call(kernel, out_shape=out_shape, in_specs=[vmem] * len(operand...  32.1 us
    reduce_scatter x1, waiting for transfers between devices, per_device(): lax.psum_scatter(grad_out_table, 'img', scatter_dimension=0, tiled=True)  27.9 us
  transfers between devices with their start and end apart: 25, of which 15 were waited for; matrix products, arithmetic and copies ran while one was open for 14% of the time, Pallas kernels for 57%

profile of v6, /device:TPU:0, one launch (start us, length us, event | category | flops | bytes accessed | tf_op | source)
XLA Modules:
  0.0 1025.5 jit_solution(17154728347425047313)
XLA Ops:
  13.4 229.9 %gather.11 = (bf16[4,1024,512]{2,1,0:T(8,128)(2,1)}, bf16[4,1024,512]{2,1,0:T(8,128)(2,1)}, bf16[2,1024,2048]{2,1,0:T(8,128)(2,1)}, bf16[1,4096,1024]{2,1,0:T(8,128)(2,1)}) custom-call(bf16[4,256,128]{2,1,0:T(8,128)(2,1)} %get-tuple-element.223.refs_0_, bf16[4,256,128]{2,1,0:T(8,128)(2,1)} %get-tuple-element.222.refs_1_, ...), custom_call_target="tpu_custom_call" | custom-call | bytes 402653184 | tf_op jit(solution)/shard_map/gather/pallas_call | solution.py:230
  243.4 13.8 %fusion.20 = bf16[4096,1024]{1,0:T(8,128)(2,1)} fusion(bf16[1024,1024]{1,0:T(8,128)(2,1)} %bitcast.259, s32[4096]{0:T(1024)S(1)} %bitcast.242, pred[4096]{0:T(1024)(128)(4,1)S(1)} %bitcast.252), kind=kOutput, calls=%fused_computation.28 | convolution fusion | flops 8602517504 | bytes 10506240 | tf_op jit(solution)/shard_map/dot_general | solution.py:1114
  260.1 15.9 %share.1 = f32[4,8,16,128]{3,2,1,0:T(8,128)} custom-call(f32[16,128]{1,0:T(8,128)} %copy-done.111), custom_call_target="tpu_custom_call" | custom-call | bytes 16777216 | tf_op jit(solution)/shard_map/share/pallas_call | solution.py:519
  278.7 4.6 gather_fusion
  285.1 76.1 %encoder.1 = (bf16[256,1024]{1,0:T(8,128)(2,1)S(1)}, f32[32,1024]{1,0:T(8,128)S(1)}, f32[32,1024]{1,0:T(8,128)S(1)}, f32[32,1024]{1,0:T(8,128)S(1)}, bf16[256,10...) custom-call(bf16[4,256,256]{2,1,0:T(8,128)(2,1)S(1)} %select_convert, ...), custom_call_target="tpu_custom_call" | custom-call | bytes 134217728 | tf_op jit(solution)/shard_map/encoder/pallas_call | solution.py:650
  377.7 14.5 %causal.2 = (bf16[1024,512]{1,0:T(8,128)(2,1)S(1)}, f32[1024,512]{1,0:T(8,128)S(1)}) custom-call(bf16[1024,512]{1,0:T(8,128)(2,1)S(1)} %convolution_convert_fusion.16.query, bf16[1024,512]{1,0:T(8,128)(2,1)S(1)} %convolution_convert_fusion.15.key, bf16[1024,512]{1,0:T(8,128)(2,1)S(1)} %convolution_convert_fusion.14.value), custom_call_target="tpu_custom_call" | custom-call | flops 2147483648 | bytes 33554432 | tf_op jit(solution)/shard_map/causal/pallas_call | solution.py:856
  398.6 3.0 multiply_reduce_fusion.13
  425.0 3.1 multiply_reduce_fusion.12
  431.7 7.3 multiply_convert_fusion.1
  439.0 4.5 fusion.24
  449.7 3.0 multiply_reduce_fusion.11
  460.6 14.7 %fusion.149 = (f32[1024]{0:T(1024)S(1)}, f32[1024,4096]{1,0:T(8,128)}) fusion(bf16[1,4096,1024]{2,1,0:T(8,128)(2,1)} %get-tuple-element.132, bf16[512,1024]{1,0:T(8,128)(2,1)S(1)} %get-tuple-element.210, bf16[512,1024]{1,0:T(8,128)(2,1)S(1)} %get-tuple-element.209), kind=kOutput, calls=%fused_computation.325 | convolution fusion | flops 8598322176 | bytes 27267072 | tf_op jit(solution)/shard_map/dot_general | solution.py:982
  475.3 9.9 exponential_reduce_fusion
  487.8 8.4 multiply_convert_fusion
  496.2 3.3 copy-done.55
  499.5 11.3 %convolution_convert_fusion = bf16[4096,1024]{1,0:T(8,128)(2,1)} fusion(bf16[1024,4096]{1,0:T(8,128)(2,1)S(1)} %multiply_convert_fusion, bf16[512,1024]{1,0:T(8,128)(2,1)S(1)} %get-tuple-element.210, bf16[512,1024]{1,0:T(8,128)(2,1)S(1)} %get-tuple-element.209), kind=kOutput, calls=%fused_computation.29 | convolution fusion | flops 8598323200 | bytes 18874368 | tf_op jit(solution)/shard_map/dot_general | solution.py:982
  510.9 12.8 %fusion.11 = f32[1024,1024]{1,0:T(8,128)S(1)} fusion(bf16[1024,4096]{1,0:T(8,128)(2,1)} %copy-done.55, bf16[1,4096,1024]{2,1,0:T(8,128)(2,1)} %get-tuple-element.132), kind=kOutput, calls=%fused_computation.16 | convolution fusion | flops 8589934592 | bytes 20971520 | tf_op jit(solution)/shard_map/dot_general | solution.py:1314
  531.5 11.8 %fusion.10 = bf16[1024,2048]{1,0:T(8,128)(2,1)S(1)} fusion(f32[1024,2048]{1,0:T(8,128)} %get-tuple-element.239, bf16[2,1024,2048]{2,1,0:T(8,128)(2,1)S(1)} %bitcast.258, bf16[512,1024]{1,0:T(8,128)(2,1)S(1)} %get-tuple-element.208, bf16[512,1024]{1,0:T(8,128)(2,1)S(1)} %get-tuple-element.207), kind=kOutput, calls=%fused_computation.15 | convolution fusion | flops 4320133120 | bytes 18874368 | tf_op jit(solution)/shard_map/dot_general | solution.py:1095
  543.4 4.5 fusion.26
  569.6 27.9 %reduce-scatter.13.cloned.1.call-done = bf16[1024,1024]{1,0:T(8,128)(2,1)} async-done(((bf16[4096,1024]{1,0:T(8,128)(2,1)}), bf16[1024,1024]{1,0:T(8,128)(2,1)}) %reduce-scatter.13.cloned.1.call-update) | async-done | bytes 2097168 | tf_op jit(solution)/shard_map/reduce_scatter | solution.py:1308
  602.6 22.9 %causal.3 = (bf16[1024,512]{1,0:T(8,128)(2,1)S(1)}, bf16[1024,512]{1,0:T(8,128)(2,1)S(1)}, bf16[1024,512]{1,0:T(8,128)(2,1)S(1)}) custom-call(bf16[1024,512]{1,0:T(8,128)(2,1)S(1)} %copy-done.32, bf16[1024,512]{1,0:T(8,128)(2,1)S(1)} %copy-done.30, bf16[1024,512]{1,0:T(8,128)(2,1)S(1)} %copy-done.28, ...), custom_call_target="tpu_custom_call" | custom-call | flops 2147483648 | bytes 33554432 | tf_op jit(solution)/shard_map/causal/pallas_call | solution.py:856
  634.9 8.6 reduce-scatter.15.cloned.1.call-done
  654.9 86.4 %encoder_back.1 = (bf16[4,256,256]{2,1,0:T(8,128)(2,1)S(1)}, f32[8,1024]{1,0:T(8,128)S(1)}, bf16[4,1024,128]{2,1,0:T(8,128)(2,1)}, bf16[2,1024,512]{2,1,0:T(8,128)(2,1)}) custom-call(f32[256,1024]{1,0:T(8,128)S(1)} %fusion.48.grad_encoded, f32[8,1024]{1,0:T(8,128)S(1)} %concatenate.41.gains, bf16[4,1024,128]{2,1,0:T(8,128)(2,1)} %bitcast.198, ...), custom_call_target="tpu_custom_call" | custom-call | bytes 134217728 | tf_op jit(solution)/shard_map/encoder_back/pallas_call | solution.py:650
  746.0 9.1 convolution_convert_fusion.1.refs_9_
  755.1 14.6 %fusion.44 = bf16[1024,1024]{1,0:T(8,128)(2,1)} fusion(bf16[4096,1024]{1,0:T(8,128)(2,1)} %all-gather.8.cloned.1.call-done, s32[4096]{0:T(1024)S(1)} %bitcast.243, pred[4096]{0:T(1024)(128)(4,1)S(1)} %bitcast.253), kind=kOutput, calls=%fused_computation.115 | convolution fusion | flops 8599371776 | bytes 10506240 | tf_op jit(solution)/shard_map/dot_general | solution.py:982
  770.9 9.2 convolution_convert_fusion.2.refs_8_
  783.0 3.5 multiply_reduce_fusion.15
  800.5 149.1 %scatter.33 = (f32[1024,128]{1,0:T(8,128)}, f32[1024,128]{1,0:T(8,128)}, f32[512,512]{1,0:T(8,128)}) custom-call(bf16[1024,512]{1,0:T(8,128)(2,1)} %convolution_convert_fusion.10.refs_0_, bf16[1024,512]{1,0:T(8,128)(2,1)} %convolution_convert_fusion.9.refs_1_, bf16[1024,512]{1,0:T(8,128)(2,1)} %convolution_convert_fusion.8.refs_2_, ...), custom_call_target="tpu_custom_call" | custom-call | bytes 268435456 | tf_op jit(solution)/shard_map/scatter/pallas_call | solution.py:412
  966.4 16.2 %total.1 = (f32[8,1024]{1,0:T(8,128)}, f32[16,1024]{1,0:T(8,128)}) custom-call(f32[16,1024]{1,0:T(8,128)} %concatenate.49.mine), custom_call_target="tpu_custom_call" | custom-call | bytes 16777216 | tf_op jit(solution)/shard_map/total/pallas_call | solution.py:519
  986.7 5.3 fusion.135
  992.1 3.2 fusion.137
  1002.1 3.3 multiply_add_fusion
  (483 shorter events, 187.7 us)
Async XLA Ops:
  7.2 236.1 %all-gather.12.cloned.1.call-start = ((), (), s32[]{:S(2)}) async-start(), calls=%async_computation.14 | async-start | bytes 1310720 | tf_op jit(solution)/shard_map/all_gather | solution.py:1197
  9.9 233.5 %all-gather.10.cloned.1.call-start = ((), (), s32[]{:S(2)}) async-start(), calls=%async_computation.13 | async-start | bytes 2621440 | tf_op jit(solution)/shard_map/all_gather | solution.py:1199
  11.1 232.3 %all-gather.14.cloned.1.call-start = ((), (), s32[]{:S(2)}) async-start(), calls=%async_computation.15 | async-start | bytes 2621440 | tf_op jit(solution)/shard_map/all_gather | solution.py:1198
  13.2 351.8 %reduce-scatter.7.cloned.1.call-start = ((), (), s32[]{:S(2)}) async-start(), calls=%async_computation.6 | async-start | bytes 9437184 | tf_op jit(solution)/shard_map/reduce_scatter | solution.py:1115
  13.4 243.8 %copy-start.120 = (s32[1,8,4,128]{3,1,2,0:T(8,128)}, s32[1,8,4,128]{3,1,2,0:T(8,128)S(1)}, u32[]{:S(2)}) copy-start(s32[1,8,4,128]{3,1,2,0:T(8,128)S(1)} %copy.73) | copy-start | bytes 49156
  13.4 243.8 %copy-start.127 = (pred[1,8,4,128]{3,1,2,0:T(8,128)(4,1)}, pred[1,8,4,128]{3,1,2,0:T(8,128)(4,1)S(1)}, u32[]{:S(2)}) copy-start(pred[1,8,4,128]{3,1,2,0:T(8,128)(4,1)S(1)} %copy.74) | copy-start | bytes 12292
  257.2 21.5 %copy-start.45 = (f32[2000,256]{1,0:T(8,128)S(1)}, f32[2000,256]{1,0:T(8,128)}, u32[]{:S(2)}) copy-start(f32[2000,256]{1,0:T(8,128)} %param.41) | copy-start | bytes 6144004
  257.3 340.2 %reduce-scatter.13.cloned.1.call-start = ((), (), s32[]{:S(2)}) async-start(), calls=%async_computation.9 | async-start | bytes 10485760 | tf_op jit(solution)/shard_map/reduce_scatter | solution.py:1308
  278.6 92.8 %copy-start.105 = (f32[1024]{0:T(1024)}, f32[1024]{0:T(1024)S(1)}, u32[]{:S(2)}) copy-start(f32[1024]{0:T(1024)S(1)} %mul.623) | copy-start | bytes 12292
  365.0 42.5 %copy-start.3 = (bf16[256,1024]{1,0:T(8,128)(2,1)}, bf16[256,1024]{1,0:T(8,128)(2,1)S(1)}, u32[]{:S(2)}) copy-start(bf16[256,1024]{1,0:T(8,128)(2,1)S(1)} %get-tuple-element.130) | copy-start | bytes 1572868
  368.0 3.4 collective-permute-start
  377.7 14.5 %copy-start.31 = (bf16[1024,512]{1,0:T(8,128)(2,1)}, bf16[1024,512]{1,0:T(8,128)(2,1)S(1)}, u32[]{:S(2)}) copy-start(bf16[1024,512]{1,0:T(8,128)(2,1)S(1)} %convolution_convert_fusion.16.query) | copy-start | bytes 3145732
  395.8 2.8 collective-permute-start.1
  404.1 5.1 collective-permute-start.2
  422.0 3.0 collective-permute-start.3
  428.4 2.7 collective-permute-start.4
  446.7 3.0 collective-permute-start.5
  455.2 3.0 collective-permute-start.6
  475.3 12.5 %copy-start.44 = (f32[1024,4096]{1,0:T(8,128)S(1)}, f32[1024,4096]{1,0:T(8,128)}, u32[]{:S(2)}) copy-start(f32[1024,4096]{1,0:T(8,128)} %get-tuple-element.241) | copy-start | bytes 50331652
  485.2 1.2 collective-permute-start.7
  510.9 132.6 %reduce-scatter.15.cloned.1.call-start = ((), (), s32[]{:S(2)}) async-start(), calls=%async_computation.10 | async-start | bytes 2621440 | tf_op jit(solution)/shard_map/reduce_scatter | solution.py:1307
  524.0 2.7 collective-permute-start.8
  528.5 2.7 collective-permute-start.9
  548.1 2.7 collective-permute-start.10
  553.3 2.7 collective-permute-start.11
  563.9 2.7 collective-permute-start.12
  569.4 28.1 %collective-permute-start.13 = (bf16[512,1024]{1,0:T(8,128)(2,1)S(1)}, bf16[512,1024]{1,0:T(8,128)(2,1)}, u32[]{:S(2)}, u32[]{:S(2)}) collective-permute-start(bf16[512,1024]{1,0:T(8,128)(2,1)S(1)} %get-tuple-element.191), channel_id=1, source_target_pairs={{0,1},{1,0},{2,3},{3,2},{4,5},{5,4},{6,7},{7,6},{8,9},{9,8},{10,11... | collective-permute-start | bytes 3145736 | tf_op jit(solution)/shard_map/ppermute | solution.py:961
  597.5 157.6 %all-gather.8.cloned.1.call-start = ((), (), s32[]{:S(2)}) async-start(), calls=%async_computation.11 | async-start | bytes 9437184 | tf_op jit(solution)/shard_map/all_gather | solution.py:1119
  629.8 2.7 collective-permute-start.14
  645.6 304.0 %reduce-scatter.9.cloned.1.call-start = ((), (), s32[]{:S(2)}) async-start(), calls=%async_computation.7 | async-start | bytes 1310720 | tf_op jit(solution)/shard_map/reduce_scatter | solution.py:1357
  742.2 211.5 %reduce-scatter.11.cloned.1.call-start = ((), (), s32[]{:S(2)}) async-start(), calls=%async_computation.8 | async-start | bytes 2621440 | tf_op jit(solution)/shard_map/reduce_scatter | solution.py:1357
  742.9 215.1 %reduce-scatter.17.cloned.1.call-start = ((), (), s32[]{:S(2)}) async-start(), calls=%async_computation.12 | async-start | bytes 2621440 | tf_op jit(solution)/shard_map/reduce_scatter | solution.py:1357
  (133 other events, 422.6 us)
Sparse Core Ops, SparseCore 0:
  10.2 39.7 all-gather.11
  52.1 61.5 all-gather.9
  115.9 63.1 all-gather.13
  257.4 89.3 reduce-scatter.6
  511.0 86.4 reduce-scatter.12
  599.6 43.8 reduce-scatter.14
  646.1 77.5 all-gather.7
  742.3 27.7 reduce-scatter.8
  772.4 42.5 reduce-scatter.10
  817.8 72.4 reduce-scatter.16
